TPU v7x, 512 devices: a whole 4x4x16 slice. The times are simulated.
512 devices in a mesh: fsdp: 64 (over y_hi, z, core), rep: 8 (over x, y_lo).
Axes of the slice: x: 4, y: 4 (y_hi: 2, y_lo: 2; y = y_hi * 2 + y_lo), z: 16, core: 2. Of those that a mesh axis runs over, the one named last changes fastest.
Arguments:
- activations: bfloat16 [131072, 4096], P(('fsdp', 'rep')), may hold values from -6 to 6
- blocks: bfloat16 [64, 128, 128], P('fsdp'), may hold values from -0.1875 to 0.1875
- block_row: int32 [64], P('fsdp'), may hold values from 0 to 31, as said below
- block_column: int32 [64], P('fsdp'), may hold values from 0 to 7, as said below
- cotangent: bfloat16 [131072, 1024], P(('fsdp', 'rep')), may hold values from -6 to 6
Outputs:
- values_out: bfloat16 [131072, 1024], P(('fsdp', 'rep'))
- input_grad: bfloat16 [131072, 4096], P(('fsdp', 'rep'))
- weight_grad: float32 [64, 128, 128], P('fsdp')
Inputs may be any that keep to these rules, and one draw needn't show every extreme that they name: `block_row`: every block row holds exactly 2 nonzero blocks and every block column exactly 8; no pair of block row and block column appears twice. `block_column`: taken together with block_row as above.
All inputs are finite; a program needn't handle non-finite values.
Results may differ from a plain program's by a relative error of at most 0.001.
Values may be sent and summed in bfloat16 or wider, within the bound.
No kernel may reach another device: no remote copies, remote signals or barrier semaphores. Data moves between devices by JAX's collectives and lax.ppermute only.
A program may use at most 64 MiB of HBM per device.

v0:
```python
import jax
import jax.numpy as jnp
from jax import lax
from jax.sharding import PartitionSpec as P


def per_device(activations, blocks, block_row, block_column, cotangent):
    tokens_here = activations.shape[0]
    block_size = blocks.shape[1]
    row_blocks = activations.shape[1] // block_size
    column_blocks = cotangent.shape[1] // block_size
    inputs_three = activations.reshape(tokens_here, row_blocks, block_size)
    outgrad_three = cotangent.reshape(tokens_here, column_blocks, block_size)
    weights = lax.all_gather(blocks, "fsdp", axis=0, tiled=True)
    rows_here = lax.all_gather(block_row, "fsdp", axis=0, tiled=True)
    columns_here = lax.all_gather(block_column, "fsdp", axis=0, tiled=True)
    inputs_sel = jnp.take(inputs_three, rows_here, axis=1)
    outgrad_sel = jnp.take(outgrad_three, columns_here, axis=1)
    forward = jnp.einsum("tnb,nbc->tnc", inputs_sel, weights, preferred_element_type=jnp.float32)
    backward = jnp.einsum("tnc,nbc->tnb", outgrad_sel, weights, preferred_element_type=jnp.float32)
    column_hits = (
        columns_here[:, None] == jnp.arange(column_blocks, dtype=jnp.int32)[None, :]
    ).astype(jnp.float32)
    row_hits = (rows_here[:, None] == jnp.arange(row_blocks, dtype=jnp.int32)[None, :]).astype(
        jnp.float32
    )
    values_acc = jnp.einsum("tnc,nj->tjc", forward, column_hits, precision=lax.Precision.HIGHEST)
    grads_acc = jnp.einsum("tnb,ni->tib", backward, row_hits, precision=lax.Precision.HIGHEST)
    block_grads = jnp.einsum(
        "tnb,tnc->nbc", inputs_sel, outgrad_sel, preferred_element_type=jnp.float32
    )
    values_out = values_acc.reshape(tokens_here, -1).astype(jnp.bfloat16)
    input_grad = grads_acc.reshape(tokens_here, -1).astype(jnp.bfloat16)
    loss_scale = (tokens_here * lax.axis_size("fsdp") * lax.axis_size("rep")) ** (-0.5)
    owned = lax.psum_scatter(block_grads, "fsdp", scatter_dimension=0, tiled=True)
    summed = lax.psum(owned, "rep")
    weight_grad = summed * loss_scale
    return (values_out, input_grad, weight_grad)


def solution(mesh):
    in_specs = (
        P(("fsdp", "rep"), None),
        P("fsdp", None, None),
        P("fsdp"),
        P("fsdp"),
        P(("fsdp", "rep"), None),
    )
    out_specs = (P(("fsdp", "rep"), None), P(("fsdp", "rep"), None), P("fsdp", None, None))
    return jax.shard_map(
        per_device, mesh=mesh, in_specs=in_specs, out_specs=out_specs, check_vma=False
    )
```

profile of v0, /device:TPU:32, one launch (start us, length us, event | category | flops | bytes accessed | tf_op | source)
XLA Modules:
  0.0 476.5 jit_solution(6904893197582444805)
XLA Ops:
  7.2 0.0 all-gather.2.cloned.1.call-start
  7.2 0.7 all-gather.2.cloned.1.call-update
  7.9 0.0 reduce-scatter.2.cloned.1.call-start
  9.2 1.2 copy.20
  10.5 0.3 copy.21
  10.8 4.1 copy.17
  14.8 3.2 copy.18
  18.1 1.3 dynamic-slice
  19.3 0.8 dynamic-update-slice.1
  20.1 0.8 dynamic-update-slice
  20.9 30.8 %all-reduce.2 = (s32[64]{0:T(128)S(1)}, s32[64]{0:T(128)S(1)}) all-reduce(s32[64]{0:T(128)S(1)} %dynamic-update-slice.1, s32[64]{0:T(128)S(1)} %dynamic-update-slice), channel_id=1, replica_groups=mesh['fsdp'=64,'rep'=8] {'fsdp'}, use_global_device_ids=true, to_apply=%add.1 | all-reduce | flops 128 | bytes 1024
  51.7 3.0 gather_fusion
  54.7 3.1 gather_fusion.1
  57.8 7.0 %fusion.4 = f32[64,128,128]{2,1,0:T(8,128)} fusion(bf16[64,256,128]{2,1,0:T(8,128)(2,1)} %gather_fusion, pred[64]{0:T(512)(128)(4,1)S(1)} %get-tuple-element.8, bf16[64,256,128]{2,1,0:T(8,128)(2,1)} %gather_fusion.1, pred[64]{0:T(512)(128)(4,1)S(1)} %get-tuple-element.7), kind=kOutput, calls=%fused_computation.6 | convolution fusion | flops 541065216 | bytes 12583040 | tf_op jit(solution)/shard_map/tnb,tnc->nbc/dot_general | solution.py:29
  64.8 0.0 reduce-scatter.2.cloned.1.call-update
  64.8 0.0 all-reduce.5.cloned.1.call-start
  64.9 94.3 %all-gather.2.cloned.1.call-done = bf16[64,128,128]{2,1,0:T(8,128)(2,1)} async-done(((bf16[1,128,128]{2,1,0:T(8,128)(2,1)}), bf16[64,128,128]{2,1,0:T(8,128)(2,1)}) %all-gather.2.cloned.1.call-update) | async-done | bytes 2097168 | tf_op jit(solution)/shard_map/all_gather | solution.py:14
  159.1 4.2 fusion.14
  163.3 0.0 copy-start
  163.3 0.0 copy-start.1
  163.3 10.6 %fusion.17 = bf16[32,256,128]{2,0,1:T(8,128)(2,1)S(1)} fusion(f32[256,64,128]{2,0,1:T(8,128)S(1)} %fusion.14, s32[64]{0:T(128)S(1)} %get-tuple-element.3), kind=kOutput, calls=%fused_computation.18 | convolution fusion | flops 806356992 | bytes 10486016 | tf_op jit(solution)/shard_map/tnb,ni->tib/dot_general | solution.py:28
  173.9 0.0 copy-done
  173.9 0.0 copy-done.1
  173.9 4.5 fusion.11
  178.5 200.9 %reduce-scatter.2.cloned.1.call-done = f32[1,128,128]{2,1,0:T(8,128)} async-done(((f32[64,128,128]{2,1,0:T(8,128)}), f32[1,128,128]{2,1,0:T(8,128)}) %reduce-scatter.2.cloned.1.call-update) | async-done | bytes 65552 | tf_op jit(solution)/shard_map/reduce_scatter | solution.py:35
  379.4 0.0 all-reduce.5.cloned.1.call-update
  379.4 10.4 %fusion.20 = bf16[8,256,128]{2,0,1:T(8,128)(2,1)S(1)} fusion(f32[256,64,128]{2,0,1:T(8,128)} %fusion.11, s32[64]{0:T(128)S(1)} %get-tuple-element.4), kind=kOutput, calls=%fused_computation.19 | convolution fusion | flops 201589248 | bytes 8913152 | tf_op jit(solution)/shard_map/tnc,nj->tjc/dot_general | solution.py:27
  389.8 2.3 copy.37
  392.1 0.9 copy.38
  393.0 75.4 %all-reduce.5.cloned.1.call-done = f32[1,128,128]{2,1,0:T(8,128)} async-done(((f32[1,128,128]{2,1,0:T(8,128)}), f32[1,128,128]{2,1,0:T(8,128)}) %all-reduce.5.cloned.1.call-update) | async-done | bytes 65552 | tf_op jit(solution)/shard_map/psum | solution.py:36
  468.5 1.5 broadcast_multiply_fusion
  (6 shorter events, 0.0 us)
Async XLA Ops:
  7.2 152.0 %all-gather.2.cloned.1.call-start = ((), (), s32[]{:S(2)}) async-start(), calls=%async_computation.1 | async-start | bytes 2129920 | tf_op jit(solution)/shard_map/all_gather | solution.py:14
  7.9 371.5 %reduce-scatter.2.cloned.1.call-start = ((), (), s32[]{:S(2)}) async-start(), calls=%async_computation.2 | async-start | bytes 4259840 | tf_op jit(solution)/shard_map/reduce_scatter | solution.py:35
  64.8 403.6 %all-reduce.5.cloned.1.call-start = ((), (), s32[]{:S(2)}) async-start(), calls=%async_computation.3 | async-start | bytes 131072 | tf_op jit(solution)/shard_map/psum | solution.py:36
  163.3 10.6 %copy-start = (bf16[64,256,128]{2,1,0:T(8,128)(2,1)S(1)}, bf16[64,256,128]{2,1,0:T(8,128)(2,1)}, u32[]{:S(2)}) copy-start(bf16[64,256,128]{2,1,0:T(8,128)(2,1)} %gather_fusion) | copy-start | bytes 12582916
  163.3 10.6 %copy-start.1 = (bf16[64,128,128]{2,1,0:T(8,128)(2,1)S(1)}, bf16[64,128,128]{2,1,0:T(8,128)(2,1)}, u32[]{:S(2)}) copy-start(bf16[64,128,128]{2,1,0:T(8,128)(2,1)} %all-gather.2.cloned.1.call-done) | copy-start | bytes 6291460
Sparse Core Ops, SparseCore 0:
  11.3 147.7 all-gather.1
  163.8 215.5 reduce-scatter.1
  382.6 85.8 all-reduce.4
where the time goes:
time: 477 us; the launch traced here: 476 us
  waiting for transfers between devices  371 us (78%)
  matrix products  36.8 us (8%)
  blocking collectives  30.8 us (6%)
  local copies, waits for them, and re-layouts  20.9 us (4%)
  between operations  15.1 us (3%)
    reduce_scatter x1, waiting for transfers between devices, per_device(): lax.psum_scatter(block_grads, 'fsdp', scatter_dimension=0, tiled=True)  201 us
    all_gather x1, waiting for transfers between devices, per_device(): weights = lax.all_gather(blocks, 'fsdp', axis=0, tiled=True)  94.3 us
    psum x1, waiting for transfers between devices, per_device(): summed = lax.psum(owned, 'rep')  75.4 us
    unnamed x1, blocking collectives  30.8 us
    unnamed x13, local copies, waits for them, and re-layouts  11.3 us
    dot_general x1, matrix products, per_device(): jnp.einsum('tnb,ni->tib', backward, row_hits, precision=lax.Precision.HIG...  10.6 us
    dot_general x1, matrix products, per_device(): jnp.einsum('tnc,nj->tjc', forward, column_hits, precision=lax.Precision.H...  10.4 us
  transfers between devices with their start and end apart: 3, of which 3 were waited for; matrix products, arithmetic and copies ran while one was open for 12% of the time, Pallas kernels for 0%

commit v1 on v0

v1 whole, which is shorter than its diff:
```python
import functools

import jax
import jax.numpy as jnp
from jax import lax
from jax.experimental import pallas as pl
from jax.experimental.pallas import tpu as pltpu
from jax.sharding import Mesh, PartitionSpec as P

AXES = ("yh", "z", "c", "x", "yl")
SIZES = (2, 16, 2, 4, 2)
FSDP = ("yh", "z", "c")
REP = ("x", "yl")
PLANE = ("yh", "x", "yl")
B = 128
NNZ, RB, CB = 64, 32, 8
VMEM = pltpu.CompilerParams(vmem_limit_bytes=48 * 1024 * 1024)


def grads_kernel(parity_ref, code_ref, x_ref, g_ref, out_ref):
    parity = parity_ref[0]
    for yh in range(2):
        for z in range(16):
            code = code_ref[yh * 32 + z * 2 + parity]
            row = pl.multiple_of((code // CB) * B, B)
            col = pl.multiple_of((code % CB) * B, B)
            grad = lax.dot_general(
                x_ref[:, pl.ds(row, B)],
                g_ref[:, pl.ds(col, B)],
                (((0,), (0,)), ((), ())),
                preferred_element_type=jnp.float32,
            )
            out_ref[yh * 8 : (yh + 1) * 8, z] = grad.reshape(8, 16, B)


def half_grads(parity, codes, x, g):
    smem = pl.BlockSpec(memory_space=pltpu.SMEM)
    vmem = pl.BlockSpec(memory_space=pltpu.VMEM)
    return pl.pallas_call(
        grads_kernel,
        out_shape=jax.ShapeDtypeStruct((16, 16, 16, B), jnp.float32),
        in_specs=[smem, smem, vmem, vmem],
        out_specs=vmem,
        compiler_params=VMEM,
        name="block_grads",
    )(parity.reshape(1), codes, x, g)


def project_kernel(code_ref, x_ref, g_ref, w_ref, v_ref, d_ref, by_col, by_row, fill):
    for k in range(CB):
        fill[k] = 0
    for k in range(RB):
        fill[CB + k] = 0

    def place(n, carry):
        code = code_ref[n]
        row, col = code // CB, code % CB
        at = fill[col]
        by_col[col * 8 + at] = n
        fill[col] = at + 1
        at = fill[CB + row]
        by_row[row * 2 + at] = n
        fill[CB + row] = at + 1
        return carry

    lax.fori_loop(0, NNZ, place, 0)

    def block(n):
        return jnp.concatenate(
            [w_ref[:, pl.ds(pl.multiple_of(n * 512 + i * B, B), B)] for i in range(4)], axis=0
        )

    for col in range(CB):
        ns = [by_col[col * 8 + k] for k in range(8)]
        rows = [code_ref[n] // CB for n in ns]
        xs = jnp.concatenate(
            [x_ref[:, pl.ds(pl.multiple_of(r * B, B), B)] for r in rows], axis=1
        )
        ws = jnp.concatenate([block(n) for n in ns], axis=0)
        v_ref[:, col * B : (col + 1) * B] = jnp.dot(
            xs, ws, preferred_element_type=jnp.float32
        ).astype(v_ref.dtype)
    for row in range(RB):
        ns = [by_row[row * 2 + k] for k in range(2)]
        cols = [code_ref[n] % CB for n in ns]
        gs = jnp.concatenate(
            [g_ref[:, pl.ds(pl.multiple_of(c * B, B), B)] for c in cols], axis=1
        )
        ws = jnp.concatenate([block(n) for n in ns], axis=1)
        d_ref[:, row * B : (row + 1) * B] = lax.dot_general(
            gs, ws, (((1,), (1,)), ((), ())), preferred_element_type=jnp.float32
        ).astype(d_ref.dtype)


def project(codes, x, g, w):
    smem = pl.BlockSpec(memory_space=pltpu.SMEM)
    vmem = pl.BlockSpec(memory_space=pltpu.VMEM)
    return pl.pallas_call(
        project_kernel,
        out_shape=[
            jax.ShapeDtypeStruct(g.shape, jnp.bfloat16),
            jax.ShapeDtypeStruct(x.shape, jnp.bfloat16),
        ],
        in_specs=[smem, vmem, vmem, vmem],
        out_specs=[vmem, vmem],
        scratch_shapes=[
            pltpu.SMEM((NNZ,), jnp.int32),
            pltpu.SMEM((NNZ,), jnp.int32),
            pltpu.SMEM((CB + RB,), jnp.int32),
        ],
        compiler_params=VMEM,
        name="project",
    )(codes, x, g, w)


def to_all(part, axes, count):
    return lax.all_to_all(
        jnp.broadcast_to(part[None], (count,) + part.shape), axes, 0, 0, tiled=True
    )


def per_device(x, blocks, block_row, block_column, g):
    core = lax.axis_index("c")
    rep = lax.axis_index(REP)
    pieces = blocks.reshape(4, 2, 2, 8, B)
    mine = lax.dynamic_index_in_dim(pieces, rep, 3, keepdims=False)
    mine = mine.transpose(2, 1, 0, 3)
    code = (block_row * CB + block_column).astype(jnp.bfloat16)
    tail = jnp.broadcast_to(code.reshape(1, 1, 1, 1), (2, 2, 4, B))
    packet = jnp.concatenate([mine, tail], axis=2)
    packet = jnp.broadcast_to(packet[:, None], (2, 16, 2, 8, B)).reshape(64, 8, B)
    got = lax.all_to_all(packet, FSDP, 0, 0, tiled=True)
    codes = got[:, 4, 0].astype(jnp.int32)
    share = got[:, :4, :].reshape(NNZ * 512)

    other = half_grads(1 - core, codes, x, g)
    swap = [(0, 1), (1, 0)]
    incoming = lax.ppermute(other, "c", swap)
    own = half_grads(core, codes, x, g)
    paired = own + incoming
    spread = lax.all_to_all(paired, PLANE, 0, 0, tiled=True)
    plane_sum = jnp.sum(spread, axis=0)

    half_w = to_all(share, PLANE, 16)
    far_w = lax.ppermute(half_w, "c", swap)
    low = jnp.where(core == 0, half_w, far_w)
    high = jnp.where(core == 0, far_w, half_w)
    w = jnp.concatenate([low, high], axis=0)
    values_out, input_grad = project(codes, x, g, w)

    ring = lax.all_to_all(plane_sum, "z", 0, 0, tiled=True)
    strip = jnp.sum(ring, axis=0)
    whole = to_all(strip, REP, 8)
    loss_scale = (x.shape[0] * lax.axis_size(AXES)) ** (-0.5)
    weight_grad = whole.reshape(1, B, B) * loss_scale
    return values_out, input_grad, weight_grad


def solution(mesh):
    cut = Mesh(mesh.devices.reshape(SIZES), AXES)
    in_specs = (P(AXES, None), P(FSDP, None, None), P(FSDP), P(FSDP), P(AXES, None))
    out_specs = (P(AXES, None), P(AXES, None), P(FSDP, None, None))
    return jax.shard_map(
        per_device, mesh=cut, in_specs=in_specs, out_specs=out_specs, check_vma=False
    )
```

time: 477 us -> 158 us (0.33)
  the two profiles are of different devices: /device:TPU:32 before, /device:TPU:2 now
where the time goes in v1:
time: 158 us; the launch traced here: 157 us
  waiting for transfers between devices  52.8 us (33%)
  starting transfers between devices  48.3 us (31%)
  other arithmetic  21.9 us (14%)
  local copies, waits for them, and re-layouts  19.2 us (12%)
  Pallas kernels  12.4 us (8%)
  between operations  2.09 us (1%)
    all_to_all x1, starting transfers between devices, per_device(): got = lax.all_to_all(packet, FSDP, 0, 0, tiled=True)  18.7 us
    all_to_all x1, waiting for transfers between devices, per_device(): got = lax.all_to_all(packet, FSDP, 0, 0, tiled=True)  18.6 us
    unnamed x15, local copies, waits for them, and re-layouts  15.7 us
    all_to_all x1, waiting for transfers between devices, per_device(): spread = lax.all_to_all(paired, PLANE, 0, 0, tiled=True)  15 us
    all_to_all x2, starting transfers between devices, to_all(): lax.all_to_all(jnp.broadcast_to(part[None], (count,) + part.shape), axes,...  13.6 us
    all_to_all x2, waiting for transfers between devices, to_all(): lax.all_to_all(jnp.broadcast_to(part[None], (count,) + part.shape), axes,...  9.82 us
    all_to_all x1, waiting for transfers between devices, per_device(): ring = lax.all_to_all(plane_sum, 'z', 0, 0, tiled=True)  9.41 us
    all_to_all x1, starting transfers between devices, per_device(): spread = lax.all_to_all(paired, PLANE, 0, 0, tiled=True)  8.55 us
  transfers between devices with their start and end apart: 7, of which 4 were waited for; matrix products, arithmetic and copies ran while one was open for 22% of the time, Pallas kernels for 6%

profile of v1, /device:TPU:2, one launch (start us, length us, event | category | flops | bytes accessed | tf_op | source)
XLA Modules:
  0.0 156.6 jit_solution(11415961716684373016)
XLA Ops:
  0.6 0.0 copy-start
  0.7 0.7 copy-done
  2.7 0.7 broadcast_in_dim.11
  3.4 18.7 %all-to-all-start = ((bf16[64,8,128]{2,1,0:T(8,128)(2,1)}), bf16[64,8,128]{2,1,0:T(8,128)(2,1)S(1)}, u32[]{:S(2)}, u32[]{:S(2)}) async-start(bf16[64,8,128]{2,1,0:T(8,128)(2,1)} %bitcast.4), calls=%async_computation | async-start | bytes 262144 | tf_op jit(solution)/shard_map/all_to_all | solution.py:132
  22.2 18.6 %all-to-all-done = bf16[64,8,128]{2,1,0:T(8,128)(2,1)S(1)} async-done(((bf16[64,8,128]{2,1,0:T(8,128)(2,1)}), bf16[64,8,128]{2,1,0:T(8,128)(2,1)S(1)}, u32[]{:S(2)}, u32[]{:S(2)}) %all-to-all-start) | async-done | bytes 131104 | tf_op jit(solution)/shard_map/all_to_all | solution.py:132
  40.7 1.2 fusion.code_ref
  42.0 0.0 copy-start.1
  42.0 1.6 %copy-done.1 = bf16[256,4096]{1,0:T(8,128)(2,1)S(1)} copy-done((bf16[256,4096]{1,0:T(8,128)(2,1)S(1)}, bf16[256,4096]{1,0:T(8,128)(2,1)}, u32[]{:S(2)}) %copy-start.1) | copy-done | bytes 2097176
  43.6 0.0 copy-start.3
  43.6 1.0 copy-done.3
  44.6 3.3 %block_grads.3 = f32[16,16,16,128]{3,2,1,0:T(8,128)} custom-call(s32[1]{0:T(128)} %bitcast.7.parity_ref, s32[64]{0:T(128)S(1)} %fusion.code_ref, bf16[256,4096]{1,0:T(8,128)(2,1)S(1)} %copy-done.1, bf16[256,1024]{1,0:T(8,128)(2,1)S(1)} %copy-done.3), custom_call_target="tpu_custom_call" | custom-call | tf_op jit(solution)/shard_map/block_grads/pallas_call | solution.py:39
  47.9 2.0 %collective-permute-start.1 = (f32[16,16,16,128]{3,2,1,0:T(8,128)}, f32[16,16,16,128]{3,2,1,0:T(8,128)}, u32[]{:S(2)}, u32[]{:S(2)}) collective-permute-start(f32[16,16,16,128]{3,2,1,0:T(8,128)} %block_grads.3), channel_id=1, source_target_pairs={{0,8},{8,0},{1,9},{9,1},{2,10},{10,2},{3,11},{11,3},{4,12},{12,4},... | collective-permute-start | bytes 6291464 | tf_op jit(solution)/shard_map/ppermute | solution.py:138
  49.9 1.6 %broadcast_in_dim.13 = bf16[16,1,32768]{2,1,0:T(2,128)(2,1)S(1)} broadcast(bf16[32768]{0:T(1024)(128)(2,1)S(1)} %bitcast.18), dimensions={2} | broadcast | bytes 1114112 | tf_op jit(solution)/shard_map/broadcast_in_dim | solution.py:118
  51.5 0.5 broadcast.18
  52.1 8.3 %reduce.2 = bf16[16,32768]{1,0:T(8,128)(2,1)} reduce(bf16[16,1,32768]{2,1,0:T(2,128)(2,1)S(1)} %broadcast_in_dim.13, bf16[]{:T(256)} %broadcast.18), dimensions={1}, to_apply=%broadcast_in_dim.13.reduce_sub_computation | reduce | bytes 2097154 | tf_op jit(solution)/shard_map/broadcast_in_dim | solution.py:118
  60.3 0.0 copy-start.2
  60.3 0.0 copy-start.4
  60.3 2.8 %reshape.53 = bf16[16,2,16384]{2,1,0:T(2,128)(2,1)} reshape(bf16[16,32768]{1,0:T(8,128)(2,1)} %reduce.2) | data formatting | bytes 2097152
  63.1 5.0 %all-to-all-start.1 = ((bf16[16,2,16384]{2,1,0:T(2,128)(2,1)}), bf16[16,2,16384]{2,1,0:T(2,128)(2,1)}, u32[]{:S(2)}, u32[]{:S(2)}) async-start(bf16[16,2,16384]{2,1,0:T(2,128)(2,1)} %reshape.53), calls=%async_computation.1 | async-start | bytes 2097152 | tf_op jit(solution)/shard_map/all_to_all | solution.py:117
  68.1 0.0 copy-done.2
  68.1 0.0 copy-done.4
  68.1 2.0 %block_grads.2 = f32[16,16,16,128]{3,2,1,0:T(8,128)S(1)} custom-call(s32[1]{0:T(128)} %bitcast.6.parity_ref, s32[64]{0:T(128)S(1)} %fusion.code_ref, bf16[256,4096]{1,0:T(8,128)(2,1)S(1)} %copy-done.2, bf16[256,1024]{1,0:T(8,128)(2,1)S(1)} %copy-done.4), custom_call_target="tpu_custom_call" | custom-call | tf_op jit(solution)/shard_map/block_grads/pallas_call | solution.py:39
  70.1 0.0 collective-permute-done.1
  70.1 3.3 %add.18 = f32[16,16,16,128]{3,2,1,0:T(8,128)} add(f32[16,16,16,128]{3,2,1,0:T(8,128)S(1)} %block_grads.2, f32[16,16,16,128]{3,2,1,0:T(8,128)} %collective-permute-done.1) | non-fusion elementwise | flops 524288 | bytes 6291456 | tf_op jit(solution)/shard_map/add | solution.py:140
  73.3 9.8 %all-to-all-done.1 = bf16[16,2,16384]{2,1,0:T(2,128)(2,1)} async-done(((bf16[16,2,16384]{2,1,0:T(2,128)(2,1)}), bf16[16,2,16384]{2,1,0:T(2,128)(2,1)}, u32[]{:S(2)}, u32[]{:S(2)}) %all-to-all-start.1) | async-done | bytes 1048608 | tf_op jit(solution)/shard_map/all_to_all | solution.py:117
  83.1 8.5 %all-to-all-start.2 = ((f32[16,16,16,128]{3,2,1,0:T(8,128)}), f32[16,16,16,128]{3,2,1,0:T(8,128)}, u32[]{:S(2)}, u32[]{:S(2)}) async-start(f32[16,16,16,128]{3,2,1,0:T(8,128)} %add.18), calls=%async_computation.2 | async-start | bytes 4194304 | tf_op jit(solution)/shard_map/all_to_all | solution.py:141
  91.7 5.8 %reshape.54 = bf16[16,1,32768]{2,1,0:T(2,128)(2,1)} reshape(bf16[16,2,16384]{2,1,0:T(2,128)(2,1)} %all-to-all-done.1) | data formatting | bytes 2097152
  97.5 3.8 %copy.25 = bf16[16,1,32768]{2,0,1:T(8,128)(2,1)} copy(bf16[16,1,32768]{2,1,0:T(2,128)(2,1)} %reshape.54) | data formatting | bytes 2097152
  101.2 1.9 %collective-permute-start = (bf16[16,32768]{1,0:T(8,128)(2,1)}, bf16[16,32768]{1,0:T(8,128)(2,1)}, u32[]{:S(2)}, u32[]{:S(2)}) collective-permute-start(bf16[16,32768]{1,0:T(8,128)(2,1)} %bitcast.15), channel_id=1, source_target_pairs={{0,8},{8,0},{1,9},{9,1},{2,10},{10,2},{3,11},{11,3},{4,12},{12,4},... | collective-permute-start | bytes 3145736 | tf_op jit(solution)/shard_map/ppermute | solution.py:145
  103.1 15.0 %all-to-all-done.2 = f32[16,16,16,128]{3,2,1,0:T(8,128)} async-done(((f32[16,16,16,128]{3,2,1,0:T(8,128)}), f32[16,16,16,128]{3,2,1,0:T(8,128)}, u32[]{:S(2)}, u32[]{:S(2)}) %all-to-all-start.2) | async-done | bytes 2097184 | tf_op jit(solution)/shard_map/all_to_all | solution.py:141
  118.1 2.4 %reduce_sum.18 = f32[16,16,128]{2,1,0:T(8,128)} reduce(f32[16,16,16,128]{3,2,1,0:T(8,128)} %all-to-all-done.2, f32[]{:T(128)} %constant.26.clone.1), dimensions={0}, to_apply=%region_0.1 | reduce | flops 491520 | bytes 2228228 | tf_op jit(solution)/shard_map/reduce_sum | solution.py:142
  120.5 3.5 %all-to-all-start.3 = ((f32[16,16,128]{2,1,0:T(8,128)}), f32[16,16,128]{2,1,0:T(8,128)S(1)}, u32[]{:S(2)}, u32[]{:S(2)}) async-start(f32[16,16,128]{2,1,0:T(8,128)} %reduce_sum.18), calls=%async_computation.3 | async-start | bytes 262144 | tf_op jit(solution)/shard_map/all_to_all | solution.py:151
  124.0 0.0 collective-permute-done
  124.0 4.4 %broadcast_select_fusion.1 = (bf16[16,32768]{1,0:T(8,128)(2,1)}, bf16[16,32768]{1,0:T(8,128)(2,1)}) fusion(bf16[16,32768]{1,0:T(8,128)(2,1)} %collective-permute-done, pred[]{:T(512)S(6)} %eq.4, bf16[16,1,32768]{2,1,0:T(2,128)(2,1)} %reshape.54), kind=kLoop, calls=%fused_computation.3 | loop fusion | flops 1048576 | bytes 4194305 | tf_op jit(solution)/shard_map/jit(_where)/select_n | solution.py:146
  128.5 9.4 %all-to-all-done.3 = f32[16,16,128]{2,1,0:T(8,128)S(1)} async-done(((f32[16,16,128]{2,1,0:T(8,128)}), f32[16,16,128]{2,1,0:T(8,128)S(1)}, u32[]{:S(2)}, u32[]{:S(2)}) %all-to-all-start.3) | async-done | bytes 131104 | tf_op jit(solution)/shard_map/all_to_all | solution.py:151
  137.9 0.6 broadcast_in_dim.28
  138.5 8.6 %all-to-all-start.4 = ((f32[8,16,128]{2,1,0:T(8,128)}), f32[8,16,128]{2,1,0:T(8,128)S(1)}, u32[]{:S(2)}, u32[]{:S(2)}) async-start(f32[8,16,128]{2,1,0:T(8,128)} %broadcast_in_dim.28), calls=%async_computation.4 | async-start | bytes 131072 | tf_op jit(solution)/shard_map/all_to_all | solution.py:117
  147.1 1.7 %pad_maximum_fusion.w_ref = bf16[32,32768]{1,0:T(8,128)(2,1)S(1)} fusion(bf16[16,32768]{1,0:T(8,128)(2,1)} %get-tuple-element.8, bf16[16,32768]{1,0:T(8,128)(2,1)} %get-tuple-element.7), kind=kLoop, calls=%fused_computation | loop fusion | flops 4194304 | bytes 4194304 | tf_op jit(solution)/shard_map/concatenate | solution.py:148
  148.8 7.1 %project.1 = (bf16[256,1024]{1,0:T(8,128)(2,1)}, bf16[256,4096]{1,0:T(8,128)(2,1)}) custom-call(s32[64]{0:T(128)S(1)} %fusion.code_ref, bf16[256,4096]{1,0:T(8,128)(2,1)S(1)} %copy-done.2, bf16[256,1024]{1,0:T(8,128)(2,1)S(1)} %copy-done.4, bf16[32,32768]{1,0:T(8,128)(2,1)S(1)} %pad_maximum_fusion.w_ref), custom_call_target="tpu_custom_call" | custom-call | tf_op jit(solution)/shard_map/project/pallas_call | solution.py:98
  156.0 0.0 all-to-all-done.4
  156.0 0.6 broadcast_multiply_fusion
  (6 shorter events, 0.1 us)
Async XLA Ops:
  0.6 0.8 copy-start
  3.4 37.3 %all-to-all-start = ((bf16[64,8,128]{2,1,0:T(8,128)(2,1)}), bf16[64,8,128]{2,1,0:T(8,128)(2,1)S(1)}, u32[]{:S(2)}, u32[]{:S(2)}) async-start(bf16[64,8,128]{2,1,0:T(8,128)(2,1)} %bitcast.4), calls=%async_computation | async-start | bytes 262144 | tf_op jit(solution)/shard_map/all_to_all | solution.py:132
  42.0 1.6 %copy-start.1 = (bf16[256,4096]{1,0:T(8,128)(2,1)S(1)}, bf16[256,4096]{1,0:T(8,128)(2,1)}, u32[]{:S(2)}) copy-start(bf16[256,4096]{1,0:T(8,128)(2,1)} %x_ref.5) | copy-start | bytes 6291460
  43.6 1.0 copy-start.3
  47.9 22.2 %collective-permute-start.1 = (f32[16,16,16,128]{3,2,1,0:T(8,128)}, f32[16,16,16,128]{3,2,1,0:T(8,128)}, u32[]{:S(2)}, u32[]{:S(2)}) collective-permute-start(f32[16,16,16,128]{3,2,1,0:T(8,128)} %block_grads.3), channel_id=1, source_target_pairs={{0,8},{8,0},{1,9},{9,1},{2,10},{10,2},{3,11},{11,3},{4,12},{12,4},... | collective-permute-start | bytes 6291464 | tf_op jit(solution)/shard_map/ppermute | solution.py:138
  60.3 7.7 %copy-start.2 = (bf16[256,4096]{1,0:T(8,128)(2,1)S(1)}, bf16[256,4096]{1,0:T(8,128)(2,1)}, u32[]{:S(2)}) copy-start(bf16[256,4096]{1,0:T(8,128)(2,1)} %x_ref.5) | copy-start | bytes 6291460
  60.3 7.7 %copy-start.4 = (bf16[256,1024]{1,0:T(8,128)(2,1)S(1)}, bf16[256,1024]{1,0:T(8,128)(2,1)}, u32[]{:S(2)}) copy-start(bf16[256,1024]{1,0:T(8,128)(2,1)} %g_ref.5) | copy-start | bytes 1572868
  63.1 20.0 %all-to-all-start.1 = ((bf16[16,2,16384]{2,1,0:T(2,128)(2,1)}), bf16[16,2,16384]{2,1,0:T(2,128)(2,1)}, u32[]{:S(2)}, u32[]{:S(2)}) async-start(bf16[16,2,16384]{2,1,0:T(2,128)(2,1)} %reshape.53), calls=%async_computation.1 | async-start | bytes 2097152 | tf_op jit(solution)/shard_map/all_to_all | solution.py:117
  83.1 35.0 %all-to-all-start.2 = ((f32[16,16,16,128]{3,2,1,0:T(8,128)}), f32[16,16,16,128]{3,2,1,0:T(8,128)}, u32[]{:S(2)}, u32[]{:S(2)}) async-start(f32[16,16,16,128]{3,2,1,0:T(8,128)} %add.18), calls=%async_computation.2 | async-start | bytes 4194304 | tf_op jit(solution)/shard_map/all_to_all | solution.py:141
  101.2 22.8 %collective-permute-start = (bf16[16,32768]{1,0:T(8,128)(2,1)}, bf16[16,32768]{1,0:T(8,128)(2,1)}, u32[]{:S(2)}, u32[]{:S(2)}) collective-permute-start(bf16[16,32768]{1,0:T(8,128)(2,1)} %bitcast.15), channel_id=1, source_target_pairs={{0,8},{8,0},{1,9},{9,1},{2,10},{10,2},{3,11},{11,3},{4,12},{12,4},... | collective-permute-start | bytes 3145736 | tf_op jit(solution)/shard_map/ppermute | solution.py:145
  120.5 17.4 %all-to-all-start.3 = ((f32[16,16,128]{2,1,0:T(8,128)}), f32[16,16,128]{2,1,0:T(8,128)S(1)}, u32[]{:S(2)}, u32[]{:S(2)}) async-start(f32[16,16,128]{2,1,0:T(8,128)} %reduce_sum.18), calls=%async_computation.3 | async-start | bytes 262144 | tf_op jit(solution)/shard_map/all_to_all | solution.py:151
  138.5 17.4 %all-to-all-start.4 = ((f32[8,16,128]{2,1,0:T(8,128)}), f32[8,16,128]{2,1,0:T(8,128)S(1)}, u32[]{:S(2)}, u32[]{:S(2)}) async-start(f32[8,16,128]{2,1,0:T(8,128)} %broadcast_in_dim.28), calls=%async_computation.4 | async-start | bytes 131072 | tf_op jit(solution)/shard_map/all_to_all | solution.py:117

commit v2 on v1

--- a/solution.py
+++ b/solution.py
@@ -14,7 +14,10 @@
 PLANE = ("yh", "x", "yl")
 B = 128
 NNZ, RB, CB = 64, 32, 8
-VMEM = pltpu.CompilerParams(vmem_limit_bytes=48 * 1024 * 1024)
+
+
+def vmem_mib(limit):
+    return pltpu.CompilerParams(vmem_limit_bytes=limit * 1024 * 1024)
 
 
 def grads_kernel(parity_ref, code_ref, x_ref, g_ref, out_ref):
@@ -41,16 +44,55 @@
         out_shape=jax.ShapeDtypeStruct((16, 16, 16, B), jnp.float32),
         in_specs=[smem, smem, vmem, vmem],
         out_specs=vmem,
-        compiler_params=VMEM,
+        compiler_params=vmem_mib(8),
         name="block_grads",
     )(parity.reshape(1), codes, x, g)
 
 
-def project_kernel(code_ref, x_ref, g_ref, w_ref, v_ref, d_ref, by_col, by_row, fill):
-    for k in range(CB):
+def share_kernel(got_ref, power_ref, share_ref, wide):
+    wide[...] = got_ref[...].astype(jnp.float32).reshape(NNZ * 4, B)
+    power = jnp.concatenate([power_ref[...]] * 2, axis=0).astype(jnp.bfloat16)
+    for i in range(2):
+        rows = wide[pl.ds(i, NNZ, stride=4), :].astype(jnp.bfloat16)
+        for copy in range(16):
+            share_ref[copy, i * NNZ : (i + 1) * NNZ, :] = rows
+    for copy in range(16):
+        share_ref[copy, 2 * NNZ :, :] = power
+
+
+def share_copies(got, power):
+    vmem = pl.BlockSpec(memory_space=pltpu.VMEM)
+    return pl.pallas_call(
+        share_kernel,
+        out_shape=jax.ShapeDtypeStruct((16, 2 * NNZ + 16, B), jnp.bfloat16),
+        in_specs=[vmem, vmem],
+        out_specs=vmem,
+        scratch_shapes=[pltpu.VMEM((NNZ * 4, B), jnp.float32)],
+        compiler_params=vmem_mib(4),
+        name="share",
+    )(got, power)
+
+
+def project_kernel(place_ref, code_ref, x_ref, g_ref, w00_ref, w01_ref, w1_ref, v_ref, d_ref, by_col, by_row, fill, wide, w):
+    core, odd = place_ref[0], place_ref[1]
+    for s in range(16):
+        for c_ref, at in (
+            (w00_ref.at[s], core * 32 + odd * 16 + s),
+            (w01_ref.at[s], core * 32 + (1 - odd) * 16 + s),
+            (w1_ref.at[0, s], (1 - core) * 32 + odd * 16 + s),
+            (w1_ref.at[1, s], (1 - core) * 32 + (1 - odd) * 16 + s),
+        ):
+            wide[pl.ds(pl.multiple_of(at * 128, 128), 128), :] = c_ref[: 2 * NNZ].astype(
+                jnp.float32
+            )
+    for n in range(NNZ):
+        for i in range(2):
+            w[n, i * 64 : (i + 1) * 64, :] = wide[
+                pl.ds(i * NNZ + n, 64, stride=128), :
+            ].astype(jnp.bfloat16)
+
+    for k in range(CB + RB):
         fill[k] = 0
-    for k in range(RB):
-        fill[CB + k] = 0
 
     def place(n, carry):
         code = code_ref[n]
@@ -65,18 +107,13 @@
 
     lax.fori_loop(0, NNZ, place, 0)
 
-    def block(n):
-        return jnp.concatenate(
-            [w_ref[:, pl.ds(pl.multiple_of(n * 512 + i * B, B), B)] for i in range(4)], axis=0
-        )
-
     for col in range(CB):
         ns = [by_col[col * 8 + k] for k in range(8)]
         rows = [code_ref[n] // CB for n in ns]
         xs = jnp.concatenate(
             [x_ref[:, pl.ds(pl.multiple_of(r * B, B), B)] for r in rows], axis=1
         )
-        ws = jnp.concatenate([block(n) for n in ns], axis=0)
+        ws = jnp.concatenate([w[n] for n in ns], axis=0)
         v_ref[:, col * B : (col + 1) * B] = jnp.dot(
             xs, ws, preferred_element_type=jnp.float32
         ).astype(v_ref.dtype)
@@ -86,13 +123,13 @@
         gs = jnp.concatenate(
             [g_ref[:, pl.ds(pl.multiple_of(c * B, B), B)] for c in cols], axis=1
         )
-        ws = jnp.concatenate([block(n) for n in ns], axis=1)
+        ws = jnp.concatenate([w[n] for n in ns], axis=1)
         d_ref[:, row * B : (row + 1) * B] = lax.dot_general(
             gs, ws, (((1,), (1,)), ((), ())), preferred_element_type=jnp.float32
         ).astype(d_ref.dtype)
 
 
-def project(codes, x, g, w):
+def project(place, codes, x, g, near, next_to, far):
     smem = pl.BlockSpec(memory_space=pltpu.SMEM)
     vmem = pl.BlockSpec(memory_space=pltpu.VMEM)
     return pl.pallas_call(
@@ -101,16 +138,23 @@
             jax.ShapeDtypeStruct(g.shape, jnp.bfloat16),
             jax.ShapeDtypeStruct(x.shape, jnp.bfloat16),
         ],
-        in_specs=[smem, vmem, vmem, vmem],
+        in_specs=[smem, smem, vmem, vmem, vmem, vmem, vmem],
         out_specs=[vmem, vmem],
         scratch_shapes=[
             pltpu.SMEM((NNZ,), jnp.int32),
             pltpu.SMEM((NNZ,), jnp.int32),
             pltpu.SMEM((CB + RB,), jnp.int32),
+            pltpu.VMEM((32 * 256, B), jnp.float32),
+            pltpu.VMEM((NNZ, B, B), jnp.bfloat16),
         ],
-        compiler_params=VMEM,
+        compiler_params=vmem_mib(20),
         name="project",
-    )(codes, x, g, w)
+    )(place, codes, x, g, near, next_to, far)
+
+
+def flip(value, axis, by=1):
+    size = lax.axis_size(axis)
+    return lax.ppermute(value, axis, [(i, i ^ by) for i in range(size)])
 
 
 def to_all(part, axes, count):
@@ -122,34 +166,40 @@
 def per_device(x, blocks, block_row, block_column, g):
     core = lax.axis_index("c")
     rep = lax.axis_index(REP)
-    pieces = blocks.reshape(4, 2, 2, 8, B)
-    mine = lax.dynamic_index_in_dim(pieces, rep, 3, keepdims=False)
-    mine = mine.transpose(2, 1, 0, 3)
+    pieces = blocks.reshape(2, 2, 2, 2, 8, B)
+    mine = lax.dynamic_index_in_dim(pieces, rep, 4, keepdims=False)
+    mine = mine.transpose(3, 2, 1, 0, 4)
     code = (block_row * CB + block_column).astype(jnp.bfloat16)
-    tail = jnp.broadcast_to(code.reshape(1, 1, 1, 1), (2, 2, 4, B))
-    packet = jnp.concatenate([mine, tail], axis=2)
-    packet = jnp.broadcast_to(packet[:, None], (2, 16, 2, 8, B)).reshape(64, 8, B)
+    tail = jnp.broadcast_to(code.reshape(1, 1, 1, 1, 1), (2, 2, 2, 2, B))
+    packet = jnp.concatenate([mine, tail], axis=3)[:, None]
+    packet = jnp.broadcast_to(packet, (2, 8, 2, 2, 4, B)).reshape(NNZ, 4, B)
     got = lax.all_to_all(packet, FSDP, 0, 0, tiled=True)
-    codes = got[:, 4, 0].astype(jnp.int32)
-    share = got[:, :4, :].reshape(NNZ * 512)
-
-    other = half_grads(1 - core, codes, x, g)
-    swap = [(0, 1), (1, 0)]
-    incoming = lax.ppermute(other, "c", swap)
+    top = jnp.max(jnp.abs(x)).astype(jnp.float32) * jnp.max(jnp.abs(g)).astype(jnp.float32)
+    power = jnp.floor(jnp.log2(16384.0 / (x.shape[0] * jnp.maximum(top, 1e-30))))
+    power = jnp.broadcast_to(power, (8, B))
+    power = jnp.minimum(power, flip(power, "c"))
+
+    got, power = lax.optimization_barrier((got, power))
+    share = share_copies(got, power)
+    codes = got[:, 2, 0].astype(jnp.int32)
+    share, codes = lax.optimization_barrier((share, codes))
+    near = lax.all_to_all(share, PLANE, 0, 0, tiled=True)
+
+    incoming = flip(half_grads(1 - core, codes, x, g), "c")
     own = half_grads(core, codes, x, g)
-    paired = own + incoming
+    paired = ((own + incoming) * jnp.exp2(power[0, 0])).astype(jnp.float16)
     spread = lax.all_to_all(paired, PLANE, 0, 0, tiled=True)
-    plane_sum = jnp.sum(spread, axis=0)
-
-    half_w = to_all(share, PLANE, 16)
-    far_w = lax.ppermute(half_w, "c", swap)
-    low = jnp.where(core == 0, half_w, far_w)
-    high = jnp.where(core == 0, far_w, half_w)
-    w = jnp.concatenate([low, high], axis=0)
-    values_out, input_grad = project(codes, x, g, w)
+    down = jnp.exp2(-near[:, 2 * NNZ, 0].astype(jnp.float32))
+    plane_sum = jnp.sum(spread.astype(jnp.float32) * down[:, None, None, None], axis=0)
+
+    next_to = flip(near, "z")
+    far = flip(jnp.stack([near, next_to]), "c")
+    place = jnp.stack([core, lax.axis_index("z") % 2]).astype(jnp.int32)
+    values_out, input_grad = project(place, codes, x, g, near, next_to, far)
 
     ring = lax.all_to_all(plane_sum, "z", 0, 0, tiled=True)
     strip = jnp.sum(ring, axis=0)
+    strip, values_out = lax.optimization_barrier((strip, values_out))
     whole = to_all(strip, REP, 8)
     loss_scale = (x.shape[0] * lax.axis_size(AXES)) ** (-0.5)
     weight_grad = whole.reshape(1, B, B) * loss_scale

time: 158 us -> 122 us (0.77)
  the two profiles are of different devices: /device:TPU:2 before, /device:TPU:8 now
where the time goes in v2:
time: 122 us; the launch traced here: 121 us
  starting transfers between devices  44.2 us (36%)
  waiting for transfers between devices  29.7 us (24%)
  Pallas kernels  15.6 us (13%)
  other arithmetic  14.3 us (12%)
  blocking collectives  9 us (7%)
  between operations  4.23 us (3%)
  local copies, waits for them, and re-layouts  4.08 us (3%)
    all_to_all x1, starting transfers between devices, per_device(): got = lax.all_to_all(packet, FSDP, 0, 0, tiled=True)  17.8 us
    pallas_call x1, Pallas kernels, project(): pl.pallas_call(project_kernel, out_shape=[jax.ShapeDtypeStruct(g.shape, j...  10.3 us
    all_to_all x1, blocking collectives, to_all(): lax.all_to_all(jnp.broadcast_to(part[None], (count,) + part.shape), axes,...  9 us
    ppermute x4, starting transfers between devices, flip(): return lax.ppermute(value, axis, [(i, i ^ by) for i in range(size)])  8.65 us
    all_to_all x1, waiting for transfers between devices, per_device(): got = lax.all_to_all(packet, FSDP, 0, 0, tiled=True)  7.37 us
    all_to_all x1, waiting for transfers between devices, per_device(): spread = lax.all_to_all(paired, PLANE, 0, 0, tiled=True)  7.07 us
    all_to_all x1, waiting for transfers between devices, per_device(): near = lax.all_to_all(share, PLANE, 0, 0, tiled=True)  7.05 us
    all_to_all x1, starting transfers between devices, per_device(): ring = lax.all_to_all(plane_sum, 'z', 0, 0, tiled=True)  6.41 us
  transfers between devices with their start and end apart: 8, of which 6 were waited for; matrix products, arithmetic and copies ran while one was open for 11% of the time, Pallas kernels for 10%

profile of v2, /device:TPU:8, one launch (start us, length us, event | category | flops | bytes accessed | tf_op | source)
XLA Modules:
  0.0 121.2 jit_solution(9375129897015692114)
XLA Ops:
  0.6 0.0 copy-start
  0.6 0.0 copy-start.1
  0.7 0.0 copy-start.3
  0.7 0.7 copy-done
  2.8 0.6 broadcast_in_dim.9
  3.4 17.8 %all-to-all-start = ((bf16[64,4,128]{2,1,0:T(4,128)(2,1)}), bf16[64,4,128]{2,1,0:T(4,128)(2,1)S(1)}, u32[]{:S(2)}, u32[]{:S(2)}) async-start(bf16[64,4,128]{2,1,0:T(4,128)(2,1)} %bitcast.5), calls=%async_computation | async-start | bytes 131072 | tf_op jit(solution)/shard_map/all_to_all | solution.py:176
  21.3 2.5 %abs_reduce_fusion = bf16[]{:T(256)} fusion(bf16[256,4096]{1,0:T(8,128)(2,1)} %x_ref.5), kind=kLoop, calls=%fused_computation.2 | loop fusion | flops 2097151 | bytes 2097154 | tf_op jit(solution)/shard_map/reduce_max | solution.py:177
  23.7 1.7 %abs_reduce_fusion.1 = bf16[]{:T(256)} fusion(bf16[256,1024]{1,0:T(8,128)(2,1)} %g_ref.5), kind=kLoop, calls=%fused_computation.4 | loop fusion | flops 524287 | bytes 524290 | tf_op jit(solution)/shard_map/reduce_max | solution.py:177
  26.9 2.0 %collective-permute-start = (f32[8,128]{1,0:T(8,128)S(1)}, f32[8,128]{1,0:T(8,128)S(1)}, u32[]{:S(2)}, u32[]{:S(2)}) collective-permute-start(f32[8,128]{1,0:T(8,128)S(1)} %broadcast_in_dim.10), channel_id=1, source_target_pairs={{0,8},{8,0},{1,9},{9,1},{2,10},{10,2},{3,11},{11,3},{4,12},{12,4},... | collective-permute-start | bytes 12296 | tf_op jit(solution)/shard_map/ppermute | solution.py:157
  28.8 1.1 collective-permute-done
  29.9 7.4 %all-to-all-done.got_ref = bf16[64,4,128]{2,1,0:T(4,128)(2,1)S(1)} async-done(((bf16[64,4,128]{2,1,0:T(4,128)(2,1)}), bf16[64,4,128]{2,1,0:T(4,128)(2,1)S(1)}, u32[]{:S(2)}, u32[]{:S(2)}) %all-to-all-start) | async-done | bytes 65568 | tf_op jit(solution)/shard_map/all_to_all | solution.py:176
  37.3 1.2 %convert_reduce_fusion.code_ref = s32[64]{0:T(128)S(1)} fusion(bf16[64,4,128]{2,1,0:T(4,128)(2,1)S(1)} %all-to-all-done.got_ref), kind=kLoop, calls=%fused_computation.5 | loop fusion | flops 64 | bytes 384 | tf_op jit(solution)/shard_map/convert_element_type | solution.py:184
  38.5 0.1 share.1
  38.6 0.0 copy-start.4
  38.6 0.8 copy-done.4
  39.4 0.0 copy-done.1
  39.4 0.0 copy-done.3
  39.4 3.3 %block_grads.3 = f32[16,16,16,128]{3,2,1,0:T(8,128)} custom-call(s32[1]{0:T(128)} %bitcast.6.parity_ref, s32[64]{0:T(128)S(1)} %convert_reduce_fusion.code_ref, bf16[256,4096]{1,0:T(8,128)(2,1)S(1)} %copy-done.1, bf16[256,1024]{1,0:T(8,128)(2,1)S(1)} %copy-done.3), custom_call_target="tpu_custom_call" | custom-call | tf_op jit(solution)/shard_map/block_grads/pallas_call | solution.py:42
  42.7 2.0 %collective-permute-start.1 = (f32[16,16,16,128]{3,2,1,0:T(8,128)}, f32[16,16,16,128]{3,2,1,0:T(8,128)}, u32[]{:S(2)}, u32[]{:S(2)}) collective-permute-start(f32[16,16,16,128]{3,2,1,0:T(8,128)} %block_grads.3), channel_id=1, source_target_pairs={{0,8},{8,0},{1,9},{9,1},{2,10},{10,2},{3,11},{11,3},{4,12},{12,4},... | collective-permute-start | bytes 6291464 | tf_op jit(solution)/shard_map/ppermute | solution.py:157
  44.7 5.8 %all-to-all-start.2 = ((bf16[16,144,128]{2,1,0:T(8,128)(2,1)}), bf16[16,144,128]{2,1,0:T(8,128)(2,1)S(1)}, u32[]{:S(2)}, u32[]{:S(2)}) async-start(bf16[16,144,128]{2,1,0:T(8,128)(2,1)} %copy-done.4), calls=%async_computation.2 | async-start | bytes 1179648 | tf_op jit(solution)/shard_map/all_to_all | solution.py:186
  50.5 0.5 slice.10
  51.1 2.0 %block_grads.2 = f32[16,16,16,128]{3,2,1,0:T(8,128)S(1)} custom-call(s32[1]{0:T(128)} %bitcast.parity_ref, s32[64]{0:T(128)S(1)} %convert_reduce_fusion.code_ref, bf16[256,4096]{1,0:T(8,128)(2,1)S(1)} %copy-done.1, bf16[256,1024]{1,0:T(8,128)(2,1)S(1)} %copy-done.3), custom_call_target="tpu_custom_call" | custom-call | tf_op jit(solution)/shard_map/block_grads/pallas_call | solution.py:42
  53.0 0.0 copy-start.2
  53.0 1.3 %copy-done.2 = f32[16,16,16,128]{3,2,1,0:T(8,128)} copy-done((f32[16,16,16,128]{3,2,1,0:T(8,128)}, f32[16,16,16,128]{3,2,1,0:T(8,128)S(1)}, u32[]{:S(2)}) %copy-start.2) | copy-done | bytes 2097176
  55.0 7.1 %all-to-all-done.2.w00_ref = bf16[16,144,128]{2,1,0:T(8,128)(2,1)S(1)} async-done(((bf16[16,144,128]{2,1,0:T(8,128)(2,1)}), bf16[16,144,128]{2,1,0:T(8,128)(2,1)S(1)}, u32[]{:S(2)}, u32[]{:S(2)}) %all-to-all-start.2) | async-done | bytes 589856 | tf_op jit(solution)/shard_map/all_to_all | solution.py:186
  62.1 2.8 %collective-permute-start.2 = (bf16[16,144,128]{2,1,0:T(8,128)(2,1)S(1)}, bf16[16,144,128]{2,1,0:T(8,128)(2,1)}, u32[]{:S(2)}, u32[]{:S(2)}) collective-permute-start(bf16[16,144,128]{2,1,0:T(8,128)(2,1)S(1)} %all-to-all-done.2.w00_ref), channel_id=1, source_target_pairs={{0,16},{16,0},{32,48},{48,32},{64,80},{80,64},{96,112},{112,96},{1... | collective-permute-start | bytes 1769480 | tf_op jit(solution)/shard_map/ppermute | solution.py:157
  64.9 0.0 collective-permute-done.1
  64.9 3.5 %multiply_convert_fusion = f16[16,16,16,128]{3,2,1,0:T(8,128)(2,1)} fusion(f32[16,16,16,128]{3,2,1,0:T(8,128)} %copy-done.2, f32[16,16,16,128]{3,2,1,0:T(8,128)} %collective-permute-done.1, f32[]{:T(128)} %bitcast.7), kind=kLoop, calls=%fused_computation.1 | loop fusion | flops 1572864 | bytes 5242884 | tf_op jit(solution)/shard_map/convert_element_type | solution.py:190
  68.4 5.5 %all-to-all-start.1 = ((f16[16,16,16,128]{3,2,1,0:T(8,128)(2,1)}), f16[16,16,16,128]{3,2,1,0:T(8,128)(2,1)}, u32[]{:S(2)}, u32[]{:S(2)}) async-start(f16[16,16,16,128]{3,2,1,0:T(8,128)(2,1)} %multiply_convert_fusion), calls=%async_computation.1 | async-start | bytes 2097152 | tf_op jit(solution)/shard_map/all_to_all | solution.py:191
  73.9 4.3 %collective-permute-done.2.w01_ref = bf16[16,144,128]{2,1,0:T(8,128)(2,1)} collective-permute-done((bf16[16,144,128]{2,1,0:T(8,128)(2,1)S(1)}, bf16[16,144,128]{2,1,0:T(8,128)(2,1)}, u32[]{:S(2)}, u32[]{:S(2)}) %collective-permute-start.2) | collective-permute-done | bytes 589856 | tf_op jit(solution)/shard_map/ppermute | solution.py:157
  78.3 2.2 %pad_maximum_fusion = bf16[2,16,144,128]{3,2,1,0:T(8,128)(2,1)} fusion(bf16[1,16,144,128]{3,2,1,0:T(8,128)(2,1)} %bitcast.10, bf16[1,16,144,128]{3,2,1,0:T(8,128)(2,1)S(1)} %bitcast.17), kind=kLoop, calls=%fused_computation.3 | loop fusion | flops 589824 | bytes 2359296 | tf_op jit(solution)/shard_map/stack | solution.py:196
  80.5 1.9 %collective-permute-start.3 = (bf16[2,16,144,128]{3,2,1,0:T(8,128)(2,1)}, bf16[2,16,144,128]{3,2,1,0:T(8,128)(2,1)}, u32[]{:S(2)}, u32[]{:S(2)}) collective-permute-start(bf16[2,16,144,128]{3,2,1,0:T(8,128)(2,1)} %pad_maximum_fusion), channel_id=1, source_target_pairs={{0,8},{8,0},{1,9},{9,1},{2,10},{10,2},{3,11},{11,3},{4,12},{12,4},... | collective-permute-start | bytes 3538952 | tf_op jit(solution)/shard_map/ppermute | solution.py:157
  82.4 0.2 fusion.3
  82.6 7.1 %all-to-all-done.1 = f16[16,16,16,128]{3,2,1,0:T(8,128)(2,1)} async-done(((f16[16,16,16,128]{3,2,1,0:T(8,128)(2,1)}), f16[16,16,16,128]{3,2,1,0:T(8,128)(2,1)}, u32[]{:S(2)}, u32[]{:S(2)}) %all-to-all-start.1) | async-done | bytes 1048608 | tf_op jit(solution)/shard_map/all_to_all | solution.py:191
  89.7 2.2 %multiply_reduce_fusion = f32[16,16,128]{2,1,0:T(8,128)} fusion(f16[16,16,16,128]{3,2,1,0:T(8,128)(2,1)} %all-to-all-done.1, f32[16]{0:T(128)S(1)} %fusion.3), kind=kLoop, calls=%fused_computation | loop fusion | flops 1540096 | bytes 1179712 | tf_op jit(solution)/shard_map/reduce_sum | solution.py:193
  91.8 6.4 %all-to-all-start.3 = ((f32[16,16,128]{2,1,0:T(8,128)}), f32[16,16,128]{2,1,0:T(8,128)S(1)}, u32[]{:S(2)}, u32[]{:S(2)}) async-start(f32[16,16,128]{2,1,0:T(8,128)} %multiply_reduce_fusion), calls=%async_computation.3 | async-start | bytes 262144 | tf_op jit(solution)/shard_map/all_to_all | solution.py:200
  98.3 0.1 pad_add_fusion.place_ref
  98.3 0.0 collective-permute-done.3.w1_ref
  98.4 10.3 %project.1 = (bf16[256,1024]{1,0:T(8,128)(2,1)}, bf16[256,4096]{1,0:T(8,128)(2,1)}) custom-call(s32[2]{0:T(128)S(1)} %pad_add_fusion.place_ref, s32[64]{0:T(128)S(1)} %convert_reduce_fusion.code_ref, bf16[256,4096]{1,0:T(8,128)(2,1)S(1)} %copy-done.1, bf16[256,1024]{1,0:T(8,128)(2,1)S(1)} %copy-done.3, bf16[16,144,128]{2,1,0:T(8,128)(2,1)S(1)} %all-to-all-done.2.w00_ref, ...), custom_call_target="tpu_custom_call" | custom-call | tf_op jit(solution)/shard_map/project/pallas_call | solution.py:135
  108.7 2.8 %all-to-all-done.3 = f32[16,16,128]{2,1,0:T(8,128)S(1)} async-done(((f32[16,16,128]{2,1,0:T(8,128)}), f32[16,16,128]{2,1,0:T(8,128)S(1)}, u32[]{:S(2)}, u32[]{:S(2)}) %all-to-all-start.3) | async-done | bytes 131104 | tf_op jit(solution)/shard_map/all_to_all | solution.py:200
  111.5 9.0 %all_to_all.25 = f32[8,16,128]{2,1,0:T(8,128)S(1)} all-to-all(f32[8,16,128]{2,1,0:T(8,128)S(1)} %broadcast_in_dim.11), channel_id=1, replica_groups=mesh['yh'=2,'z'=16,'c'=2,'x'=4,'yl'=2] {'x','yl'}, dimensions={0} | all-to-all | bytes 131072 | tf_op jit(solution)/shard_map/all_to_all | solution.py:161
  120.5 0.6 broadcast_multiply_fusion
  (7 shorter events, 0.1 us)
Async XLA Ops:
  0.6 0.8 copy-start
  0.6 38.8 %copy-start.1 = (bf16[256,4096]{1,0:T(8,128)(2,1)S(1)}, bf16[256,4096]{1,0:T(8,128)(2,1)}, u32[]{:S(2)}) copy-start(bf16[256,4096]{1,0:T(8,128)(2,1)} %x_ref.5) | copy-start | bytes 6291460
  0.7 38.8 %copy-start.3 = (bf16[256,1024]{1,0:T(8,128)(2,1)S(1)}, bf16[256,1024]{1,0:T(8,128)(2,1)}, u32[]{:S(2)}) copy-start(bf16[256,1024]{1,0:T(8,128)(2,1)} %g_ref.5) | copy-start | bytes 1572868
  3.4 33.9 %all-to-all-start = ((bf16[64,4,128]{2,1,0:T(4,128)(2,1)}), bf16[64,4,128]{2,1,0:T(4,128)(2,1)S(1)}, u32[]{:S(2)}, u32[]{:S(2)}) async-start(bf16[64,4,128]{2,1,0:T(4,128)(2,1)} %bitcast.5), calls=%async_computation | async-start | bytes 131072 | tf_op jit(solution)/shard_map/all_to_all | solution.py:176
  26.9 3.1 %collective-permute-start = (f32[8,128]{1,0:T(8,128)S(1)}, f32[8,128]{1,0:T(8,128)S(1)}, u32[]{:S(2)}, u32[]{:S(2)}) collective-permute-start(f32[8,128]{1,0:T(8,128)S(1)} %broadcast_in_dim.10), channel_id=1, source_target_pairs={{0,8},{8,0},{1,9},{9,1},{2,10},{10,2},{3,11},{11,3},{4,12},{12,4},... | collective-permute-start | bytes 12296 | tf_op jit(solution)/shard_map/ppermute | solution.py:157
  38.6 0.8 copy-start.4
  42.7 22.2 %collective-permute-start.1 = (f32[16,16,16,128]{3,2,1,0:T(8,128)}, f32[16,16,16,128]{3,2,1,0:T(8,128)}, u32[]{:S(2)}, u32[]{:S(2)}) collective-permute-start(f32[16,16,16,128]{3,2,1,0:T(8,128)} %block_grads.3), channel_id=1, source_target_pairs={{0,8},{8,0},{1,9},{9,1},{2,10},{10,2},{3,11},{11,3},{4,12},{12,4},... | collective-permute-start | bytes 6291464 | tf_op jit(solution)/shard_map/ppermute | solution.py:157
  44.7 17.4 %all-to-all-start.2 = ((bf16[16,144,128]{2,1,0:T(8,128)(2,1)}), bf16[16,144,128]{2,1,0:T(8,128)(2,1)S(1)}, u32[]{:S(2)}, u32[]{:S(2)}) async-start(bf16[16,144,128]{2,1,0:T(8,128)(2,1)} %copy-done.4), calls=%async_computation.2 | async-start | bytes 1179648 | tf_op jit(solution)/shard_map/all_to_all | solution.py:186
  53.0 1.3 %copy-start.2 = (f32[16,16,16,128]{3,2,1,0:T(8,128)}, f32[16,16,16,128]{3,2,1,0:T(8,128)S(1)}, u32[]{:S(2)}) copy-start(f32[16,16,16,128]{3,2,1,0:T(8,128)S(1)} %block_grads.2) | copy-start | bytes 6291460
  62.1 16.2 %collective-permute-start.2 = (bf16[16,144,128]{2,1,0:T(8,128)(2,1)S(1)}, bf16[16,144,128]{2,1,0:T(8,128)(2,1)}, u32[]{:S(2)}, u32[]{:S(2)}) collective-permute-start(bf16[16,144,128]{2,1,0:T(8,128)(2,1)S(1)} %all-to-all-done.2.w00_ref), channel_id=1, source_target_pairs={{0,16},{16,0},{32,48},{48,32},{64,80},{80,64},{96,112},{112,96},{1... | collective-permute-start | bytes 1769480 | tf_op jit(solution)/shard_map/ppermute | solution.py:157
  68.4 21.2 %all-to-all-start.1 = ((f16[16,16,16,128]{3,2,1,0:T(8,128)(2,1)}), f16[16,16,16,128]{3,2,1,0:T(8,128)(2,1)}, u32[]{:S(2)}, u32[]{:S(2)}) async-start(f16[16,16,16,128]{3,2,1,0:T(8,128)(2,1)} %multiply_convert_fusion), calls=%async_computation.1 | async-start | bytes 2097152 | tf_op jit(solution)/shard_map/all_to_all | solution.py:191
  80.5 17.9 %collective-permute-start.3 = (bf16[2,16,144,128]{3,2,1,0:T(8,128)(2,1)}, bf16[2,16,144,128]{3,2,1,0:T(8,128)(2,1)}, u32[]{:S(2)}, u32[]{:S(2)}) collective-permute-start(bf16[2,16,144,128]{3,2,1,0:T(8,128)(2,1)} %pad_maximum_fusion), channel_id=1, source_target_pairs={{0,8},{8,0},{1,9},{9,1},{2,10},{10,2},{3,11},{11,3},{4,12},{12,4},... | collective-permute-start | bytes 3538952 | tf_op jit(solution)/shard_map/ppermute | solution.py:157
  91.8 19.7 %all-to-all-start.3 = ((f32[16,16,128]{2,1,0:T(8,128)}), f32[16,16,128]{2,1,0:T(8,128)S(1)}, u32[]{:S(2)}, u32[]{:S(2)}) async-start(f32[16,16,128]{2,1,0:T(8,128)} %multiply_reduce_fusion), calls=%async_computation.3 | async-start | bytes 262144 | tf_op jit(solution)/shard_map/all_to_all | solution.py:200

commit v3 on v2

--- a/solution.py
+++ b/solution.py
@@ -73,23 +73,37 @@
     )(got, power)
 
 
-def project_kernel(place_ref, code_ref, x_ref, g_ref, w00_ref, w01_ref, w1_ref, v_ref, d_ref, by_col, by_row, fill, wide, w):
-    core, odd = place_ref[0], place_ref[1]
-    for s in range(16):
-        for c_ref, at in (
-            (w00_ref.at[s], core * 32 + odd * 16 + s),
-            (w01_ref.at[s], core * 32 + (1 - odd) * 16 + s),
-            (w1_ref.at[0, s], (1 - core) * 32 + odd * 16 + s),
-            (w1_ref.at[1, s], (1 - core) * 32 + (1 - odd) * 16 + s),
-        ):
-            wide[pl.ds(pl.multiple_of(at * 128, 128), 128), :] = c_ref[: 2 * NNZ].astype(
+def stage_kernel(parity_ref, near_ref, next_ref, w_ref, wide):
+    for slots, at in ((near_ref, parity_ref[0]), (next_ref, 1 - parity_ref[0])):
+        for s in range(16):
+            wide[pl.ds(pl.multiple_of((at * 16 + s) * B, B), B), :] = slots[s, :B].astype(
                 jnp.float32
             )
     for n in range(NNZ):
         for i in range(2):
-            w[n, i * 64 : (i + 1) * 64, :] = wide[
-                pl.ds(i * NNZ + n, 64, stride=128), :
+            w_ref[n, i * 32 : (i + 1) * 32, :] = wide[
+                pl.ds(i * NNZ + n, 32, stride=B), :
             ].astype(jnp.bfloat16)
+
+
+def stage(parity, near, next_to):
+    vmem = pl.BlockSpec(memory_space=pltpu.VMEM)
+    return pl.pallas_call(
+        stage_kernel,
+        out_shape=jax.ShapeDtypeStruct((NNZ, B // 2, B), jnp.bfloat16),
+        in_specs=[pl.BlockSpec(memory_space=pltpu.SMEM), vmem, vmem],
+        out_specs=vmem,
+        scratch_shapes=[pltpu.VMEM((32 * B, B), jnp.float32)],
+        compiler_params=vmem_mib(8),
+        name="stage",
+    )(parity, near, next_to)
+
+
+def project_kernel(core_ref, code_ref, x_ref, g_ref, near_ref, far_ref, v_ref, d_ref, by_col, by_row, fill, w):
+    for half_ref, core in ((near_ref, core_ref[0]), (far_ref, 1 - core_ref[0])):
+        for i in range(2):
+            at = pl.multiple_of(i * 64 + core * 32, 32)
+            w[:, pl.ds(at, 32), :] = half_ref[:, i * 32 : (i + 1) * 32, :]
 
     for k in range(CB + RB):
         fill[k] = 0
@@ -129,7 +143,7 @@
         ).astype(d_ref.dtype)
 
 
-def project(place, codes, x, g, near, next_to, far):
+def project(place, codes, x, g, near, far):
     smem = pl.BlockSpec(memory_space=pltpu.SMEM)
     vmem = pl.BlockSpec(memory_space=pltpu.VMEM)
     return pl.pallas_call(
@@ -138,18 +152,18 @@
             jax.ShapeDtypeStruct(g.shape, jnp.bfloat16),
             jax.ShapeDtypeStruct(x.shape, jnp.bfloat16),
         ],
-        in_specs=[smem, smem, vmem, vmem, vmem, vmem, vmem],
+        in_specs=[smem, smem, vmem, vmem, vmem, vmem],
         out_specs=[vmem, vmem],
         scratch_shapes=[
             pltpu.SMEM((NNZ,), jnp.int32),
             pltpu.SMEM((NNZ,), jnp.int32),
             pltpu.SMEM((CB + RB,), jnp.int32),
-            pltpu.VMEM((32 * 256, B), jnp.float32),
             pltpu.VMEM((NNZ, B, B), jnp.bfloat16),
         ],
         compiler_params=vmem_mib(20),
+        cost_estimate=pl.CostEstimate(flops=1, transcendentals=0, bytes_accessed=1),
         name="project",
-    )(place, codes, x, g, near, next_to, far)
+    )(place, codes, x, g, near, far)
 
 
 def flip(value, axis, by=1):
@@ -164,7 +178,7 @@
 
 
 def per_device(x, blocks, block_row, block_column, g):
-    core = lax.axis_index("c")
+    core = lax.axis_index("c").astype(jnp.int32)
     rep = lax.axis_index(REP)
     pieces = blocks.reshape(2, 2, 2, 2, 8, B)
     mine = lax.dynamic_index_in_dim(pieces, rep, 4, keepdims=False)
@@ -174,32 +188,40 @@
     packet = jnp.concatenate([mine, tail], axis=3)[:, None]
     packet = jnp.broadcast_to(packet, (2, 8, 2, 2, 4, B)).reshape(NNZ, 4, B)
     got = lax.all_to_all(packet, FSDP, 0, 0, tiled=True)
+
     top = jnp.max(jnp.abs(x)).astype(jnp.float32) * jnp.max(jnp.abs(g)).astype(jnp.float32)
     power = jnp.floor(jnp.log2(16384.0 / (x.shape[0] * jnp.maximum(top, 1e-30))))
-    power = jnp.broadcast_to(power, (8, B))
+    power = jnp.broadcast_to(power, (16, B))
     power = jnp.minimum(power, flip(power, "c"))
-
     got, power = lax.optimization_barrier((got, power))
-    share = share_copies(got, power)
-    codes = got[:, 2, 0].astype(jnp.int32)
-    share, codes = lax.optimization_barrier((share, codes))
+
+    share = share_copies(got, power[:8])
     near = lax.all_to_all(share, PLANE, 0, 0, tiled=True)
 
-    incoming = flip(half_grads(1 - core, codes, x, g), "c")
-    own = half_grads(core, codes, x, g)
-    paired = ((own + incoming) * jnp.exp2(power[0, 0])).astype(jnp.float16)
+    def grads(got, power, x, g):
+        codes = got[:, 2, 0].astype(jnp.int32)
+        up = jnp.exp2(power)
+        outgoing = (half_grads(1 - core, codes, x, g) * up).astype(jnp.float16)
+        incoming = flip(outgoing, "c").astype(jnp.float32)
+        own = half_grads(core, codes, x, g)
+        return (own * up + incoming).astype(jnp.float16), codes
+
+    def nothing(got, power, x, g):
+        return jnp.zeros((16, 16, 16, B), jnp.float16), jnp.zeros((NNZ,), jnp.int32)
+
+    paired, codes = lax.cond(block_row[0] < RB, grads, nothing, got, power, x, g)
+    paired, near = lax.optimization_barrier((paired, near))
     spread = lax.all_to_all(paired, PLANE, 0, 0, tiled=True)
-    down = jnp.exp2(-near[:, 2 * NNZ, 0].astype(jnp.float32))
-    plane_sum = jnp.sum(spread.astype(jnp.float32) * down[:, None, None, None], axis=0)
-
-    next_to = flip(near, "z")
-    far = flip(jnp.stack([near, next_to]), "c")
-    place = jnp.stack([core, lax.axis_index("z") % 2]).astype(jnp.int32)
-    values_out, input_grad = project(place, codes, x, g, near, next_to, far)
+    down = jnp.exp2(-near[:, B:].astype(jnp.float32))
+    plane_sum = jnp.sum(spread.astype(jnp.float32) * down[:, None], axis=0)
+
+    parity = (lax.axis_index("z") % 2).astype(jnp.int32).reshape(1)
+    half = stage(parity, near, flip(near, "z"))
+    values_out, input_grad = project(core.reshape(1), codes, x, g, half, flip(half, "c"))
 
     ring = lax.all_to_all(plane_sum, "z", 0, 0, tiled=True)
+    ring, values_out = lax.optimization_barrier((ring, values_out))
     strip = jnp.sum(ring, axis=0)
-    strip, values_out = lax.optimization_barrier((strip, values_out))
     whole = to_all(strip, REP, 8)
     loss_scale = (x.shape[0] * lax.axis_size(AXES)) ** (-0.5)
     weight_grad = whole.reshape(1, B, B) * loss_scale

time: 122 us -> 114 us (0.934)
  the two profiles are of different devices: /device:TPU:8 before, /device:TPU:32 now
where the time goes in v3:
time: 114 us; the launch traced here: 113 us
  starting transfers between devices  43.4 us (38%)
  waiting for transfers between devices  33.3 us (29%)
  Pallas kernels  13.3 us (12%)
  blocking collectives  11.2 us (10%)
  other arithmetic  7.7 us (7%)
  between operations  3.55 us (3%)
    all_to_all x1, starting transfers between devices, per_device(): got = lax.all_to_all(packet, FSDP, 0, 0, tiled=True)  18.4 us
    ppermute x4, waiting for transfers between devices, flip(): return lax.ppermute(value, axis, [(i, i ^ by) for i in range(size)])  14.4 us
    all_to_all x1, blocking collectives, to_all(): lax.all_to_all(jnp.broadcast_to(part[None], (count,) + part.shape), axes,...  11.2 us
    ppermute x4, starting transfers between devices, flip(): return lax.ppermute(value, axis, [(i, i ^ by) for i in range(size)])  9.05 us
    all_to_all x1, waiting for transfers between devices, per_device(): got = lax.all_to_all(packet, FSDP, 0, 0, tiled=True)  7.46 us
    all_to_all x1, waiting for transfers between devices, per_device(): ring = lax.all_to_all(plane_sum, 'z', 0, 0, tiled=True)  7.25 us
    pallas_call x1, Pallas kernels, project(): pl.pallas_call(project_kernel, out_shape=[jax.ShapeDtypeStruct(g.shape, j...  7.22 us
    all_to_all x1, starting transfers between devices, per_device(): ring = lax.all_to_all(plane_sum, 'z', 0, 0, tiled=True)  7.12 us
  transfers between devices with their start and end apart: 8, of which 6 were waited for; matrix products, arithmetic and copies ran while one was open for 6% of the time, Pallas kernels for 11%

profile of v3, /device:TPU:32, one launch (start us, length us, event | category | flops | bytes accessed | tf_op | source)
XLA Modules:
  0.0 113.5 jit_solution(14404795394777593932)
XLA Ops:
  0.6 0.0 copy-start
  0.6 0.0 copy-start.2
  1.4 0.0 copy-done
  2.1 0.6 broadcast_in_dim.9
  2.7 18.4 %all-to-all-start = ((bf16[64,4,128]{2,1,0:T(4,128)(2,1)}), bf16[64,4,128]{2,1,0:T(4,128)(2,1)S(1)}, u32[]{:S(2)}, u32[]{:S(2)}) async-start(bf16[64,4,128]{2,1,0:T(4,128)(2,1)} %bitcast.9), calls=%async_computation | async-start | bytes 131072 | tf_op jit(solution)/shard_map/all_to_all | solution.py:190
  21.1 0.0 copy-start.1
  21.2 2.6 %abs_reduce_fusion = bf16[]{:T(256)} fusion(bf16[256,4096]{1,0:T(8,128)(2,1)} %x_ref.1), kind=kLoop, calls=%fused_computation.6 | loop fusion | flops 2097151 | bytes 2097154 | tf_op jit(solution)/shard_map/reduce_max | solution.py:192
  23.8 0.0 copy-done.2
  23.8 0.7 abs_reduce_fusion.1
  25.9 2.1 %collective-permute-start.1 = (f32[16,128]{1,0:T(8,128)S(1)}, f32[16,128]{1,0:T(8,128)S(1)}, u32[]{:S(2)}, u32[]{:S(2)}) collective-permute-start(f32[16,128]{1,0:T(8,128)S(1)} %broadcast_in_dim.12), channel_id=1, source_target_pairs={{0,8},{8,0},{1,9},{9,1},{2,10},{10,2},{3,11},{11,3},{4,12},{12,4},... | collective-permute-start | bytes 24584 | tf_op jit(solution)/shard_map/ppermute | solution.py:171
  27.9 1.0 collective-permute-done.1
  28.9 7.5 %all-to-all-done.got_ref = bf16[64,4,128]{2,1,0:T(4,128)(2,1)S(1)} async-done(((bf16[64,4,128]{2,1,0:T(4,128)(2,1)}), bf16[64,4,128]{2,1,0:T(4,128)(2,1)S(1)}, u32[]{:S(2)}, u32[]{:S(2)}) %all-to-all-start) | async-done | bytes 65568 | tf_op jit(solution)/shard_map/all_to_all | solution.py:190
  36.4 0.9 share.1
  37.3 4.5 %all-to-all-start.1 = ((bf16[16,144,128]{2,1,0:T(8,128)(2,1)}), bf16[16,144,128]{2,1,0:T(8,128)(2,1)S(1)}, u32[]{:S(2)}, u32[]{:S(2)}) async-start(bf16[16,144,128]{2,1,0:T(8,128)(2,1)} %share.1), calls=%async_computation.1 | async-start | bytes 1179648 | tf_op jit(solution)/shard_map/all_to_all | solution.py:199
  41.8 0.0 copy-done.1
  41.8 8.3 %conditional.1 = (f16[16,16,16,128]{3,2,1,0:T(8,128)(2,1)}, s32[64]{0:T(128)S(1)}) conditional(s32[]{:T(128)} %bitcast.4, () %tuple.19, (s32[]{:T(128)}, bf16[64,4,128]{2,1,0:T(4,128)(2,1)S(1)}, bf16[256,4096]{1,0:T(8,128)(2,1)S(1)}, bf16[256,1024]{1,0:T(8,128)(2,1)S(1)}, f32[16,128]{1,0:T(8,128)S(1)}) %tuple.30), branch_computations={%region_2.3_spmd, %region_3.4_spmd} | conditional | flops 3147841 | bytes 11700732 | solution.py:212
  41.8 0.1 copy.11
  42.0 0.0 copy-start.3
  42.0 2.0 %block_grads.3 = f32[16,16,16,128]{3,2,1,0:T(8,128)S(1)} custom-call(s32[1]{0:T(128)} %bitcast.2.parity_ref, s32[64]{0:T(128)S(1)} %fusion.code_ref, bf16[256,4096]{1,0:T(8,128)(2,1)S(1)} %get-tuple-element.12.x_ref, bf16[256,1024]{1,0:T(8,128)(2,1)S(1)} %get-tuple-element.13.g_ref), custom_call_target="tpu_custom_call" | custom-call | tf_op jit(solution)/shard_map/cond/branch_1_fun/block_grads/pallas_call | solution.py:42
  44.0 0.3 multiply_convert_fusion
  44.3 1.9 %collective-permute-start = (f16[16,16,16,128]{3,2,1,0:T(8,128)(2,1)S(1)}, f16[16,16,16,128]{3,2,1,0:T(8,128)(2,1)S(1)}, u32[]{:S(2)}, u32[]{:S(2)}) collective-permute-start(f16[16,16,16,128]{3,2,1,0:T(8,128)(2,1)S(1)} %multiply_convert_fusion), channel_id=1, source_target_pairs={{0,8},{8,0},{1,9},{9,1},{2,10},{10,2},{3,11},{11,3},{4,12},{12,4},... | collective-permute-start | bytes 3145736 | tf_op jit(solution)/shard_map/cond/branch_1_fun/ppermute | solution.py:171
  46.2 0.0 copy-done.3
  46.2 2.0 %block_grads.2 = f32[16,16,16,128]{3,2,1,0:T(8,128)S(1)} custom-call(s32[1]{0:T(128)} %bitcast.parity_ref, s32[64]{0:T(128)S(1)} %fusion.code_ref, bf16[256,4096]{1,0:T(8,128)(2,1)S(1)} %get-tuple-element.12.x_ref, bf16[256,1024]{1,0:T(8,128)(2,1)S(1)} %get-tuple-element.13.g_ref), custom_call_target="tpu_custom_call" | custom-call | tf_op jit(solution)/shard_map/cond/branch_1_fun/block_grads/pallas_call | solution.py:42
  48.2 0.0 copy-start.4
  48.2 0.6 collective-permute-done
  48.8 1.3 %add_convert_fusion = f16[16,16,16,128]{3,2,1,0:T(8,128)(2,1)} fusion(f16[16,16,16,128]{3,2,1,0:T(8,128)(2,1)S(1)} %collective-permute-done, f32[16,16,16,128]{3,2,1,0:T(8,128)S(1)} %block_grads.2, f32[16,128]{1,0:T(8,128)S(1)} %multiply_exponential_fusion), kind=kLoop, calls=%fused_computation | loop fusion | flops 2097152 | bytes 4202496 | tf_op jit(solution)/shard_map/cond/branch_1_fun/convert_element_type | solution.py:207
  50.1 0.0 copy-done.4
  50.1 4.2 %all-to-all-done.1.near_ref = bf16[16,144,128]{2,1,0:T(8,128)(2,1)S(1)} async-done(((bf16[16,144,128]{2,1,0:T(8,128)(2,1)}), bf16[16,144,128]{2,1,0:T(8,128)(2,1)S(1)}, u32[]{:S(2)}, u32[]{:S(2)}) %all-to-all-start.1) | async-done | bytes 589856 | tf_op jit(solution)/shard_map/all_to_all | solution.py:199
  54.3 4.4 %all-to-all-start.2 = ((f16[16,16,16,128]{3,2,1,0:T(8,128)(2,1)}), f16[16,16,16,128]{3,2,1,0:T(8,128)(2,1)}, u32[]{:S(2)}, u32[]{:S(2)}) async-start(f16[16,16,16,128]{3,2,1,0:T(8,128)(2,1)} %get-tuple-element.31), calls=%async_computation.2 | async-start | bytes 2097152 | tf_op jit(solution)/shard_map/all_to_all | solution.py:214
  58.7 3.1 %collective-permute-start.2 = (bf16[16,144,128]{2,1,0:T(8,128)(2,1)S(1)}, bf16[16,144,128]{2,1,0:T(8,128)(2,1)S(1)}, u32[]{:S(2)}, u32[]{:S(2)}) collective-permute-start(bf16[16,144,128]{2,1,0:T(8,128)(2,1)S(1)} %all-to-all-done.1.near_ref), channel_id=1, source_target_pairs={{0,16},{16,0},{32,48},{48,32},{64,80},{80,64},{96,112},{112,96},{1... | collective-permute-start | bytes 1769480 | tf_op jit(solution)/shard_map/ppermute | solution.py:171
  61.8 12.7 %collective-permute-done.2.next_ref = bf16[16,144,128]{2,1,0:T(8,128)(2,1)S(1)} collective-permute-done((bf16[16,144,128]{2,1,0:T(8,128)(2,1)S(1)}, bf16[16,144,128]{2,1,0:T(8,128)(2,1)S(1)}, u32[]{:S(2)}, u32[]{:S(2)}) %collective-permute-start.2) | collective-permute-done | bytes 589856 | tf_op jit(solution)/shard_map/ppermute | solution.py:171
  74.6 1.3 %stage.1.near_ref = bf16[64,64,128]{2,1,0:T(8,128)(2,1)S(1)} custom-call(s32[1]{0:T(128)} %bitcast.11.parity_ref, bf16[16,144,128]{2,1,0:T(8,128)(2,1)S(1)} %all-to-all-done.1.near_ref, bf16[16,144,128]{2,1,0:T(8,128)(2,1)S(1)} %collective-permute-done.2.next_ref), custom_call_target="tpu_custom_call" | custom-call | tf_op jit(solution)/shard_map/stage/pallas_call | solution.py:91
  75.9 1.9 %collective-permute-start.3 = (bf16[64,64,128]{2,1,0:T(8,128)(2,1)S(1)}, bf16[64,64,128]{2,1,0:T(8,128)(2,1)S(1)}, u32[]{:S(2)}, u32[]{:S(2)}) collective-permute-start(bf16[64,64,128]{2,1,0:T(8,128)(2,1)S(1)} %stage.1.near_ref), channel_id=1, source_target_pairs={{0,8},{8,0},{1,9},{9,1},{2,10},{10,2},{3,11},{11,3},{4,12},{12,4},... | collective-permute-start | bytes 3145736 | tf_op jit(solution)/shard_map/ppermute | solution.py:171
  77.9 0.0 all-to-all-done.2
  77.9 2.1 %multiply_reduce_fusion = f32[16,16,128]{2,1,0:T(8,128)} fusion(f16[16,16,16,128]{3,2,1,0:T(8,128)(2,1)} %all-to-all-done.2, f32[16,16,128]{2,1,0:T(8,128)S(1)} %multiply_exponential_fusion.1), kind=kLoop, calls=%fused_computation.5 | loop fusion | flops 1540096 | bytes 1310720 | tf_op jit(solution)/shard_map/reduce_sum | solution.py:216
  80.0 7.1 %all-to-all-start.3 = ((f32[16,16,128]{2,1,0:T(8,128)}), f32[16,16,128]{2,1,0:T(8,128)S(1)}, u32[]{:S(2)}, u32[]{:S(2)}) async-start(f32[16,16,128]{2,1,0:T(8,128)} %multiply_reduce_fusion), calls=%async_computation.3 | async-start | bytes 262144 | tf_op jit(solution)/shard_map/all_to_all | solution.py:222
  87.1 0.0 collective-permute-done.3.far_ref
  87.1 7.2 %project.1 = (bf16[256,1024]{1,0:T(8,128)(2,1)}, bf16[256,4096]{1,0:T(8,128)(2,1)}) custom-call(s32[1]{0:T(128)} %bitcast.10.core_ref, s32[64]{0:T(128)S(1)} %get-tuple-element.33.code_ref, bf16[256,4096]{1,0:T(8,128)(2,1)} %x_ref.1, bf16[256,1024]{1,0:T(8,128)(2,1)} %g_ref.1, bf16[64,64,128]{2,1,0:T(8,128)(2,1)S(1)} %stage.1.near_ref, ...), custom_call_target="tpu_custom_call" | custom-call | flops 1 | bytes 1 | tf_op jit(solution)/shard_map/project/pallas_call | solution.py:149
  94.3 7.2 %all-to-all-done.3 = f32[16,16,128]{2,1,0:T(8,128)S(1)} async-done(((f32[16,16,128]{2,1,0:T(8,128)}), f32[16,16,128]{2,1,0:T(8,128)S(1)}, u32[]{:S(2)}, u32[]{:S(2)}) %all-to-all-start.3) | async-done | bytes 131104 | tf_op jit(solution)/shard_map/all_to_all | solution.py:222
  101.6 11.2 %all_to_all.25 = f32[8,16,128]{2,1,0:T(8,128)S(1)} all-to-all(f32[8,16,128]{2,1,0:T(8,128)S(1)} %broadcast_in_dim.13), channel_id=1, replica_groups=mesh['yh'=2,'z'=16,'c'=2,'x'=4,'yl'=2] {'x','yl'}, dimensions={0} | all-to-all | bytes 131072 | tf_op jit(solution)/shard_map/all_to_all | solution.py:175
  112.8 0.6 broadcast_multiply_fusion
  (11 shorter events, 0.1 us)
Async XLA Ops:
  0.6 0.8 copy-start
  0.6 23.1 %copy-start.2 = (bf16[256,1024]{1,0:T(8,128)(2,1)S(1)}, bf16[256,1024]{1,0:T(8,128)(2,1)}, u32[]{:S(2)}) copy-start(bf16[256,1024]{1,0:T(8,128)(2,1)} %g_ref.1) | copy-start | bytes 1572868
  2.7 33.6 %all-to-all-start = ((bf16[64,4,128]{2,1,0:T(4,128)(2,1)}), bf16[64,4,128]{2,1,0:T(4,128)(2,1)S(1)}, u32[]{:S(2)}, u32[]{:S(2)}) async-start(bf16[64,4,128]{2,1,0:T(4,128)(2,1)} %bitcast.9), calls=%async_computation | async-start | bytes 131072 | tf_op jit(solution)/shard_map/all_to_all | solution.py:190
  21.1 20.7 %copy-start.1 = (bf16[256,4096]{1,0:T(8,128)(2,1)S(1)}, bf16[256,4096]{1,0:T(8,128)(2,1)}, u32[]{:S(2)}) copy-start(bf16[256,4096]{1,0:T(8,128)(2,1)} %x_ref.1) | copy-start | bytes 6291460
  25.9 3.1 %collective-permute-start.1 = (f32[16,128]{1,0:T(8,128)S(1)}, f32[16,128]{1,0:T(8,128)S(1)}, u32[]{:S(2)}, u32[]{:S(2)}) collective-permute-start(f32[16,128]{1,0:T(8,128)S(1)} %broadcast_in_dim.12), channel_id=1, source_target_pairs={{0,8},{8,0},{1,9},{9,1},{2,10},{10,2},{3,11},{11,3},{4,12},{12,4},... | collective-permute-start | bytes 24584 | tf_op jit(solution)/shard_map/ppermute | solution.py:171
  37.3 17.1 %all-to-all-start.1 = ((bf16[16,144,128]{2,1,0:T(8,128)(2,1)}), bf16[16,144,128]{2,1,0:T(8,128)(2,1)S(1)}, u32[]{:S(2)}, u32[]{:S(2)}) async-start(bf16[16,144,128]{2,1,0:T(8,128)(2,1)} %share.1), calls=%async_computation.1 | async-start | bytes 1179648 | tf_op jit(solution)/shard_map/all_to_all | solution.py:199
  42.0 4.2 %copy-start.3 = (s32[64]{0:T(128)}, s32[64]{0:T(128)S(1)}, u32[]{:S(2)}) copy-start(s32[64]{0:T(128)S(1)} %fusion.code_ref) | copy-start | bytes 772 | tf_op jit(solution)/shard_map/cond
  44.3 4.6 %collective-permute-start = (f16[16,16,16,128]{3,2,1,0:T(8,128)(2,1)S(1)}, f16[16,16,16,128]{3,2,1,0:T(8,128)(2,1)S(1)}, u32[]{:S(2)}, u32[]{:S(2)}) collective-permute-start(f16[16,16,16,128]{3,2,1,0:T(8,128)(2,1)S(1)} %multiply_convert_fusion), channel_id=1, source_target_pairs={{0,8},{8,0},{1,9},{9,1},{2,10},{10,2},{3,11},{11,3},{4,12},{12,4},... | collective-permute-start | bytes 3145736 | tf_op jit(solution)/shard_map/cond/branch_1_fun/ppermute | solution.py:171
  48.2 2.0 %copy-start.4 = (s32[64]{0:T(128)S(1)}, s32[64]{0:T(128)}, u32[]{:S(2)}) copy-start(s32[64]{0:T(128)} %copy-done.3) | copy-start | bytes 772 | tf_op jit(solution)/shard_map/cond
  54.3 23.5 %all-to-all-start.2 = ((f16[16,16,16,128]{3,2,1,0:T(8,128)(2,1)}), f16[16,16,16,128]{3,2,1,0:T(8,128)(2,1)}, u32[]{:S(2)}, u32[]{:S(2)}) async-start(f16[16,16,16,128]{3,2,1,0:T(8,128)(2,1)} %get-tuple-element.31), calls=%async_computation.2 | async-start | bytes 2097152 | tf_op jit(solution)/shard_map/all_to_all | solution.py:214
  58.7 15.9 %collective-permute-start.2 = (bf16[16,144,128]{2,1,0:T(8,128)(2,1)S(1)}, bf16[16,144,128]{2,1,0:T(8,128)(2,1)S(1)}, u32[]{:S(2)}, u32[]{:S(2)}) collective-permute-start(bf16[16,144,128]{2,1,0:T(8,128)(2,1)S(1)} %all-to-all-done.1.near_ref), channel_id=1, source_target_pairs={{0,16},{16,0},{32,48},{48,32},{64,80},{80,64},{96,112},{112,96},{1... | collective-permute-start | bytes 1769480 | tf_op jit(solution)/shard_map/ppermute | solution.py:171
  75.9 11.2 %collective-permute-start.3 = (bf16[64,64,128]{2,1,0:T(8,128)(2,1)S(1)}, bf16[64,64,128]{2,1,0:T(8,128)(2,1)S(1)}, u32[]{:S(2)}, u32[]{:S(2)}) collective-permute-start(bf16[64,64,128]{2,1,0:T(8,128)(2,1)S(1)} %stage.1.near_ref), channel_id=1, source_target_pairs={{0,8},{8,0},{1,9},{9,1},{2,10},{10,2},{3,11},{11,3},{4,12},{12,4},... | collective-permute-start | bytes 3145736 | tf_op jit(solution)/shard_map/ppermute | solution.py:171
  80.0 21.6 %all-to-all-start.3 = ((f32[16,16,128]{2,1,0:T(8,128)}), f32[16,16,128]{2,1,0:T(8,128)S(1)}, u32[]{:S(2)}, u32[]{:S(2)}) async-start(f32[16,16,128]{2,1,0:T(8,128)} %multiply_reduce_fusion), calls=%async_computation.3 | async-start | bytes 262144 | tf_op jit(solution)/shard_map/all_to_all | solution.py:222

commit v4 on v3

--- a/solution.py
+++ b/solution.py
@@ -36,6 +36,57 @@
             out_ref[yh * 8 : (yh + 1) * 8, z] = grad.reshape(8, 16, B)
 
 
+def packet_kernel(rep_ref, row_ref, column_ref, blocks_ref, out_ref, wide):
+    wide[...] = blocks_ref[0].astype(jnp.float32)
+    code = jnp.full((2, B), row_ref[0] * CB + column_ref[0], jnp.int32).astype(jnp.float32)
+    for yh in range(2):
+        for odd in range(2):
+            for core in range(2):
+                at = core * 32 + odd * 16 + yh * 8 + rep_ref[0]
+                rows = [wide[pl.ds(at, 1), :], wide[pl.ds(64 + at, 1), :], code]
+                piece = jnp.concatenate(rows, axis=0).astype(jnp.bfloat16)
+                for z in range(odd, 16, 2):
+                    out_ref[yh * 32 + z * 2 + core] = piece
+
+
+def make_packet(rep, row, column, blocks):
+    smem = pl.BlockSpec(memory_space=pltpu.SMEM)
+    vmem = pl.BlockSpec(memory_space=pltpu.VMEM)
+    return pl.pallas_call(
+        packet_kernel,
+        out_shape=jax.ShapeDtypeStruct((NNZ, 4, B), jnp.bfloat16),
+        in_specs=[smem, smem, smem, vmem],
+        out_specs=vmem,
+        scratch_shapes=[pltpu.VMEM((B, B), jnp.float32)],
+        compiler_params=vmem_mib(4),
+        name="packet",
+    )(rep, row, column, blocks)
+
+
+def power_kernel(x_ref, g_ref, out_ref):
+    tops = []
+    for ref in (x_ref, g_ref):
+        top = jnp.abs(ref[:16, :])
+        for row in range(16, ref.shape[0], 16):
+            top = jnp.maximum(top, jnp.abs(ref[row : row + 16, :]))
+        tops.append(jnp.max(top.astype(jnp.float32), axis=(0, 1), keepdims=True))
+    bound = x_ref.shape[0] * jnp.maximum(tops[0] * tops[1], 1e-30)
+    power = jnp.floor(jnp.log2(16384.0 / bound))
+    out_ref[...] = jnp.broadcast_to(power, out_ref.shape)
+
+
+def own_power(x, g):
+    vmem = pl.BlockSpec(memory_space=pltpu.VMEM)
+    return pl.pallas_call(
+        power_kernel,
+        out_shape=jax.ShapeDtypeStruct((16, B), jnp.float32),
+        in_specs=[vmem, vmem],
+        out_specs=vmem,
+        compiler_params=vmem_mib(8),
+        name="power",
+    )(x, g)
+
+
 def half_grads(parity, codes, x, g):
     smem = pl.BlockSpec(memory_space=pltpu.SMEM)
     vmem = pl.BlockSpec(memory_space=pltpu.VMEM)
@@ -73,10 +124,11 @@
     )(got, power)
 
 
-def stage_kernel(parity_ref, near_ref, next_ref, w_ref, wide):
-    for slots, at in ((near_ref, parity_ref[0]), (next_ref, 1 - parity_ref[0])):
-        for s in range(16):
-            wide[pl.ds(pl.multiple_of((at * 16 + s) * B, B), B), :] = slots[s, :B].astype(
+def stage_kernel(parity_ref, near_ref, up_ref, down_ref, w_ref, wide):
+    for s in range(16):
+        beside = (up_ref if s < 8 else down_ref).at[s % 8]
+        for slot, at in ((near_ref.at[s], parity_ref[0]), (beside, 1 - parity_ref[0])):
+            wide[pl.ds(pl.multiple_of((at * 16 + s) * B, B), B), :] = slot[:B].astype(
                 jnp.float32
             )
     for n in range(NNZ):
@@ -86,29 +138,24 @@
             ].astype(jnp.bfloat16)
 
 
-def stage(parity, near, next_to):
-    vmem = pl.BlockSpec(memory_space=pltpu.VMEM)
+def stage(parity, near, up, down):
+    vmem = pl.BlockSpec(memory_space=pltpu.VMEM)
+    smem = pl.BlockSpec(memory_space=pltpu.SMEM)
     return pl.pallas_call(
         stage_kernel,
         out_shape=jax.ShapeDtypeStruct((NNZ, B // 2, B), jnp.bfloat16),
-        in_specs=[pl.BlockSpec(memory_space=pltpu.SMEM), vmem, vmem],
+        in_specs=[smem, vmem, vmem, vmem],
         out_specs=vmem,
         scratch_shapes=[pltpu.VMEM((32 * B, B), jnp.float32)],
         compiler_params=vmem_mib(8),
         name="stage",
-    )(parity, near, next_to)
-
-
-def project_kernel(core_ref, code_ref, x_ref, g_ref, near_ref, far_ref, v_ref, d_ref, by_col, by_row, fill, w):
-    for half_ref, core in ((near_ref, core_ref[0]), (far_ref, 1 - core_ref[0])):
-        for i in range(2):
-            at = pl.multiple_of(i * 64 + core * 32, 32)
-            w[:, pl.ds(at, 32), :] = half_ref[:, i * 32 : (i + 1) * 32, :]
-
+    )(parity, near, up, down)
+
+
+def project_kernel(core_ref, code_ref, x_ref, g_ref, near_ref, far_ref, v_out, d_out, by_col, by_row, fill, w, v, d, sems):
     for k in range(CB + RB):
         fill[k] = 0
-
-    def place(n, carry):
+    for n in range(NNZ):
         code = code_ref[n]
         row, col = code // CB, code % CB
         at = fill[col]
@@ -117,10 +164,29 @@
         at = fill[CB + row]
         by_row[row * 2 + at] = n
         fill[CB + row] = at + 1
-        return carry
-
-    lax.fori_loop(0, NNZ, place, 0)
-
+
+    for half_ref, core in ((near_ref, core_ref[0]), (far_ref, 1 - core_ref[0])):
+        for i in range(2):
+            at = pl.multiple_of(i * 64 + core * 32, 32)
+            w[:, pl.ds(at, 32), :] = half_ref[:, i * 32 : (i + 1) * 32, :]
+
+    copies = []
+    for row in range(RB):
+        ns = [by_row[row * 2 + k] for k in range(2)]
+        cols = [code_ref[n] % CB for n in ns]
+        gs = jnp.concatenate(
+            [g_ref[:, pl.ds(pl.multiple_of(c * B, B), B)] for c in cols], axis=1
+        )
+        ws = jnp.concatenate([w[n] for n in ns], axis=1)
+        d[:, row * B : (row + 1) * B] = lax.dot_general(
+            gs, ws, (((1,), (1,)), ((), ())), preferred_element_type=jnp.float32
+        ).astype(d.dtype)
+        if row % 8 == 7:
+            span = pl.ds((row - 7) * B, 8 * B)
+            copies.append(
+                pltpu.make_async_copy(d.at[:, span], d_out.at[:, span], sems.at[row // 8])
+            )
+            copies[-1].start()
     for col in range(CB):
         ns = [by_col[col * 8 + k] for k in range(8)]
         rows = [code_ref[n] // CB for n in ns]
@@ -128,42 +194,43 @@
             [x_ref[:, pl.ds(pl.multiple_of(r * B, B), B)] for r in rows], axis=1
         )
         ws = jnp.concatenate([w[n] for n in ns], axis=0)
-        v_ref[:, col * B : (col + 1) * B] = jnp.dot(
+        v[:, col * B : (col + 1) * B] = jnp.dot(
             xs, ws, preferred_element_type=jnp.float32
-        ).astype(v_ref.dtype)
-    for row in range(RB):
-        ns = [by_row[row * 2 + k] for k in range(2)]
-        cols = [code_ref[n] % CB for n in ns]
-        gs = jnp.concatenate(
-            [g_ref[:, pl.ds(pl.multiple_of(c * B, B), B)] for c in cols], axis=1
-        )
-        ws = jnp.concatenate([w[n] for n in ns], axis=1)
-        d_ref[:, row * B : (row + 1) * B] = lax.dot_general(
-            gs, ws, (((1,), (1,)), ((), ())), preferred_element_type=jnp.float32
-        ).astype(d_ref.dtype)
-
-
-def project(place, codes, x, g, near, far):
-    smem = pl.BlockSpec(memory_space=pltpu.SMEM)
-    vmem = pl.BlockSpec(memory_space=pltpu.VMEM)
+        ).astype(v.dtype)
+        if col % 4 == 3:
+            span = pl.ds((col - 3) * B, 4 * B)
+            copies.append(
+                pltpu.make_async_copy(v.at[:, span], v_out.at[:, span], sems.at[4 + col // 4])
+            )
+            copies[-1].start()
+    for copy in copies:
+        copy.wait()
+
+
+def project(core, codes, x, g, near, far):
+    smem = pl.BlockSpec(memory_space=pltpu.SMEM)
+    vmem = pl.BlockSpec(memory_space=pltpu.VMEM)
+    hbm = pl.BlockSpec(memory_space=pl.ANY)
     return pl.pallas_call(
         project_kernel,
         out_shape=[
             jax.ShapeDtypeStruct(g.shape, jnp.bfloat16),
             jax.ShapeDtypeStruct(x.shape, jnp.bfloat16),
         ],
-        in_specs=[smem, smem, vmem, vmem, vmem, vmem],
-        out_specs=[vmem, vmem],
+        in_specs=[smem] * 2 + [vmem] * 4,
+        out_specs=[hbm, hbm],
         scratch_shapes=[
             pltpu.SMEM((NNZ,), jnp.int32),
             pltpu.SMEM((NNZ,), jnp.int32),
             pltpu.SMEM((CB + RB,), jnp.int32),
             pltpu.VMEM((NNZ, B, B), jnp.bfloat16),
+            pltpu.VMEM(g.shape, jnp.bfloat16),
+            pltpu.VMEM(x.shape, jnp.bfloat16),
+            pltpu.SemaphoreType.DMA((6,)),
         ],
         compiler_params=vmem_mib(20),
-        cost_estimate=pl.CostEstimate(flops=1, transcendentals=0, bytes_accessed=1),
         name="project",
-    )(place, codes, x, g, near, far)
+    )(core, codes, x, g, near, far)
 
 
 def flip(value, axis, by=1):
@@ -179,19 +246,11 @@
 
 def per_device(x, blocks, block_row, block_column, g):
     core = lax.axis_index("c").astype(jnp.int32)
-    rep = lax.axis_index(REP)
-    pieces = blocks.reshape(2, 2, 2, 2, 8, B)
-    mine = lax.dynamic_index_in_dim(pieces, rep, 4, keepdims=False)
-    mine = mine.transpose(3, 2, 1, 0, 4)
-    code = (block_row * CB + block_column).astype(jnp.bfloat16)
-    tail = jnp.broadcast_to(code.reshape(1, 1, 1, 1, 1), (2, 2, 2, 2, B))
-    packet = jnp.concatenate([mine, tail], axis=3)[:, None]
-    packet = jnp.broadcast_to(packet, (2, 8, 2, 2, 4, B)).reshape(NNZ, 4, B)
+    rep = lax.axis_index(REP).astype(jnp.int32).reshape(1)
+    packet = make_packet(rep, block_row, block_column, blocks)
     got = lax.all_to_all(packet, FSDP, 0, 0, tiled=True)
 
-    top = jnp.max(jnp.abs(x)).astype(jnp.float32) * jnp.max(jnp.abs(g)).astype(jnp.float32)
-    power = jnp.floor(jnp.log2(16384.0 / (x.shape[0] * jnp.maximum(top, 1e-30))))
-    power = jnp.broadcast_to(power, (16, B))
+    power = own_power(x, g)
     power = jnp.minimum(power, flip(power, "c"))
     got, power = lax.optimization_barrier((got, power))
 
@@ -216,15 +275,17 @@
     plane_sum = jnp.sum(spread.astype(jnp.float32) * down[:, None], axis=0)
 
     parity = (lax.axis_index("z") % 2).astype(jnp.int32).reshape(1)
-    half = stage(parity, near, flip(near, "z"))
-    values_out, input_grad = project(core.reshape(1), codes, x, g, half, flip(half, "c"))
+    from_below = lax.ppermute(near[:8], "z", [(i, (i + 1) % 16) for i in range(16)])
+    from_above = lax.ppermute(near[8:], "z", [(i, (i - 1) % 16) for i in range(16)])
+    half = stage(parity, near, from_below, from_above)
+    far = flip(half, "c")
+    values_out, input_grad = project(core.reshape(1), codes, x, g, half, far)
 
     ring = lax.all_to_all(plane_sum, "z", 0, 0, tiled=True)
     ring, values_out = lax.optimization_barrier((ring, values_out))
-    strip = jnp.sum(ring, axis=0)
-    whole = to_all(strip, REP, 8)
     loss_scale = (x.shape[0] * lax.axis_size(AXES)) ** (-0.5)
-    weight_grad = whole.reshape(1, B, B) * loss_scale
+    strip = jnp.sum(ring, axis=0) * loss_scale
+    weight_grad = to_all(strip, REP, 8).reshape(1, B, B)
     return values_out, input_grad, weight_grad
 
 

time: 114 us -> 110 us (0.965)
  other arithmetic: 7.7 us -> 3.76 us
  between operations: 3.55 us -> 2.11 us
  Pallas kernels: 13.3 us -> 14.7 us
    ppermute x4 -> x3, waiting for transfers between devices: 14.4 us -> 1.64 us  [flip(): return lax.ppermute(value, axis, [(i, i ^ by) for i in range(size)])]
    ppermute x0 -> x2, waiting for transfers between devices: none -> 5.96 us  [the longest x1 3.72 us: per_device(): lax.ppermute(near[:8], 'z', [(i, (i + 1) % 16) for i in range(16)])]
    ppermute x0 -> x2, starting transfers between devices: none -> 5.84 us  [the longest x1 3.33 us: per_device(): lax.ppermute(near[8:], 'z', [(i, (i - 1) % 16) for i in range(16)])]
    reduce_max x2 -> x0, other arithmetic: 3.3 us -> none  [the longest x1 2.62 us: per_device(): jnp.max(jnp.abs(x)).astype(jnp.float32)]
    ppermute x4 -> x3, starting transfers between devices: 9.05 us -> 5.9 us  [flip(): return lax.ppermute(value, axis, [(i, i ^ by) for i in range(size)])]
    pallas_call x0 -> x2, Pallas kernels: none -> 2.79 us  [the longest x1 2.13 us: own_power(): pl.pallas_call(power_kernel, out_shape=jax.ShapeDtypeStruct((16, B), jnp....]
    all_to_all x1, waiting for transfers between devices: 7.46 us -> 10 us  [per_device(): got = lax.all_to_all(packet, FSDP, 0, 0, tiled=True)]
    all_to_all x1, starting transfers between devices: 7.12 us -> 4.87 us  [per_device(): ring = lax.all_to_all(plane_sum, 'z', 0, 0, tiled=True)]
  transfers between devices with their start and end apart: 8 -> 9, of which waited for: 6 -> 8; matrix products, arithmetic and copies ran while one was open for 6% -> 4% of each run, Pallas kernels for 11% -> 12%
where the time goes in v4:
time: 110 us
  starting transfers between devices  43.9 us (40%)
  waiting for transfers between devices  32.2 us (29%)
  Pallas kernels  14.7 us (13%)
  blocking collectives  11.3 us (10%)
  other arithmetic  3.76 us (3%)
  between operations  2.11 us (2%)
  local copies, waits for them, and re-layouts  1.59 us (1%)
    all_to_all x1, starting transfers between devices, per_device(): got = lax.all_to_all(packet, FSDP, 0, 0, tiled=True)  18.4 us
    all_to_all x1, blocking collectives, to_all(): lax.all_to_all(jnp.broadcast_to(part[None], (count,) + part.shape), axes,...  11.3 us
    all_to_all x1, waiting for transfers between devices, per_device(): got = lax.all_to_all(packet, FSDP, 0, 0, tiled=True)  10 us
    all_to_all x1, waiting for transfers between devices, per_device(): ring = lax.all_to_all(plane_sum, 'z', 0, 0, tiled=True)  8.62 us
    ppermute x3, starting transfers between devices, flip(): return lax.ppermute(value, axis, [(i, i ^ by) for i in range(size)])  5.9 us
    pallas_call x1, Pallas kernels, project(): pl.pallas_call(project_kernel, out_shape=[jax.ShapeDtypeStruct(g.shape, j...  5.84 us
    all_to_all x1, starting transfers between devices, per_device(): ring = lax.all_to_all(plane_sum, 'z', 0, 0, tiled=True)  4.87 us
    all_to_all x1, starting transfers between devices, per_device(): near = lax.all_to_all(share, PLANE, 0, 0, tiled=True)  4.52 us
  transfers between devices with their start and end apart: 9, of which 8 were waited for; matrix products, arithmetic and copies ran while one was open for 4% of the time, Pallas kernels for 12%

profile of v4, /device:TPU:32, one launch (start us, length us, event | category | flops | bytes accessed | tf_op | source)
XLA Modules:
  0.0 109.6 jit_solution(1848316943001565697)
XLA Ops:
  1.9 0.0 copy-start
  1.9 0.7 copy-done
  2.7 0.7 packet.1
  3.3 18.4 %all-to-all-start = ((bf16[64,4,128]{2,1,0:T(4,128)(2,1)}), bf16[64,4,128]{2,1,0:T(4,128)(2,1)S(1)}, u32[]{:S(2)}, u32[]{:S(2)}) async-start(bf16[64,4,128]{2,1,0:T(4,128)(2,1)} %packet.1), calls=%async_computation | async-start | bytes 131072 | tf_op jit(solution)/shard_map/all_to_all | solution.py:251
  21.7 0.0 copy-start.1
  21.8 0.0 copy-start.2
  21.8 2.1 %power.1 = f32[16,128]{1,0:T(8,128)S(1)} custom-call(bf16[256,4096]{1,0:T(8,128)(2,1)} %x_ref.3, bf16[256,1024]{1,0:T(8,128)(2,1)} %g_ref.3), custom_call_target="tpu_custom_call" | custom-call | tf_op jit(solution)/shard_map/power/pallas_call | solution.py:80
  23.9 2.1 %collective-permute-start.1 = (f32[16,128]{1,0:T(8,128)S(1)}, f32[16,128]{1,0:T(8,128)S(1)}, u32[]{:S(2)}, u32[]{:S(2)}) collective-permute-start(f32[16,128]{1,0:T(8,128)S(1)} %power.1), channel_id=1, source_target_pairs={{0,8},{8,0},{1,9},{9,1},{2,10},{10,2},{3,11},{11,3},{4,12},{12,4},... | collective-permute-start | bytes 24584 | tf_op jit(solution)/shard_map/ppermute | solution.py:238
  26.0 1.0 collective-permute-done.1
  27.0 10.0 %all-to-all-done.got_ref = bf16[64,4,128]{2,1,0:T(4,128)(2,1)S(1)} async-done(((bf16[64,4,128]{2,1,0:T(4,128)(2,1)}), bf16[64,4,128]{2,1,0:T(4,128)(2,1)S(1)}, u32[]{:S(2)}, u32[]{:S(2)}) %all-to-all-start) | async-done | bytes 65568 | tf_op jit(solution)/shard_map/all_to_all | solution.py:251
  37.0 0.9 share.1
  37.9 4.5 %all-to-all-start.1 = ((bf16[16,144,128]{2,1,0:T(8,128)(2,1)}), bf16[16,144,128]{2,1,0:T(8,128)(2,1)S(1)}, u32[]{:S(2)}, u32[]{:S(2)}) async-start(bf16[16,144,128]{2,1,0:T(8,128)(2,1)} %share.1), calls=%async_computation.1 | async-start | bytes 1179648 | tf_op jit(solution)/shard_map/all_to_all | solution.py:258
  42.4 0.0 copy-done.1
  42.4 0.0 copy-done.2
  42.4 8.3 %conditional.1 = (f16[16,16,16,128]{3,2,1,0:T(8,128)(2,1)}, s32[64]{0:T(128)S(1)}) conditional(s32[]{:T(128)} %bitcast.4, () %tuple.19, (s32[]{:T(128)}, bf16[64,4,128]{2,1,0:T(4,128)(2,1)S(1)}, bf16[256,4096]{1,0:T(8,128)(2,1)S(1)}, bf16[256,1024]{1,0:T(8,128)(2,1)S(1)}, f32[16,128]{1,0:T(8,128)S(1)}) %tuple.32), branch_computations={%region_0.0_spmd, %region_1.0_spmd} | conditional | flops 3147841 | bytes 11700732 | solution.py:271
  42.4 0.1 copy.8
  42.6 0.0 copy-start.3
  42.6 2.0 %block_grads.3 = f32[16,16,16,128]{3,2,1,0:T(8,128)S(1)} custom-call(s32[1]{0:T(128)} %bitcast.2.parity_ref, s32[64]{0:T(128)S(1)} %fusion.code_ref, bf16[256,4096]{1,0:T(8,128)(2,1)S(1)} %get-tuple-element.12.x_ref, bf16[256,1024]{1,0:T(8,128)(2,1)S(1)} %get-tuple-element.13.g_ref), custom_call_target="tpu_custom_call" | custom-call | tf_op jit(solution)/shard_map/cond/branch_1_fun/block_grads/pallas_call | solution.py:93
  44.6 0.3 multiply_convert_fusion
  44.9 1.9 %collective-permute-start = (f16[16,16,16,128]{3,2,1,0:T(8,128)(2,1)S(1)}, f16[16,16,16,128]{3,2,1,0:T(8,128)(2,1)S(1)}, u32[]{:S(2)}, u32[]{:S(2)}) collective-permute-start(f16[16,16,16,128]{3,2,1,0:T(8,128)(2,1)S(1)} %multiply_convert_fusion), channel_id=1, source_target_pairs={{0,8},{8,0},{1,9},{9,1},{2,10},{10,2},{3,11},{11,3},{4,12},{12,4},... | collective-permute-start | bytes 3145736 | tf_op jit(solution)/shard_map/cond/branch_1_fun/ppermute | solution.py:238
  46.8 0.0 copy-done.3
  46.8 2.0 %block_grads.2 = f32[16,16,16,128]{3,2,1,0:T(8,128)S(1)} custom-call(s32[1]{0:T(128)} %bitcast.parity_ref, s32[64]{0:T(128)S(1)} %fusion.code_ref, bf16[256,4096]{1,0:T(8,128)(2,1)S(1)} %get-tuple-element.12.x_ref, bf16[256,1024]{1,0:T(8,128)(2,1)S(1)} %get-tuple-element.13.g_ref), custom_call_target="tpu_custom_call" | custom-call | tf_op jit(solution)/shard_map/cond/branch_1_fun/block_grads/pallas_call | solution.py:93
  48.8 0.0 copy-start.4
  48.8 0.6 collective-permute-done
  49.4 1.3 %add_convert_fusion = f16[16,16,16,128]{3,2,1,0:T(8,128)(2,1)} fusion(f16[16,16,16,128]{3,2,1,0:T(8,128)(2,1)S(1)} %collective-permute-done, f32[16,16,16,128]{3,2,1,0:T(8,128)S(1)} %block_grads.2, f32[16,128]{1,0:T(8,128)S(1)} %multiply_exponential_fusion), kind=kLoop, calls=%fused_computation | loop fusion | flops 2097152 | bytes 4202496 | tf_op jit(solution)/shard_map/cond/branch_1_fun/convert_element_type | solution.py:266
  50.7 0.0 copy-done.4
  50.7 4.2 %all-to-all-done.1.near_ref = bf16[16,144,128]{2,1,0:T(8,128)(2,1)S(1)} async-done(((bf16[16,144,128]{2,1,0:T(8,128)(2,1)}), bf16[16,144,128]{2,1,0:T(8,128)(2,1)S(1)}, u32[]{:S(2)}, u32[]{:S(2)}) %all-to-all-start.1) | async-done | bytes 589856 | tf_op jit(solution)/shard_map/all_to_all | solution.py:258
  54.9 4.3 %all-to-all-start.2 = ((f16[16,16,16,128]{3,2,1,0:T(8,128)(2,1)}), f16[16,16,16,128]{3,2,1,0:T(8,128)(2,1)}, u32[]{:S(2)}, u32[]{:S(2)}) async-start(f16[16,16,16,128]{3,2,1,0:T(8,128)(2,1)} %get-tuple-element.31), calls=%async_computation.2 | async-start | bytes 2097152 | tf_op jit(solution)/shard_map/all_to_all | solution.py:273
  59.3 2.5 %collective-permute-start.2 = (bf16[8,144,128]{2,1,0:T(8,128)(2,1)S(1)}, bf16[8,144,128]{2,1,0:T(8,128)(2,1)S(1)}, u32[]{:S(2)}, u32[]{:S(2)}) collective-permute-start(bf16[8,144,128]{2,1,0:T(8,128)(2,1)S(1)} %get-tuple-element.44), channel_id=1, source_target_pairs={{0,16},{16,32},{32,48},{48,64},{64,80},{80,96},{96,112},{112,128},... | collective-permute-start | bytes 884744 | tf_op jit(solution)/shard_map/ppermute | solution.py:278
  61.8 3.3 %collective-permute-start.3 = (bf16[8,144,128]{2,1,0:T(8,128)(2,1)S(1)}, bf16[8,144,128]{2,1,0:T(8,128)(2,1)S(1)}, u32[]{:S(2)}, u32[]{:S(2)}) collective-permute-start(bf16[8,144,128]{2,1,0:T(8,128)(2,1)S(1)} %get-tuple-element.43), channel_id=1, source_target_pairs={{0,240},{16,0},{32,16},{48,32},{64,48},{80,64},{96,80},{112,96},{1... | collective-permute-start | bytes 884744 | tf_op jit(solution)/shard_map/ppermute | solution.py:279
  65.2 3.7 %collective-permute-done.2.up_ref = bf16[8,144,128]{2,1,0:T(8,128)(2,1)S(1)} collective-permute-done((bf16[8,144,128]{2,1,0:T(8,128)(2,1)S(1)}, bf16[8,144,128]{2,1,0:T(8,128)(2,1)S(1)}, u32[]{:S(2)}, u32[]{:S(2)}) %collective-permute-start.2) | collective-permute-done | bytes 294944 | tf_op jit(solution)/shard_map/ppermute | solution.py:278
  68.9 2.2 %collective-permute-done.3.down_ref = bf16[8,144,128]{2,1,0:T(8,128)(2,1)S(1)} collective-permute-done((bf16[8,144,128]{2,1,0:T(8,128)(2,1)S(1)}, bf16[8,144,128]{2,1,0:T(8,128)(2,1)S(1)}, u32[]{:S(2)}, u32[]{:S(2)}) %collective-permute-start.3) | collective-permute-done | bytes 294944 | tf_op jit(solution)/shard_map/ppermute | solution.py:279
  71.1 1.3 %stage.1.near_ref = bf16[64,64,128]{2,1,0:T(8,128)(2,1)S(1)} custom-call(s32[1]{0:T(128)} %bitcast.7.parity_ref, bf16[16,144,128]{2,1,0:T(8,128)(2,1)S(1)} %all-to-all-done.1.near_ref, bf16[8,144,128]{2,1,0:T(8,128)(2,1)S(1)} %collective-permute-done.2.up_ref, bf16[8,144,128]{2,1,0:T(8,128)(2,1)S(1)} %collective-permute-done.3.down_ref), custom_call_target="tpu_custom_call" | custom-call | tf_op jit(solution)/shard_map/stage/pallas_call | solution.py:144
  72.4 1.9 %collective-permute-start.4 = (bf16[64,64,128]{2,1,0:T(8,128)(2,1)S(1)}, bf16[64,64,128]{2,1,0:T(8,128)(2,1)S(1)}, u32[]{:S(2)}, u32[]{:S(2)}) collective-permute-start(bf16[64,64,128]{2,1,0:T(8,128)(2,1)S(1)} %stage.1.near_ref), channel_id=1, source_target_pairs={{0,8},{8,0},{1,9},{9,1},{2,10},{10,2},{3,11},{11,3},{4,12},{12,4},... | collective-permute-start | bytes 3145736 | tf_op jit(solution)/shard_map/ppermute | solution.py:238
  74.4 1.8 %all-to-all-done.2 = f16[16,16,16,128]{3,2,1,0:T(8,128)(2,1)} async-done(((f16[16,16,16,128]{3,2,1,0:T(8,128)(2,1)}), f16[16,16,16,128]{3,2,1,0:T(8,128)(2,1)}, u32[]{:S(2)}, u32[]{:S(2)}) %all-to-all-start.2) | async-done | bytes 1048608 | tf_op jit(solution)/shard_map/all_to_all | solution.py:273
  76.2 2.1 %multiply_reduce_fusion = f32[16,16,128]{2,1,0:T(8,128)} fusion(f16[16,16,16,128]{3,2,1,0:T(8,128)(2,1)} %all-to-all-done.2, f32[16,16,128]{2,1,0:T(8,128)S(1)} %multiply_exponential_fusion.1), kind=kLoop, calls=%fused_computation.5 | loop fusion | flops 1540096 | bytes 1310720 | tf_op jit(solution)/shard_map/reduce_sum | solution.py:275
  78.3 4.9 %all-to-all-start.3 = ((f32[16,16,128]{2,1,0:T(8,128)}), f32[16,16,128]{2,1,0:T(8,128)S(1)}, u32[]{:S(2)}, u32[]{:S(2)}) async-start(f32[16,16,128]{2,1,0:T(8,128)} %multiply_reduce_fusion), calls=%async_computation.3 | async-start | bytes 262144 | tf_op jit(solution)/shard_map/all_to_all | solution.py:284
  83.2 0.0 collective-permute-done.4.far_ref
  83.2 5.8 %project.1 = (bf16[256,1024]{1,0:T(8,128)(2,1)}, bf16[256,4096]{1,0:T(8,128)(2,1)}) custom-call(s32[1]{0:T(128)} %bitcast.6.core_ref, s32[64]{0:T(128)S(1)} %get-tuple-element.33.code_ref, bf16[256,4096]{1,0:T(8,128)(2,1)} %x_ref.3, bf16[256,1024]{1,0:T(8,128)(2,1)} %g_ref.3, bf16[64,64,128]{2,1,0:T(8,128)(2,1)S(1)} %stage.1.near_ref, ...), custom_call_target="tpu_custom_call" | custom-call | tf_op jit(solution)/shard_map/project/pallas_call | solution.py:214
  89.0 8.6 %all-to-all-done.3 = f32[16,16,128]{2,1,0:T(8,128)S(1)} async-done(((f32[16,16,128]{2,1,0:T(8,128)}), f32[16,16,128]{2,1,0:T(8,128)S(1)}, u32[]{:S(2)}, u32[]{:S(2)}) %all-to-all-start.3) | async-done | bytes 131104 | tf_op jit(solution)/shard_map/all_to_all | solution.py:284
  97.7 11.3 %all_to_all.25 = f32[8,16,128]{2,1,0:T(8,128)S(1)} all-to-all(f32[8,16,128]{2,1,0:T(8,128)S(1)} %broadcast_in_dim.4), channel_id=1, replica_groups=mesh['yh'=2,'z'=16,'c'=2,'x'=4,'yl'=2] {'x','yl'}, dimensions={0} | all-to-all | bytes 131072 | tf_op jit(solution)/shard_map/all_to_all | solution.py:242
  109.0 0.6 copy.16
  (9 shorter events, 0.1 us)
Async XLA Ops:
  1.9 0.8 copy-start
  3.3 33.6 %all-to-all-start = ((bf16[64,4,128]{2,1,0:T(4,128)(2,1)}), bf16[64,4,128]{2,1,0:T(4,128)(2,1)S(1)}, u32[]{:S(2)}, u32[]{:S(2)}) async-start(bf16[64,4,128]{2,1,0:T(4,128)(2,1)} %packet.1), calls=%async_computation | async-start | bytes 131072 | tf_op jit(solution)/shard_map/all_to_all | solution.py:251
  21.7 20.7 %copy-start.1 = (bf16[256,4096]{1,0:T(8,128)(2,1)S(1)}, bf16[256,4096]{1,0:T(8,128)(2,1)}, u32[]{:S(2)}) copy-start(bf16[256,4096]{1,0:T(8,128)(2,1)} %x_ref.3) | copy-start | bytes 6291460
  21.8 20.7 %copy-start.2 = (bf16[256,1024]{1,0:T(8,128)(2,1)S(1)}, bf16[256,1024]{1,0:T(8,128)(2,1)}, u32[]{:S(2)}) copy-start(bf16[256,1024]{1,0:T(8,128)(2,1)} %g_ref.3) | copy-start | bytes 1572868
  23.9 3.1 %collective-permute-start.1 = (f32[16,128]{1,0:T(8,128)S(1)}, f32[16,128]{1,0:T(8,128)S(1)}, u32[]{:S(2)}, u32[]{:S(2)}) collective-permute-start(f32[16,128]{1,0:T(8,128)S(1)} %power.1), channel_id=1, source_target_pairs={{0,8},{8,0},{1,9},{9,1},{2,10},{10,2},{3,11},{11,3},{4,12},{12,4},... | collective-permute-start | bytes 24584 | tf_op jit(solution)/shard_map/ppermute | solution.py:238
  37.9 17.1 %all-to-all-start.1 = ((bf16[16,144,128]{2,1,0:T(8,128)(2,1)}), bf16[16,144,128]{2,1,0:T(8,128)(2,1)S(1)}, u32[]{:S(2)}, u32[]{:S(2)}) async-start(bf16[16,144,128]{2,1,0:T(8,128)(2,1)} %share.1), calls=%async_computation.1 | async-start | bytes 1179648 | tf_op jit(solution)/shard_map/all_to_all | solution.py:258
  42.6 4.2 %copy-start.3 = (s32[64]{0:T(128)}, s32[64]{0:T(128)S(1)}, u32[]{:S(2)}) copy-start(s32[64]{0:T(128)S(1)} %fusion.code_ref) | copy-start | bytes 772 | tf_op jit(solution)/shard_map/cond
  44.9 4.6 %collective-permute-start = (f16[16,16,16,128]{3,2,1,0:T(8,128)(2,1)S(1)}, f16[16,16,16,128]{3,2,1,0:T(8,128)(2,1)S(1)}, u32[]{:S(2)}, u32[]{:S(2)}) collective-permute-start(f16[16,16,16,128]{3,2,1,0:T(8,128)(2,1)S(1)} %multiply_convert_fusion), channel_id=1, source_target_pairs={{0,8},{8,0},{1,9},{9,1},{2,10},{10,2},{3,11},{11,3},{4,12},{12,4},... | collective-permute-start | bytes 3145736 | tf_op jit(solution)/shard_map/cond/branch_1_fun/ppermute | solution.py:238
  48.8 2.0 %copy-start.4 = (s32[64]{0:T(128)S(1)}, s32[64]{0:T(128)}, u32[]{:S(2)}) copy-start(s32[64]{0:T(128)} %copy-done.3) | copy-start | bytes 772 | tf_op jit(solution)/shard_map/cond
  54.9 21.3 %all-to-all-start.2 = ((f16[16,16,16,128]{3,2,1,0:T(8,128)(2,1)}), f16[16,16,16,128]{3,2,1,0:T(8,128)(2,1)}, u32[]{:S(2)}, u32[]{:S(2)}) async-start(f16[16,16,16,128]{3,2,1,0:T(8,128)(2,1)} %get-tuple-element.31), calls=%async_computation.2 | async-start | bytes 2097152 | tf_op jit(solution)/shard_map/all_to_all | solution.py:273
  59.3 9.6 %collective-permute-start.2 = (bf16[8,144,128]{2,1,0:T(8,128)(2,1)S(1)}, bf16[8,144,128]{2,1,0:T(8,128)(2,1)S(1)}, u32[]{:S(2)}, u32[]{:S(2)}) collective-permute-start(bf16[8,144,128]{2,1,0:T(8,128)(2,1)S(1)} %get-tuple-element.44), channel_id=1, source_target_pairs={{0,16},{16,32},{32,48},{48,64},{64,80},{80,96},{96,112},{112,128},... | collective-permute-start | bytes 884744 | tf_op jit(solution)/shard_map/ppermute | solution.py:278
  61.8 9.3 %collective-permute-start.3 = (bf16[8,144,128]{2,1,0:T(8,128)(2,1)S(1)}, bf16[8,144,128]{2,1,0:T(8,128)(2,1)S(1)}, u32[]{:S(2)}, u32[]{:S(2)}) collective-permute-start(bf16[8,144,128]{2,1,0:T(8,128)(2,1)S(1)} %get-tuple-element.43), channel_id=1, source_target_pairs={{0,240},{16,0},{32,16},{48,32},{64,48},{80,64},{96,80},{112,96},{1... | collective-permute-start | bytes 884744 | tf_op jit(solution)/shard_map/ppermute | solution.py:279
  72.4 10.7 %collective-permute-start.4 = (bf16[64,64,128]{2,1,0:T(8,128)(2,1)S(1)}, bf16[64,64,128]{2,1,0:T(8,128)(2,1)S(1)}, u32[]{:S(2)}, u32[]{:S(2)}) collective-permute-start(bf16[64,64,128]{2,1,0:T(8,128)(2,1)S(1)} %stage.1.near_ref), channel_id=1, source_target_pairs={{0,8},{8,0},{1,9},{9,1},{2,10},{10,2},{3,11},{11,3},{4,12},{12,4},... | collective-permute-start | bytes 3145736 | tf_op jit(solution)/shard_map/ppermute | solution.py:238
  78.3 19.3 %all-to-all-start.3 = ((f32[16,16,128]{2,1,0:T(8,128)}), f32[16,16,128]{2,1,0:T(8,128)S(1)}, u32[]{:S(2)}, u32[]{:S(2)}) async-start(f32[16,16,128]{2,1,0:T(8,128)} %multiply_reduce_fusion), calls=%async_computation.3 | async-start | bytes 262144 | tf_op jit(solution)/shard_map/all_to_all | solution.py:284

commit v5 on v4

--- a/solution.py
+++ b/solution.py
@@ -152,7 +152,7 @@
     )(parity, near, up, down)
 
 
-def project_kernel(core_ref, code_ref, x_ref, g_ref, near_ref, far_ref, v_out, d_out, by_col, by_row, fill, w, v, d, sems):
+def order_kernel(code_ref, by_col, by_row, fill):
     for k in range(CB + RB):
         fill[k] = 0
     for n in range(NNZ):
@@ -165,6 +165,21 @@
         by_row[row * 2 + at] = n
         fill[CB + row] = at + 1
 
+
+def order_blocks(codes):
+    smem = pl.BlockSpec(memory_space=pltpu.SMEM)
+    order = jax.ShapeDtypeStruct((NNZ,), jnp.int32)
+    return pl.pallas_call(
+        order_kernel,
+        out_shape=[order, order],
+        in_specs=[smem],
+        out_specs=[smem, smem],
+        scratch_shapes=[pltpu.SMEM((CB + RB,), jnp.int32)],
+        name="order",
+    )(codes)
+
+
+def project_kernel(core_ref, code_ref, by_col, by_row, x_ref, g_ref, near_ref, far_ref, v_out, d_out, w, v, d, sems):
     for half_ref, core in ((near_ref, core_ref[0]), (far_ref, 1 - core_ref[0])):
         for i in range(2):
             at = pl.multiple_of(i * 64 + core * 32, 32)
@@ -207,7 +222,7 @@
         copy.wait()
 
 
-def project(core, codes, x, g, near, far):
+def project(core, codes, by_col, by_row, x, g, near, far):
     smem = pl.BlockSpec(memory_space=pltpu.SMEM)
     vmem = pl.BlockSpec(memory_space=pltpu.VMEM)
     hbm = pl.BlockSpec(memory_space=pl.ANY)
@@ -217,12 +232,9 @@
             jax.ShapeDtypeStruct(g.shape, jnp.bfloat16),
             jax.ShapeDtypeStruct(x.shape, jnp.bfloat16),
         ],
-        in_specs=[smem] * 2 + [vmem] * 4,
+        in_specs=[smem] * 4 + [vmem] * 4,
         out_specs=[hbm, hbm],
         scratch_shapes=[
-            pltpu.SMEM((NNZ,), jnp.int32),
-            pltpu.SMEM((NNZ,), jnp.int32),
-            pltpu.SMEM((CB + RB,), jnp.int32),
             pltpu.VMEM((NNZ, B, B), jnp.bfloat16),
             pltpu.VMEM(g.shape, jnp.bfloat16),
             pltpu.VMEM(x.shape, jnp.bfloat16),
@@ -230,7 +242,7 @@
         ],
         compiler_params=vmem_mib(20),
         name="project",
-    )(core, codes, x, g, near, far)
+    )(core, codes, by_col, by_row, x, g, near, far)
 
 
 def flip(value, axis, by=1):
@@ -271,21 +283,31 @@
     paired, codes = lax.cond(block_row[0] < RB, grads, nothing, got, power, x, g)
     paired, near = lax.optimization_barrier((paired, near))
     spread = lax.all_to_all(paired, PLANE, 0, 0, tiled=True)
-    down = jnp.exp2(-near[:, B:].astype(jnp.float32))
-    plane_sum = jnp.sum(spread.astype(jnp.float32) * down[:, None], axis=0)
-
     parity = (lax.axis_index("z") % 2).astype(jnp.int32).reshape(1)
     from_below = lax.ppermute(near[:8], "z", [(i, (i + 1) % 16) for i in range(16)])
     from_above = lax.ppermute(near[8:], "z", [(i, (i - 1) % 16) for i in range(16)])
-    half = stage(parity, near, from_below, from_above)
-    far = flip(half, "c")
-    values_out, input_grad = project(core.reshape(1), codes, x, g, half, far)
+    by_col, by_row = order_blocks(codes)
+    spread, from_below, from_above, by_col, by_row = lax.optimization_barrier(
+        (spread, from_below, from_above, by_col, by_row)
+    )
+    down = jnp.exp2(-near[:, B:].astype(jnp.float32))
+    plane_sum = jnp.sum(spread.astype(jnp.float32) * down[:, None], axis=0)
+
+    def halves(near, from_below, from_above):
+        half = stage(parity, near, from_below, from_above)
+        return half, flip(half, "c")
+
+    def no_halves(near, from_below, from_above):
+        half = jnp.zeros((NNZ, B // 2, B), jnp.bfloat16)
+        return half, half
 
     ring = lax.all_to_all(plane_sum, "z", 0, 0, tiled=True)
-    ring, values_out = lax.optimization_barrier((ring, values_out))
+    half, far = lax.cond(block_row[0] < RB, halves, no_halves, near, from_below, from_above)
+    ring, half, far = lax.optimization_barrier((ring, half, far))
     loss_scale = (x.shape[0] * lax.axis_size(AXES)) ** (-0.5)
     strip = jnp.sum(ring, axis=0) * loss_scale
     weight_grad = to_all(strip, REP, 8).reshape(1, B, B)
+    values_out, input_grad = project(core.reshape(1), codes, by_col, by_row, x, g, half, far)
     return values_out, input_grad, weight_grad
 
 

time: 110 us -> 107 us (0.973)
  the two profiles are of different devices: /device:TPU:32 before, /device:TPU:2 now
where the time goes in v5:
time: 107 us
  starting transfers between devices  52.6 us (49%)
  waiting for transfers between devices  27.3 us (26%)
  Pallas kernels  17.8 us (17%)
  other arithmetic  3.77 us (4%)
  local copies, waits for them, and re-layouts  3.03 us (3%)
  between operations  2.09 us (2%)
    all_to_all x1, starting transfers between devices, per_device(): got = lax.all_to_all(packet, FSDP, 0, 0, tiled=True)  18.7 us
    all_to_all x1, waiting for transfers between devices, per_device(): got = lax.all_to_all(packet, FSDP, 0, 0, tiled=True)  10.8 us
    all_to_all x1, starting transfers between devices, per_device(): spread = lax.all_to_all(paired, PLANE, 0, 0, tiled=True)  6.81 us
    all_to_all x1, starting transfers between devices, to_all(): lax.all_to_all(jnp.broadcast_to(part[None], (count,) + part.shape), axes,...  6.03 us
    ppermute x3, starting transfers between devices, flip(): return lax.ppermute(value, axis, [(i, i ^ by) for i in range(size)])  5.79 us
    pallas_call x1, Pallas kernels, project(): pl.pallas_call(project_kernel, out_shape=[jax.ShapeDtypeStruct(g.shape, j...  5.02 us
    all_to_all x1, starting transfers between devices, per_device(): near = lax.all_to_all(share, PLANE, 0, 0, tiled=True)  4.96 us
    all_to_all x1, waiting for transfers between devices, per_device(): ring = lax.all_to_all(plane_sum, 'z', 0, 0, tiled=True)  4.95 us
  transfers between devices with their start and end apart: 10, of which 9 were waited for; matrix products, arithmetic and copies ran while one was open for 2% of the time, Pallas kernels for 15%

profile of v5, /device:TPU:2, one launch (start us, length us, event | category | flops | bytes accessed | tf_op | source)
XLA Modules:
  0.0 106.7 jit_solution(6812982776040390914)
XLA Ops:
  1.9 0.0 copy-start
  1.9 0.7 copy-done
  2.7 0.7 packet.1
  3.3 18.7 %all-to-all-start = ((bf16[64,4,128]{2,1,0:T(4,128)(2,1)}), bf16[64,4,128]{2,1,0:T(4,128)(2,1)S(1)}, u32[]{:S(2)}, u32[]{:S(2)}) async-start(bf16[64,4,128]{2,1,0:T(4,128)(2,1)} %packet.1), calls=%async_computation | async-start | bytes 131072 | tf_op jit(solution)/shard_map/all_to_all | solution.py:263
  22.1 0.0 copy-start.3
  22.1 0.0 copy-start.4
  22.1 2.1 %power.1 = f32[16,128]{1,0:T(8,128)S(1)} custom-call(bf16[256,4096]{1,0:T(8,128)(2,1)} %x_ref.3, bf16[256,1024]{1,0:T(8,128)(2,1)} %g_ref.3), custom_call_target="tpu_custom_call" | custom-call | tf_op jit(solution)/shard_map/power/pallas_call | solution.py:80
  24.2 2.0 %collective-permute-start.2 = (f32[16,128]{1,0:T(8,128)S(1)}, f32[16,128]{1,0:T(8,128)S(1)}, u32[]{:S(2)}, u32[]{:S(2)}) collective-permute-start(f32[16,128]{1,0:T(8,128)S(1)} %power.1), channel_id=1, source_target_pairs={{0,8},{8,0},{1,9},{9,1},{2,10},{10,2},{3,11},{11,3},{4,12},{12,4},... | collective-permute-start | bytes 24584 | tf_op jit(solution)/shard_map/ppermute | solution.py:250
  26.2 1.1 %collective-permute-done.2 = f32[16,128]{1,0:T(8,128)S(1)} collective-permute-done((f32[16,128]{1,0:T(8,128)S(1)}, f32[16,128]{1,0:T(8,128)S(1)}, u32[]{:S(2)}, u32[]{:S(2)}) %collective-permute-start.2) | collective-permute-done | bytes 8224 | tf_op jit(solution)/shard_map/ppermute | solution.py:250
  27.3 10.8 %all-to-all-done.got_ref = bf16[64,4,128]{2,1,0:T(4,128)(2,1)S(1)} async-done(((bf16[64,4,128]{2,1,0:T(4,128)(2,1)}), bf16[64,4,128]{2,1,0:T(4,128)(2,1)S(1)}, u32[]{:S(2)}, u32[]{:S(2)}) %all-to-all-start) | async-done | bytes 65568 | tf_op jit(solution)/shard_map/all_to_all | solution.py:263
  38.1 0.9 share.1
  39.0 5.0 %all-to-all-start.1 = ((bf16[16,144,128]{2,1,0:T(8,128)(2,1)}), bf16[16,144,128]{2,1,0:T(8,128)(2,1)S(1)}, u32[]{:S(2)}, u32[]{:S(2)}) async-start(bf16[16,144,128]{2,1,0:T(8,128)(2,1)} %share.1), calls=%async_computation.1 | async-start | bytes 1179648 | tf_op jit(solution)/shard_map/all_to_all | solution.py:270
  44.0 0.0 copy-done.3
  44.0 0.0 copy-done.4
  44.0 8.3 %conditional.2 = (f16[16,16,16,128]{3,2,1,0:T(8,128)(2,1)}, s32[64]{0:T(128)S(1)}) conditional(s32[]{:T(128)} %bitcast.6, () %tuple.31, (s32[]{:T(128)}, bf16[64,4,128]{2,1,0:T(4,128)(2,1)S(1)}, bf16[256,4096]{1,0:T(8,128)(2,1)S(1)}, bf16[256,1024]{1,0:T(8,128)(2,1)S(1)}, f32[16,128]{1,0:T(8,128)S(1)}) %tuple.49), branch_computations={%region_0.0_spmd, %region_1.0_spmd} | conditional | flops 3147841 | bytes 11700732 | solution.py:283
  44.0 0.1 copy.8
  44.2 0.0 copy-start.5
  44.2 2.0 %block_grads.3 = f32[16,16,16,128]{3,2,1,0:T(8,128)S(1)} custom-call(s32[1]{0:T(128)} %bitcast.2.parity_ref, s32[64]{0:T(128)S(1)} %fusion.code_ref, bf16[256,4096]{1,0:T(8,128)(2,1)S(1)} %get-tuple-element.44.x_ref, bf16[256,1024]{1,0:T(8,128)(2,1)S(1)} %get-tuple-element.45.g_ref), custom_call_target="tpu_custom_call" | custom-call | tf_op jit(solution)/shard_map/cond/branch_1_fun/block_grads/pallas_call | solution.py:93
  46.2 0.3 multiply_convert_fusion
  46.4 1.9 %collective-permute-start.1 = (f16[16,16,16,128]{3,2,1,0:T(8,128)(2,1)S(1)}, f16[16,16,16,128]{3,2,1,0:T(8,128)(2,1)S(1)}, u32[]{:S(2)}, u32[]{:S(2)}) collective-permute-start(f16[16,16,16,128]{3,2,1,0:T(8,128)(2,1)S(1)} %multiply_convert_fusion), channel_id=1, source_target_pairs={{0,8},{8,0},{1,9},{9,1},{2,10},{10,2},{3,11},{11,3},{4,12},{12,4},... | collective-permute-start | bytes 3145736 | tf_op jit(solution)/shard_map/cond/branch_1_fun/ppermute | solution.py:250
  48.4 0.0 copy-done.5
  48.4 2.0 %block_grads.2 = f32[16,16,16,128]{3,2,1,0:T(8,128)S(1)} custom-call(s32[1]{0:T(128)} %bitcast.parity_ref, s32[64]{0:T(128)S(1)} %fusion.code_ref, bf16[256,4096]{1,0:T(8,128)(2,1)S(1)} %get-tuple-element.44.x_ref, bf16[256,1024]{1,0:T(8,128)(2,1)S(1)} %get-tuple-element.45.g_ref), custom_call_target="tpu_custom_call" | custom-call | tf_op jit(solution)/shard_map/cond/branch_1_fun/block_grads/pallas_call | solution.py:93
  50.3 0.0 copy-start.6
  50.3 0.6 collective-permute-done.1
  51.0 1.3 %add_convert_fusion = f16[16,16,16,128]{3,2,1,0:T(8,128)(2,1)} fusion(f16[16,16,16,128]{3,2,1,0:T(8,128)(2,1)S(1)} %collective-permute-done.1, f32[16,16,16,128]{3,2,1,0:T(8,128)S(1)} %block_grads.2, f32[16,128]{1,0:T(8,128)S(1)} %multiply_exponential_fusion), kind=kLoop, calls=%fused_computation | loop fusion | flops 2097152 | bytes 4202496 | tf_op jit(solution)/shard_map/cond/branch_1_fun/convert_element_type | solution.py:278
  52.3 0.0 copy-done.6
  52.3 1.5 %all-to-all-done.1 = bf16[16,144,128]{2,1,0:T(8,128)(2,1)S(1)} async-done(((bf16[16,144,128]{2,1,0:T(8,128)(2,1)}), bf16[16,144,128]{2,1,0:T(8,128)(2,1)S(1)}, u32[]{:S(2)}, u32[]{:S(2)}) %all-to-all-start.1) | async-done | bytes 589856 | tf_op jit(solution)/shard_map/all_to_all | solution.py:270
  53.9 6.8 %all-to-all-start.2 = ((f16[16,16,16,128]{3,2,1,0:T(8,128)(2,1)}), f16[16,16,16,128]{3,2,1,0:T(8,128)(2,1)}, u32[]{:S(2)}, u32[]{:S(2)}) async-start(f16[16,16,16,128]{3,2,1,0:T(8,128)(2,1)} %get-tuple-element.78), calls=%async_computation.2 | async-start | bytes 2097152 | tf_op jit(solution)/shard_map/all_to_all | solution.py:285
  60.7 0.8 fusion.1
  61.5 2.1 %collective-permute-start.4 = (bf16[8,144,128]{2,1,0:T(8,128)(2,1)}, bf16[8,144,128]{2,1,0:T(8,128)(2,1)}, u32[]{:S(2)}, u32[]{:S(2)}) collective-permute-start(bf16[8,144,128]{2,1,0:T(8,128)(2,1)} %get-tuple-element.99), channel_id=1, source_target_pairs={{0,240},{16,0},{32,16},{48,32},{64,48},{80,64},{96,80},{112,96},{1... | collective-permute-start | bytes 884744 | tf_op jit(solution)/shard_map/ppermute | solution.py:288
  63.6 3.7 %collective-permute-start.3 = (bf16[8,144,128]{2,1,0:T(8,128)(2,1)}, bf16[8,144,128]{2,1,0:T(8,128)(2,1)}, u32[]{:S(2)}, u32[]{:S(2)}) collective-permute-start(bf16[8,144,128]{2,1,0:T(8,128)(2,1)} %get-tuple-element.100), channel_id=1, source_target_pairs={{0,16},{16,32},{32,48},{48,64},{64,80},{80,96},{96,112},{112,128},... | collective-permute-start | bytes 884744 | tf_op jit(solution)/shard_map/ppermute | solution.py:287
  67.4 1.8 %order.1 = (s32[64]{0:T(128)}, s32[64]{0:T(128)}) custom-call(s32[64]{0:T(128)S(1)} %get-tuple-element.76.code_ref), custom_call_target="tpu_custom_call" | custom-call | tf_op jit(solution)/shard_map/order/pallas_call | solution.py:172
  69.2 1.9 %collective-permute-done.4 = bf16[8,144,128]{2,1,0:T(8,128)(2,1)} collective-permute-done((bf16[8,144,128]{2,1,0:T(8,128)(2,1)}, bf16[8,144,128]{2,1,0:T(8,128)(2,1)}, u32[]{:S(2)}, u32[]{:S(2)}) %collective-permute-start.4) | collective-permute-done | bytes 294944 | tf_op jit(solution)/shard_map/ppermute | solution.py:288
  71.1 3.1 %collective-permute-done.3 = bf16[8,144,128]{2,1,0:T(8,128)(2,1)} collective-permute-done((bf16[8,144,128]{2,1,0:T(8,128)(2,1)}, bf16[8,144,128]{2,1,0:T(8,128)(2,1)}, u32[]{:S(2)}, u32[]{:S(2)}) %collective-permute-start.3) | collective-permute-done | bytes 294944 | tf_op jit(solution)/shard_map/ppermute | solution.py:287
  74.3 0.3 all-to-all-done.2
  74.5 2.1 %multiply_reduce_fusion = f32[16,16,128]{2,1,0:T(8,128)} fusion(f16[16,16,16,128]{3,2,1,0:T(8,128)(2,1)} %all-to-all-done.2, f32[16,16,128]{2,1,0:T(8,128)S(1)} %multiply_exponential_fusion.1), kind=kLoop, calls=%fused_computation.5 | loop fusion | flops 1540096 | bytes 1310720 | tf_op jit(solution)/shard_map/reduce_sum | solution.py:294
  76.6 4.4 %all-to-all-start.3 = ((f32[16,16,128]{2,1,0:T(8,128)}), f32[16,16,128]{2,1,0:T(8,128)S(1)}, u32[]{:S(2)}, u32[]{:S(2)}) async-start(f32[16,16,128]{2,1,0:T(8,128)} %multiply_reduce_fusion), calls=%async_computation.3 | async-start | bytes 262144 | tf_op jit(solution)/shard_map/all_to_all | solution.py:304
  81.1 0.0 copy-start.1
  81.1 8.3 %conditional.3 = (bf16[64,64,128]{2,1,0:T(8,128)(2,1)}, bf16[64,64,128]{2,1,0:T(8,128)(2,1)}) conditional(s32[]{:T(128)} %bitcast.6, () %tuple.36, (s32[]{:T(128)}, bf16[16,144,128]{2,1,0:T(8,128)(2,1)S(1)}, bf16[8,144,128]{2,1,0:T(8,128)(2,1)}, bf16[8,144,128]{2,1,0:T(8,128)(2,1)}) %tuple.37), branch_computations={%region_3.4_spmd, %region_4.5_spmd} | conditional | flops 11 | bytes 4194469 | solution.py:305
  81.1 3.3 %stage.1 = bf16[64,64,128]{2,1,0:T(8,128)(2,1)} custom-call(s32[1]{0:T(128)} %bitcast.4.parity_ref, bf16[16,144,128]{2,1,0:T(8,128)(2,1)S(1)} %get-tuple-element.48.near_ref, bf16[8,144,128]{2,1,0:T(8,128)(2,1)} %get-tuple-element.49.up_ref, bf16[8,144,128]{2,1,0:T(8,128)(2,1)} %get-tuple-element.50.down_ref), custom_call_target="tpu_custom_call" | custom-call | tf_op jit(solution)/shard_map/cond/branch_1_fun/stage/pallas_call | solution.py:144
  84.5 1.9 %collective-permute-start = (bf16[64,64,128]{2,1,0:T(8,128)(2,1)}, bf16[64,64,128]{2,1,0:T(8,128)(2,1)}, u32[]{:S(2)}, u32[]{:S(2)}) collective-permute-start(bf16[64,64,128]{2,1,0:T(8,128)(2,1)} %stage.1), channel_id=1, source_target_pairs={{0,8},{8,0},{1,9},{9,1},{2,10},{10,2},{3,11},{11,3},{4,12},{12,4},... | collective-permute-start | bytes 3145736 | tf_op jit(solution)/shard_map/cond/branch_1_fun/ppermute | solution.py:250
  86.4 3.0 %collective-permute-done = bf16[64,64,128]{2,1,0:T(8,128)(2,1)} collective-permute-done((bf16[64,64,128]{2,1,0:T(8,128)(2,1)}, bf16[64,64,128]{2,1,0:T(8,128)(2,1)}, u32[]{:S(2)}, u32[]{:S(2)}) %collective-permute-start) | collective-permute-done | bytes 1048608 | tf_op jit(solution)/shard_map/cond/branch_1_fun/ppermute | solution.py:250
  89.4 4.9 %all-to-all-done.3 = f32[16,16,128]{2,1,0:T(8,128)S(1)} async-done(((f32[16,16,128]{2,1,0:T(8,128)}), f32[16,16,128]{2,1,0:T(8,128)S(1)}, u32[]{:S(2)}, u32[]{:S(2)}) %all-to-all-start.3) | async-done | bytes 131104 | tf_op jit(solution)/shard_map/all_to_all | solution.py:304
  94.3 0.6 broadcast_in_dim.4
  95.0 6.0 %all-to-all-start.4 = ((f32[8,16,128]{2,1,0:T(8,128)}), f32[8,16,128]{2,1,0:T(8,128)S(1)}, u32[]{:S(2)}, u32[]{:S(2)}) async-start(f32[8,16,128]{2,1,0:T(8,128)} %broadcast_in_dim.4), calls=%async_computation.4 | async-start | bytes 131072 | tf_op jit(solution)/shard_map/all_to_all | solution.py:254
  101.0 5.0 %project.1 = (bf16[256,1024]{1,0:T(8,128)(2,1)}, bf16[256,4096]{1,0:T(8,128)(2,1)}) custom-call(s32[1]{0:T(128)} %bitcast.5.core_ref, s32[64]{0:T(128)S(1)} %get-tuple-element.76.code_ref, s32[64]{0:T(128)S(1)} %copy-done.1, s32[64]{0:T(128)S(1)} %copy-done.2, bf16[256,4096]{1,0:T(8,128)(2,1)S(1)} %copy-done.3, bf16[256,1024]{1,0:T(8,128)(2,1)S(1)} %copy-done.4, ...), custom_call_target="tpu_custom_call" | custom-call | tf_op jit(solution)/shard_map/project/pallas_call | solution.py:229
  106.0 0.0 all-to-all-done.4
  106.1 0.6 copy.20
  (10 shorter events, 0.1 us)
Async XLA Ops:
  1.9 0.8 copy-start
  3.3 34.8 %all-to-all-start = ((bf16[64,4,128]{2,1,0:T(4,128)(2,1)}), bf16[64,4,128]{2,1,0:T(4,128)(2,1)S(1)}, u32[]{:S(2)}, u32[]{:S(2)}) async-start(bf16[64,4,128]{2,1,0:T(4,128)(2,1)} %packet.1), calls=%async_computation | async-start | bytes 131072 | tf_op jit(solution)/shard_map/all_to_all | solution.py:263
  22.1 21.9 %copy-start.3 = (bf16[256,4096]{1,0:T(8,128)(2,1)S(1)}, bf16[256,4096]{1,0:T(8,128)(2,1)}, u32[]{:S(2)}) copy-start(bf16[256,4096]{1,0:T(8,128)(2,1)} %x_ref.3) | copy-start | bytes 6291460
  22.1 21.9 %copy-start.4 = (bf16[256,1024]{1,0:T(8,128)(2,1)S(1)}, bf16[256,1024]{1,0:T(8,128)(2,1)}, u32[]{:S(2)}) copy-start(bf16[256,1024]{1,0:T(8,128)(2,1)} %g_ref.3) | copy-start | bytes 1572868
  24.2 3.1 %collective-permute-start.2 = (f32[16,128]{1,0:T(8,128)S(1)}, f32[16,128]{1,0:T(8,128)S(1)}, u32[]{:S(2)}, u32[]{:S(2)}) collective-permute-start(f32[16,128]{1,0:T(8,128)S(1)} %power.1), channel_id=1, source_target_pairs={{0,8},{8,0},{1,9},{9,1},{2,10},{10,2},{3,11},{11,3},{4,12},{12,4},... | collective-permute-start | bytes 24584 | tf_op jit(solution)/shard_map/ppermute | solution.py:250
  39.0 14.9 %all-to-all-start.1 = ((bf16[16,144,128]{2,1,0:T(8,128)(2,1)}), bf16[16,144,128]{2,1,0:T(8,128)(2,1)S(1)}, u32[]{:S(2)}, u32[]{:S(2)}) async-start(bf16[16,144,128]{2,1,0:T(8,128)(2,1)} %share.1), calls=%async_computation.1 | async-start | bytes 1179648 | tf_op jit(solution)/shard_map/all_to_all | solution.py:270
  44.2 4.2 %copy-start.5 = (s32[64]{0:T(128)}, s32[64]{0:T(128)S(1)}, u32[]{:S(2)}) copy-start(s32[64]{0:T(128)S(1)} %fusion.code_ref) | copy-start | bytes 772 | tf_op jit(solution)/shard_map/cond
  46.4 4.6 %collective-permute-start.1 = (f16[16,16,16,128]{3,2,1,0:T(8,128)(2,1)S(1)}, f16[16,16,16,128]{3,2,1,0:T(8,128)(2,1)S(1)}, u32[]{:S(2)}, u32[]{:S(2)}) collective-permute-start(f16[16,16,16,128]{3,2,1,0:T(8,128)(2,1)S(1)} %multiply_convert_fusion), channel_id=1, source_target_pairs={{0,8},{8,0},{1,9},{9,1},{2,10},{10,2},{3,11},{11,3},{4,12},{12,4},... | collective-permute-start | bytes 3145736 | tf_op jit(solution)/shard_map/cond/branch_1_fun/ppermute | solution.py:250
  50.3 2.0 %copy-start.6 = (s32[64]{0:T(128)S(1)}, s32[64]{0:T(128)}, u32[]{:S(2)}) copy-start(s32[64]{0:T(128)} %copy-done.5) | copy-start | bytes 772 | tf_op jit(solution)/shard_map/cond
  53.9 20.7 %all-to-all-start.2 = ((f16[16,16,16,128]{3,2,1,0:T(8,128)(2,1)}), f16[16,16,16,128]{3,2,1,0:T(8,128)(2,1)}, u32[]{:S(2)}, u32[]{:S(2)}) async-start(f16[16,16,16,128]{3,2,1,0:T(8,128)(2,1)} %get-tuple-element.78), calls=%async_computation.2 | async-start | bytes 2097152 | tf_op jit(solution)/shard_map/all_to_all | solution.py:285
  61.5 9.6 %collective-permute-start.4 = (bf16[8,144,128]{2,1,0:T(8,128)(2,1)}, bf16[8,144,128]{2,1,0:T(8,128)(2,1)}, u32[]{:S(2)}, u32[]{:S(2)}) collective-permute-start(bf16[8,144,128]{2,1,0:T(8,128)(2,1)} %get-tuple-element.99), channel_id=1, source_target_pairs={{0,240},{16,0},{32,16},{48,32},{64,48},{80,64},{96,80},{112,96},{1... | collective-permute-start | bytes 884744 | tf_op jit(solution)/shard_map/ppermute | solution.py:288
  63.6 10.6 %collective-permute-start.3 = (bf16[8,144,128]{2,1,0:T(8,128)(2,1)}, bf16[8,144,128]{2,1,0:T(8,128)(2,1)}, u32[]{:S(2)}, u32[]{:S(2)}) collective-permute-start(bf16[8,144,128]{2,1,0:T(8,128)(2,1)} %get-tuple-element.100), channel_id=1, source_target_pairs={{0,16},{16,32},{32,48},{48,64},{64,80},{80,96},{96,112},{112,128},... | collective-permute-start | bytes 884744 | tf_op jit(solution)/shard_map/ppermute | solution.py:287
  76.6 17.7 %all-to-all-start.3 = ((f32[16,16,128]{2,1,0:T(8,128)}), f32[16,16,128]{2,1,0:T(8,128)S(1)}, u32[]{:S(2)}, u32[]{:S(2)}) async-start(f32[16,16,128]{2,1,0:T(8,128)} %multiply_reduce_fusion), calls=%async_computation.3 | async-start | bytes 262144 | tf_op jit(solution)/shard_map/all_to_all | solution.py:304
  81.1 19.9 %copy-start.1 = (s32[64]{0:T(128)S(1)}, s32[64]{0:T(128)}, u32[]{:S(2)}) copy-start(s32[64]{0:T(128)} %get-tuple-element.82.by_col) | copy-start | bytes 772
  81.1 19.9 %copy-start.2 = (s32[64]{0:T(128)S(1)}, s32[64]{0:T(128)}, u32[]{:S(2)}) copy-start(s32[64]{0:T(128)} %get-tuple-element.83.by_row) | copy-start | bytes 772
  84.5 4.9 %collective-permute-start = (bf16[64,64,128]{2,1,0:T(8,128)(2,1)}, bf16[64,64,128]{2,1,0:T(8,128)(2,1)}, u32[]{:S(2)}, u32[]{:S(2)}) collective-permute-start(bf16[64,64,128]{2,1,0:T(8,128)(2,1)} %stage.1), channel_id=1, source_target_pairs={{0,8},{8,0},{1,9},{9,1},{2,10},{10,2},{3,11},{11,3},{4,12},{12,4},... | collective-permute-start | bytes 3145736 | tf_op jit(solution)/shard_map/cond/branch_1_fun/ppermute | solution.py:250
  95.0 11.1 %all-to-all-start.4 = ((f32[8,16,128]{2,1,0:T(8,128)}), f32[8,16,128]{2,1,0:T(8,128)S(1)}, u32[]{:S(2)}, u32[]{:S(2)}) async-start(f32[8,16,128]{2,1,0:T(8,128)} %broadcast_in_dim.4), calls=%async_computation.4 | async-start | bytes 131072 | tf_op jit(solution)/shard_map/all_to_all | solution.py:254

commit v6 on v5

--- a/solution.py
+++ b/solution.py
@@ -124,35 +124,58 @@
     )(got, power)
 
 
-def stage_kernel(parity_ref, near_ref, up_ref, down_ref, w_ref, wide):
-    for s in range(16):
-        beside = (up_ref if s < 8 else down_ref).at[s % 8]
-        for slot, at in ((near_ref.at[s], parity_ref[0]), (beside, 1 - parity_ref[0])):
-            wide[pl.ds(pl.multiple_of((at * 16 + s) * B, B), B), :] = slot[:B].astype(
+def stage_kernel(parity_ref, near_hbm, up_hbm, down_hbm, w_hbm, near, beside, wide, w, sems):
+    loads = [
+        pltpu.make_async_copy(near_hbm.at[:, :B], near, sems.at[0]),
+        pltpu.make_async_copy(up_hbm.at[:, :B], beside.at[:8], sems.at[1]),
+        pltpu.make_async_copy(down_hbm.at[:, :B], beside.at[8:], sems.at[2]),
+    ]
+    for load in loads:
+        load.start()
+    loads[0].wait()
+    for slots, at in ((near, parity_ref[0]), (beside, 1 - parity_ref[0])):
+        for s in range(16):
+            if slots is beside and s % 8 == 0:
+                loads[1 + s // 8].wait()
+            wide[pl.ds(pl.multiple_of((at * 16 + s) * B, B), B), :] = slots[s].astype(
                 jnp.float32
             )
+    stores = []
     for n in range(NNZ):
         for i in range(2):
-            w_ref[n, i * 32 : (i + 1) * 32, :] = wide[
+            w[n, i * 32 : (i + 1) * 32, :] = wide[
                 pl.ds(i * NNZ + n, 32, stride=B), :
             ].astype(jnp.bfloat16)
+        if n % 16 == 15:
+            span = pl.ds(n - 15, 16)
+            stores.append(pltpu.make_async_copy(w.at[span], w_hbm.at[span], sems.at[3 + n // 16]))
+            stores[-1].start()
+    for store in stores:
+        store.wait()
 
 
 def stage(parity, near, up, down):
-    vmem = pl.BlockSpec(memory_space=pltpu.VMEM)
-    smem = pl.BlockSpec(memory_space=pltpu.SMEM)
+    hbm = pl.BlockSpec(memory_space=pl.ANY)
     return pl.pallas_call(
         stage_kernel,
         out_shape=jax.ShapeDtypeStruct((NNZ, B // 2, B), jnp.bfloat16),
-        in_specs=[smem, vmem, vmem, vmem],
-        out_specs=vmem,
-        scratch_shapes=[pltpu.VMEM((32 * B, B), jnp.float32)],
-        compiler_params=vmem_mib(8),
+        in_specs=[pl.BlockSpec(memory_space=pltpu.SMEM), hbm, hbm, hbm],
+        out_specs=hbm,
+        scratch_shapes=[
+            pltpu.VMEM((16, B, B), jnp.bfloat16),
+            pltpu.VMEM((16, B, B), jnp.bfloat16),
+            pltpu.VMEM((32 * B, B), jnp.float32),
+            pltpu.VMEM((NNZ, B // 2, B), jnp.bfloat16),
+            pltpu.SemaphoreType.DMA((7,)),
+        ],
+        compiler_params=vmem_mib(10),
         name="stage",
     )(parity, near, up, down)
 
 
-def order_kernel(code_ref, by_col, by_row, fill):
+def order_kernel(code_ref, near_hbm, by_col, by_row, down_ref, lift_ref, fill, powers, sem):
+    load = pltpu.make_async_copy(near_hbm.at[:, B:], powers, sem)
+    load.start()
     for k in range(CB + RB):
         fill[k] = 0
     for n in range(NNZ):
@@ -164,19 +187,33 @@
         at = fill[CB + row]
         by_row[row * 2 + at] = n
         fill[CB + row] = at + 1
-
-
-def order_blocks(codes):
+    load.wait()
+    lift = jnp.min(powers[...].astype(jnp.float32), axis=0) - 4.0
+    down_ref[...] = jnp.exp2(lift[None] - powers[...].astype(jnp.float32))
+    lift_ref[...] = lift
+
+
+def order_blocks(codes, near):
     smem = pl.BlockSpec(memory_space=pltpu.SMEM)
     order = jax.ShapeDtypeStruct((NNZ,), jnp.int32)
     return pl.pallas_call(
         order_kernel,
-        out_shape=[order, order],
-        in_specs=[smem],
-        out_specs=[smem, smem],
-        scratch_shapes=[pltpu.SMEM((CB + RB,), jnp.int32)],
+        out_shape=[
+            order,
+            order,
+            jax.ShapeDtypeStruct((16, 16, B), jnp.float32),
+            jax.ShapeDtypeStruct((16, B), jnp.float32),
+        ],
+        in_specs=[smem, pl.BlockSpec(memory_space=pl.ANY)],
+        out_specs=[smem, smem] + [pl.BlockSpec(memory_space=pltpu.VMEM)] * 2,
+        scratch_shapes=[
+            pltpu.SMEM((CB + RB,), jnp.int32),
+            pltpu.VMEM((16, 16, B), jnp.bfloat16),
+            pltpu.SemaphoreType.DMA,
+        ],
+        compiler_params=vmem_mib(4),
         name="order",
-    )(codes)
+    )(codes, near)
 
 
 def project_kernel(core_ref, code_ref, by_col, by_row, x_ref, g_ref, near_ref, far_ref, v_out, d_out, w, v, d, sems):
@@ -286,12 +323,13 @@
     parity = (lax.axis_index("z") % 2).astype(jnp.int32).reshape(1)
     from_below = lax.ppermute(near[:8], "z", [(i, (i + 1) % 16) for i in range(16)])
     from_above = lax.ppermute(near[8:], "z", [(i, (i - 1) % 16) for i in range(16)])
-    by_col, by_row = order_blocks(codes)
-    spread, from_below, from_above, by_col, by_row = lax.optimization_barrier(
-        (spread, from_below, from_above, by_col, by_row)
+    by_col, by_row, down, lift = order_blocks(codes, near)
+    spread, from_below, from_above, by_col, by_row, down, lift = lax.optimization_barrier(
+        (spread, from_below, from_above, by_col, by_row, down, lift)
     )
-    down = jnp.exp2(-near[:, B:].astype(jnp.float32))
     plane_sum = jnp.sum(spread.astype(jnp.float32) * down[:, None], axis=0)
+    tail = jnp.broadcast_to(lift[None, :8], (16, 8, B))
+    plane_sum = jnp.concatenate([plane_sum, tail], axis=1).astype(jnp.float16)
 
     def halves(near, from_below, from_above):
         half = stage(parity, near, from_below, from_above)
@@ -305,7 +343,8 @@
     half, far = lax.cond(block_row[0] < RB, halves, no_halves, near, from_below, from_above)
     ring, half, far = lax.optimization_barrier((ring, half, far))
     loss_scale = (x.shape[0] * lax.axis_size(AXES)) ** (-0.5)
-    strip = jnp.sum(ring, axis=0) * loss_scale
+    ring = ring.astype(jnp.float32)
+    strip = jnp.sum(ring[:, :16] * jnp.exp2(-ring[:, 16:17]), axis=0) * loss_scale
     weight_grad = to_all(strip, REP, 8).reshape(1, B, B)
     values_out, input_grad = project(core.reshape(1), codes, by_col, by_row, x, g, half, far)
     return values_out, input_grad, weight_grad

time: 107 us -> 107 us (level)
  no operation moved by 1% of the time
where the time goes in v6:
time: 107 us; the launch traced here: 106 us
  starting transfers between devices  52.3 us (49%)
  waiting for transfers between devices  28.1 us (26%)
  Pallas kernels  17.5 us (16%)
  other arithmetic  3.81 us (4%)
  local copies, waits for them, and re-layouts  2.22 us (2%)
  between operations  2.09 us (2%)
    all_to_all x1, starting transfers between devices, per_device(): got = lax.all_to_all(packet, FSDP, 0, 0, tiled=True)  18.7 us
    all_to_all x1, waiting for transfers between devices, per_device(): got = lax.all_to_all(packet, FSDP, 0, 0, tiled=True)  10.8 us
    all_to_all x1, starting transfers between devices, per_device(): spread = lax.all_to_all(paired, PLANE, 0, 0, tiled=True)  6.81 us
    all_to_all x1, starting transfers between devices, to_all(): lax.all_to_all(jnp.broadcast_to(part[None], (count,) + part.shape), axes,...  6.67 us
    ppermute x3, starting transfers between devices, flip(): return lax.ppermute(value, axis, [(i, i ^ by) for i in range(size)])  5.81 us
    pallas_call x1, Pallas kernels, project(): pl.pallas_call(project_kernel, out_shape=[jax.ShapeDtypeStruct(g.shape, j...  5.02 us
    all_to_all x1, starting transfers between devices, per_device(): near = lax.all_to_all(share, PLANE, 0, 0, tiled=True)  4.96 us
    all_to_all x1, waiting for transfers between devices, per_device(): ring = lax.all_to_all(plane_sum, 'z', 0, 0, tiled=True)  4.94 us
  transfers between devices with their start and end apart: 10, of which 9 were waited for; matrix products, arithmetic and copies ran while one was open for 2% of the time, Pallas kernels for 15%

profile of v6, /device:TPU:2, one launch (start us, length us, event | category | flops | bytes accessed | tf_op | source)
XLA Modules:
  0.0 106.2 jit_solution(1821973271498774824)
XLA Ops:
  1.9 0.0 copy-start
  1.9 0.7 copy-done
  2.7 0.7 packet.1
  3.3 18.7 %all-to-all-start = ((bf16[64,4,128]{2,1,0:T(4,128)(2,1)}), bf16[64,4,128]{2,1,0:T(4,128)(2,1)S(1)}, u32[]{:S(2)}, u32[]{:S(2)}) async-start(bf16[64,4,128]{2,1,0:T(4,128)(2,1)} %packet.1), calls=%async_computation | async-start | bytes 131072 | tf_op jit(solution)/shard_map/all_to_all | solution.py:300
  22.1 0.0 copy-start.1
  22.1 0.0 copy-start.2
  22.1 2.1 %power.1 = f32[16,128]{1,0:T(8,128)S(1)} custom-call(bf16[256,4096]{1,0:T(8,128)(2,1)} %x_ref.3, bf16[256,1024]{1,0:T(8,128)(2,1)} %g_ref.3), custom_call_target="tpu_custom_call" | custom-call | tf_op jit(solution)/shard_map/power/pallas_call | solution.py:80
  24.2 2.0 %collective-permute-start.2 = (f32[16,128]{1,0:T(8,128)S(1)}, f32[16,128]{1,0:T(8,128)S(1)}, u32[]{:S(2)}, u32[]{:S(2)}) collective-permute-start(f32[16,128]{1,0:T(8,128)S(1)} %power.1), channel_id=1, source_target_pairs={{0,8},{8,0},{1,9},{9,1},{2,10},{10,2},{3,11},{11,3},{4,12},{12,4},... | collective-permute-start | bytes 24584 | tf_op jit(solution)/shard_map/ppermute | solution.py:287
  26.2 1.1 %collective-permute-done.2 = f32[16,128]{1,0:T(8,128)S(1)} collective-permute-done((f32[16,128]{1,0:T(8,128)S(1)}, f32[16,128]{1,0:T(8,128)S(1)}, u32[]{:S(2)}, u32[]{:S(2)}) %collective-permute-start.2) | collective-permute-done | bytes 8224 | tf_op jit(solution)/shard_map/ppermute | solution.py:287
  27.3 10.8 %all-to-all-done.got_ref = bf16[64,4,128]{2,1,0:T(4,128)(2,1)S(1)} async-done(((bf16[64,4,128]{2,1,0:T(4,128)(2,1)}), bf16[64,4,128]{2,1,0:T(4,128)(2,1)S(1)}, u32[]{:S(2)}, u32[]{:S(2)}) %all-to-all-start) | async-done | bytes 65568 | tf_op jit(solution)/shard_map/all_to_all | solution.py:300
  38.1 0.9 share.1
  39.0 5.0 %all-to-all-start.1 = ((bf16[16,144,128]{2,1,0:T(8,128)(2,1)}), bf16[16,144,128]{2,1,0:T(8,128)(2,1)S(1)}, u32[]{:S(2)}, u32[]{:S(2)}) async-start(bf16[16,144,128]{2,1,0:T(8,128)(2,1)} %share.1), calls=%async_computation.1 | async-start | bytes 1179648 | tf_op jit(solution)/shard_map/all_to_all | solution.py:307
  44.0 0.0 copy-done.1
  44.0 0.0 copy-done.2
  44.0 8.3 %conditional.2 = (f16[16,16,16,128]{3,2,1,0:T(8,128)(2,1)}, s32[64]{0:T(128)S(1)}) conditional(s32[]{:T(128)} %bitcast.6, () %tuple.31, (s32[]{:T(128)}, bf16[64,4,128]{2,1,0:T(4,128)(2,1)S(1)}, bf16[256,4096]{1,0:T(8,128)(2,1)S(1)}, bf16[256,1024]{1,0:T(8,128)(2,1)S(1)}, f32[16,128]{1,0:T(8,128)S(1)}) %tuple.50), branch_computations={%region_0.0_spmd, %region_1.0_spmd} | conditional | flops 3147841 | bytes 11700732 | solution.py:320
  44.0 0.1 copy.9
  44.2 0.0 copy-start.3
  44.2 2.0 %block_grads.3 = f32[16,16,16,128]{3,2,1,0:T(8,128)S(1)} custom-call(s32[1]{0:T(128)} %bitcast.2.parity_ref, s32[64]{0:T(128)S(1)} %fusion.code_ref, bf16[256,4096]{1,0:T(8,128)(2,1)S(1)} %get-tuple-element.44.x_ref, bf16[256,1024]{1,0:T(8,128)(2,1)S(1)} %get-tuple-element.45.g_ref), custom_call_target="tpu_custom_call" | custom-call | tf_op jit(solution)/shard_map/cond/branch_1_fun/block_grads/pallas_call | solution.py:93
  46.1 0.3 multiply_convert_fusion
  46.4 1.9 %collective-permute-start.1 = (f16[16,16,16,128]{3,2,1,0:T(8,128)(2,1)S(1)}, f16[16,16,16,128]{3,2,1,0:T(8,128)(2,1)S(1)}, u32[]{:S(2)}, u32[]{:S(2)}) collective-permute-start(f16[16,16,16,128]{3,2,1,0:T(8,128)(2,1)S(1)} %multiply_convert_fusion), channel_id=1, source_target_pairs={{0,8},{8,0},{1,9},{9,1},{2,10},{10,2},{3,11},{11,3},{4,12},{12,4},... | collective-permute-start | bytes 3145736 | tf_op jit(solution)/shard_map/cond/branch_1_fun/ppermute | solution.py:287
  48.3 0.0 copy-done.3
  48.4 2.0 %block_grads.2 = f32[16,16,16,128]{3,2,1,0:T(8,128)S(1)} custom-call(s32[1]{0:T(128)} %bitcast.parity_ref, s32[64]{0:T(128)S(1)} %fusion.code_ref, bf16[256,4096]{1,0:T(8,128)(2,1)S(1)} %get-tuple-element.44.x_ref, bf16[256,1024]{1,0:T(8,128)(2,1)S(1)} %get-tuple-element.45.g_ref), custom_call_target="tpu_custom_call" | custom-call | tf_op jit(solution)/shard_map/cond/branch_1_fun/block_grads/pallas_call | solution.py:93
  50.3 0.0 copy-start.4
  50.3 0.6 collective-permute-done.1
  51.0 1.3 %add_convert_fusion = f16[16,16,16,128]{3,2,1,0:T(8,128)(2,1)} fusion(f16[16,16,16,128]{3,2,1,0:T(8,128)(2,1)S(1)} %collective-permute-done.1, f32[16,16,16,128]{3,2,1,0:T(8,128)S(1)} %block_grads.2, f32[16,128]{1,0:T(8,128)S(1)} %multiply_exponential_fusion), kind=kLoop, calls=%fused_computation | loop fusion | flops 2097152 | bytes 4202496 | tf_op jit(solution)/shard_map/cond/branch_1_fun/convert_element_type | solution.py:315
  52.3 0.0 copy-done.4
  52.3 1.5 %all-to-all-done.1.near_hbm = bf16[16,144,128]{2,1,0:T(8,128)(2,1)S(1)} async-done(((bf16[16,144,128]{2,1,0:T(8,128)(2,1)}), bf16[16,144,128]{2,1,0:T(8,128)(2,1)S(1)}, u32[]{:S(2)}, u32[]{:S(2)}) %all-to-all-start.1) | async-done | bytes 589856 | tf_op jit(solution)/shard_map/all_to_all | solution.py:307
  53.9 6.8 %all-to-all-start.2 = ((f16[16,16,16,128]{3,2,1,0:T(8,128)(2,1)}), f16[16,16,16,128]{3,2,1,0:T(8,128)(2,1)}, u32[]{:S(2)}, u32[]{:S(2)}) async-start(f16[16,16,16,128]{3,2,1,0:T(8,128)(2,1)} %get-tuple-element.82), calls=%async_computation.2 | async-start | bytes 2097152 | tf_op jit(solution)/shard_map/all_to_all | solution.py:322
  60.7 2.1 %collective-permute-start.4 = (bf16[8,144,128]{2,1,0:T(8,128)(2,1)S(1)}, bf16[8,144,128]{2,1,0:T(8,128)(2,1)}, u32[]{:S(2)}, u32[]{:S(2)}) collective-permute-start(bf16[8,144,128]{2,1,0:T(8,128)(2,1)S(1)} %get-tuple-element.112), channel_id=1, source_target_pairs={{0,240},{16,0},{32,16},{48,32},{64,48},{80,64},{96,80},{112,96},{1... | collective-permute-start | bytes 884744 | tf_op jit(solution)/shard_map/ppermute | solution.py:325
  62.8 3.7 %collective-permute-start.3 = (bf16[8,144,128]{2,1,0:T(8,128)(2,1)S(1)}, bf16[8,144,128]{2,1,0:T(8,128)(2,1)}, u32[]{:S(2)}, u32[]{:S(2)}) collective-permute-start(bf16[8,144,128]{2,1,0:T(8,128)(2,1)S(1)} %get-tuple-element.113), channel_id=1, source_target_pairs={{0,16},{16,32},{32,48},{48,64},{64,80},{80,96},{96,112},{112,128},... | collective-permute-start | bytes 884744 | tf_op jit(solution)/shard_map/ppermute | solution.py:324
  66.6 1.8 %order.1 = (s32[64]{0:T(128)S(1)}, s32[64]{0:T(128)S(1)}, f32[16,16,128]{2,1,0:T(8,128)S(1)}, f32[16,128]{1,0:T(8,128)S(1)}) custom-call(s32[64]{0:T(128)S(1)} %get-tuple-element.80.code_ref, bf16[16,144,128]{2,1,0:T(8,128)(2,1)S(1)} %all-to-all-done.1.near_hbm), custom_call_target="tpu_custom_call" | custom-call | tf_op jit(solution)/shard_map/order/pallas_call | solution.py:199
  68.4 1.7 %collective-permute-done.4 = bf16[8,144,128]{2,1,0:T(8,128)(2,1)} collective-permute-done((bf16[8,144,128]{2,1,0:T(8,128)(2,1)S(1)}, bf16[8,144,128]{2,1,0:T(8,128)(2,1)}, u32[]{:S(2)}, u32[]{:S(2)}) %collective-permute-start.4) | collective-permute-done | bytes 294944 | tf_op jit(solution)/shard_map/ppermute | solution.py:325
  70.1 3.1 %collective-permute-done.3 = bf16[8,144,128]{2,1,0:T(8,128)(2,1)} collective-permute-done((bf16[8,144,128]{2,1,0:T(8,128)(2,1)S(1)}, bf16[8,144,128]{2,1,0:T(8,128)(2,1)}, u32[]{:S(2)}, u32[]{:S(2)}) %collective-permute-start.3) | collective-permute-done | bytes 294944 | tf_op jit(solution)/shard_map/ppermute | solution.py:324
  73.3 1.3 %all-to-all-done.2 = f16[16,16,16,128]{3,2,1,0:T(8,128)(2,1)} async-done(((f16[16,16,16,128]{3,2,1,0:T(8,128)(2,1)}), f16[16,16,16,128]{3,2,1,0:T(8,128)(2,1)}, u32[]{:S(2)}, u32[]{:S(2)}) %all-to-all-start.2) | async-done | bytes 1048608 | tf_op jit(solution)/shard_map/all_to_all | solution.py:322
  74.5 1.4 %multiply_reduce_fusion = f32[16,16,128]{2,1,0:T(8,128)S(1)} fusion(f16[16,16,16,128]{3,2,1,0:T(8,128)(2,1)} %all-to-all-done.2, f32[16,16,128]{2,1,0:T(8,128)S(1)} %get-tuple-element.91), kind=kLoop, calls=%fused_computation.5 | loop fusion | flops 1540096 | bytes 1310720 | tf_op jit(solution)/shard_map/reduce_sum | solution.py:330
  76.0 0.7 pad_maximum_fusion
  76.7 3.5 %all-to-all-start.3 = ((f16[16,24,128]{2,1,0:T(8,128)(2,1)}), f16[16,24,128]{2,1,0:T(8,128)(2,1)S(1)}, u32[]{:S(2)}, u32[]{:S(2)}) async-start(f16[16,24,128]{2,1,0:T(8,128)(2,1)} %pad_maximum_fusion), calls=%async_computation.3 | async-start | bytes 196608 | tf_op jit(solution)/shard_map/all_to_all | solution.py:342
  80.2 8.0 %conditional.3 = (bf16[64,64,128]{2,1,0:T(8,128)(2,1)}, bf16[64,64,128]{2,1,0:T(8,128)(2,1)}) conditional(s32[]{:T(128)} %bitcast.6, () %tuple.36, (s32[]{:T(128)}, bf16[16,144,128]{2,1,0:T(8,128)(2,1)S(1)}, bf16[8,144,128]{2,1,0:T(8,128)(2,1)}, bf16[8,144,128]{2,1,0:T(8,128)(2,1)}) %tuple.37), branch_computations={%region_3.4_spmd, %region_4.5_spmd} | conditional | flops 11 | bytes 4194469 | solution.py:343
  80.2 3.0 %stage.1 = bf16[64,64,128]{2,1,0:T(8,128)(2,1)} custom-call(s32[1]{0:T(128)} %bitcast.4.parity_ref, bf16[16,144,128]{2,1,0:T(8,128)(2,1)S(1)} %get-tuple-element.48.near_hbm, bf16[8,144,128]{2,1,0:T(8,128)(2,1)} %get-tuple-element.49.up_hbm, bf16[8,144,128]{2,1,0:T(8,128)(2,1)} %get-tuple-element.50.down_hbm), custom_call_target="tpu_custom_call" | custom-call | tf_op jit(solution)/shard_map/cond/branch_1_fun/stage/pallas_call | solution.py:159
  83.3 1.9 %collective-permute-start = (bf16[64,64,128]{2,1,0:T(8,128)(2,1)}, bf16[64,64,128]{2,1,0:T(8,128)(2,1)}, u32[]{:S(2)}, u32[]{:S(2)}) collective-permute-start(bf16[64,64,128]{2,1,0:T(8,128)(2,1)} %stage.1), channel_id=1, source_target_pairs={{0,8},{8,0},{1,9},{9,1},{2,10},{10,2},{3,11},{11,3},{4,12},{12,4},... | collective-permute-start | bytes 3145736 | tf_op jit(solution)/shard_map/cond/branch_1_fun/ppermute | solution.py:287
  85.2 3.0 %collective-permute-done = bf16[64,64,128]{2,1,0:T(8,128)(2,1)} collective-permute-done((bf16[64,64,128]{2,1,0:T(8,128)(2,1)}, bf16[64,64,128]{2,1,0:T(8,128)(2,1)}, u32[]{:S(2)}, u32[]{:S(2)}) %collective-permute-start) | collective-permute-done | bytes 1048608 | tf_op jit(solution)/shard_map/cond/branch_1_fun/ppermute | solution.py:287
  88.2 4.9 %all-to-all-done.3 = f16[16,24,128]{2,1,0:T(8,128)(2,1)S(1)} async-done(((f16[16,24,128]{2,1,0:T(8,128)(2,1)}), f16[16,24,128]{2,1,0:T(8,128)(2,1)S(1)}, u32[]{:S(2)}, u32[]{:S(2)}) %all-to-all-start.3) | async-done | bytes 98336 | tf_op jit(solution)/shard_map/all_to_all | solution.py:342
  93.2 0.6 broadcast_in_dim.7
  93.8 6.7 %all-to-all-start.4 = ((f32[8,16,128]{2,1,0:T(8,128)}), f32[8,16,128]{2,1,0:T(8,128)S(1)}, u32[]{:S(2)}, u32[]{:S(2)}) async-start(f32[8,16,128]{2,1,0:T(8,128)} %broadcast_in_dim.7), calls=%async_computation.4 | async-start | bytes 131072 | tf_op jit(solution)/shard_map/all_to_all | solution.py:291
  100.5 5.0 %project.1 = (bf16[256,1024]{1,0:T(8,128)(2,1)}, bf16[256,4096]{1,0:T(8,128)(2,1)}) custom-call(s32[1]{0:T(128)} %bitcast.5.core_ref, s32[64]{0:T(128)S(1)} %get-tuple-element.80.code_ref, s32[64]{0:T(128)S(1)} %get-tuple-element.88.by_col, s32[64]{0:T(128)S(1)} %get-tuple-element.89.by_row, bf16[256,4096]{1,0:T(8,128)(2,1)S(1)} %copy-done.1, ...), custom_call_target="tpu_custom_call" | custom-call | tf_op jit(solution)/shard_map/project/pallas_call | solution.py:266
  105.5 0.0 all-to-all-done.4
  105.5 0.6 copy.21
  (12 shorter events, 0.1 us)
Async XLA Ops:
  1.9 0.8 copy-start
  3.3 34.8 %all-to-all-start = ((bf16[64,4,128]{2,1,0:T(4,128)(2,1)}), bf16[64,4,128]{2,1,0:T(4,128)(2,1)S(1)}, u32[]{:S(2)}, u32[]{:S(2)}) async-start(bf16[64,4,128]{2,1,0:T(4,128)(2,1)} %packet.1), calls=%async_computation | async-start | bytes 131072 | tf_op jit(solution)/shard_map/all_to_all | solution.py:300
  22.1 21.9 %copy-start.1 = (bf16[256,4096]{1,0:T(8,128)(2,1)S(1)}, bf16[256,4096]{1,0:T(8,128)(2,1)}, u32[]{:S(2)}) copy-start(bf16[256,4096]{1,0:T(8,128)(2,1)} %x_ref.3) | copy-start | bytes 6291460
  22.1 21.9 %copy-start.2 = (bf16[256,1024]{1,0:T(8,128)(2,1)S(1)}, bf16[256,1024]{1,0:T(8,128)(2,1)}, u32[]{:S(2)}) copy-start(bf16[256,1024]{1,0:T(8,128)(2,1)} %g_ref.3) | copy-start | bytes 1572868
  24.2 3.1 %collective-permute-start.2 = (f32[16,128]{1,0:T(8,128)S(1)}, f32[16,128]{1,0:T(8,128)S(1)}, u32[]{:S(2)}, u32[]{:S(2)}) collective-permute-start(f32[16,128]{1,0:T(8,128)S(1)} %power.1), channel_id=1, source_target_pairs={{0,8},{8,0},{1,9},{9,1},{2,10},{10,2},{3,11},{11,3},{4,12},{12,4},... | collective-permute-start | bytes 24584 | tf_op jit(solution)/shard_map/ppermute | solution.py:287
  39.0 14.9 %all-to-all-start.1 = ((bf16[16,144,128]{2,1,0:T(8,128)(2,1)}), bf16[16,144,128]{2,1,0:T(8,128)(2,1)S(1)}, u32[]{:S(2)}, u32[]{:S(2)}) async-start(bf16[16,144,128]{2,1,0:T(8,128)(2,1)} %share.1), calls=%async_computation.1 | async-start | bytes 1179648 | tf_op jit(solution)/shard_map/all_to_all | solution.py:307
  44.2 4.2 %copy-start.3 = (s32[64]{0:T(128)}, s32[64]{0:T(128)S(1)}, u32[]{:S(2)}) copy-start(s32[64]{0:T(128)S(1)} %fusion.code_ref) | copy-start | bytes 772 | tf_op jit(solution)/shard_map/cond
  46.4 4.6 %collective-permute-start.1 = (f16[16,16,16,128]{3,2,1,0:T(8,128)(2,1)S(1)}, f16[16,16,16,128]{3,2,1,0:T(8,128)(2,1)S(1)}, u32[]{:S(2)}, u32[]{:S(2)}) collective-permute-start(f16[16,16,16,128]{3,2,1,0:T(8,128)(2,1)S(1)} %multiply_convert_fusion), channel_id=1, source_target_pairs={{0,8},{8,0},{1,9},{9,1},{2,10},{10,2},{3,11},{11,3},{4,12},{12,4},... | collective-permute-start | bytes 3145736 | tf_op jit(solution)/shard_map/cond/branch_1_fun/ppermute | solution.py:287
  50.3 2.0 %copy-start.4 = (s32[64]{0:T(128)S(1)}, s32[64]{0:T(128)}, u32[]{:S(2)}) copy-start(s32[64]{0:T(128)} %copy-done.3) | copy-start | bytes 772 | tf_op jit(solution)/shard_map/cond
  53.9 20.7 %all-to-all-start.2 = ((f16[16,16,16,128]{3,2,1,0:T(8,128)(2,1)}), f16[16,16,16,128]{3,2,1,0:T(8,128)(2,1)}, u32[]{:S(2)}, u32[]{:S(2)}) async-start(f16[16,16,16,128]{3,2,1,0:T(8,128)(2,1)} %get-tuple-element.82), calls=%async_computation.2 | async-start | bytes 2097152 | tf_op jit(solution)/shard_map/all_to_all | solution.py:322
  60.7 9.4 %collective-permute-start.4 = (bf16[8,144,128]{2,1,0:T(8,128)(2,1)S(1)}, bf16[8,144,128]{2,1,0:T(8,128)(2,1)}, u32[]{:S(2)}, u32[]{:S(2)}) collective-permute-start(bf16[8,144,128]{2,1,0:T(8,128)(2,1)S(1)} %get-tuple-element.112), channel_id=1, source_target_pairs={{0,240},{16,0},{32,16},{48,32},{64,48},{80,64},{96,80},{112,96},{1... | collective-permute-start | bytes 884744 | tf_op jit(solution)/shard_map/ppermute | solution.py:325
  62.8 10.4 %collective-permute-start.3 = (bf16[8,144,128]{2,1,0:T(8,128)(2,1)S(1)}, bf16[8,144,128]{2,1,0:T(8,128)(2,1)}, u32[]{:S(2)}, u32[]{:S(2)}) collective-permute-start(bf16[8,144,128]{2,1,0:T(8,128)(2,1)S(1)} %get-tuple-element.113), channel_id=1, source_target_pairs={{0,16},{16,32},{32,48},{48,64},{64,80},{80,96},{96,112},{112,128},... | collective-permute-start | bytes 884744 | tf_op jit(solution)/shard_map/ppermute | solution.py:324
  76.7 16.4 %all-to-all-start.3 = ((f16[16,24,128]{2,1,0:T(8,128)(2,1)}), f16[16,24,128]{2,1,0:T(8,128)(2,1)S(1)}, u32[]{:S(2)}, u32[]{:S(2)}) async-start(f16[16,24,128]{2,1,0:T(8,128)(2,1)} %pad_maximum_fusion), calls=%async_computation.3 | async-start | bytes 196608 | tf_op jit(solution)/shard_map/all_to_all | solution.py:342
  83.3 4.9 %collective-permute-start = (bf16[64,64,128]{2,1,0:T(8,128)(2,1)}, bf16[64,64,128]{2,1,0:T(8,128)(2,1)}, u32[]{:S(2)}, u32[]{:S(2)}) collective-permute-start(bf16[64,64,128]{2,1,0:T(8,128)(2,1)} %stage.1), channel_id=1, source_target_pairs={{0,8},{8,0},{1,9},{9,1},{2,10},{10,2},{3,11},{11,3},{4,12},{12,4},... | collective-permute-start | bytes 3145736 | tf_op jit(solution)/shard_map/cond/branch_1_fun/ppermute | solution.py:287
  93.8 11.7 %all-to-all-start.4 = ((f32[8,16,128]{2,1,0:T(8,128)}), f32[8,16,128]{2,1,0:T(8,128)S(1)}, u32[]{:S(2)}, u32[]{:S(2)}) async-start(f32[8,16,128]{2,1,0:T(8,128)} %broadcast_in_dim.7), calls=%async_computation.4 | async-start | bytes 131072 | tf_op jit(solution)/shard_map/all_to_all | solution.py:291

commit v7 on v6

--- a/solution.py
+++ b/solution.py
@@ -173,7 +173,7 @@
     )(parity, near, up, down)
 
 
-def order_kernel(code_ref, near_hbm, by_col, by_row, down_ref, lift_ref, fill, powers, sem):
+def order_kernel(code_ref, near_hbm, by_col, by_row, down_ref, fill, powers, sem):
     load = pltpu.make_async_copy(near_hbm.at[:, B:], powers, sem)
     load.start()
     for k in range(CB + RB):
@@ -189,8 +189,8 @@
         fill[CB + row] = at + 1
     load.wait()
     lift = jnp.min(powers[...].astype(jnp.float32), axis=0) - 4.0
-    down_ref[...] = jnp.exp2(lift[None] - powers[...].astype(jnp.float32))
-    lift_ref[...] = lift
+    down_ref[:, :16] = jnp.exp2(lift[None] - powers[...].astype(jnp.float32))
+    down_ref[:, 16:] = jnp.broadcast_to(lift[None, :8] / 16.0, (16, 8, B))
 
 
 def order_blocks(codes, near):
@@ -201,11 +201,10 @@
         out_shape=[
             order,
             order,
-            jax.ShapeDtypeStruct((16, 16, B), jnp.float32),
-            jax.ShapeDtypeStruct((16, B), jnp.float32),
+            jax.ShapeDtypeStruct((16, 24, B), jnp.float32),
         ],
         in_specs=[smem, pl.BlockSpec(memory_space=pl.ANY)],
-        out_specs=[smem, smem] + [pl.BlockSpec(memory_space=pltpu.VMEM)] * 2,
+        out_specs=[smem, smem, pl.BlockSpec(memory_space=pltpu.VMEM)],
         scratch_shapes=[
             pltpu.SMEM((CB + RB,), jnp.int32),
             pltpu.VMEM((16, 16, B), jnp.bfloat16),
@@ -323,13 +322,13 @@
     parity = (lax.axis_index("z") % 2).astype(jnp.int32).reshape(1)
     from_below = lax.ppermute(near[:8], "z", [(i, (i + 1) % 16) for i in range(16)])
     from_above = lax.ppermute(near[8:], "z", [(i, (i - 1) % 16) for i in range(16)])
-    by_col, by_row, down, lift = order_blocks(codes, near)
-    spread, from_below, from_above, by_col, by_row, down, lift = lax.optimization_barrier(
-        (spread, from_below, from_above, by_col, by_row, down, lift)
+    by_col, by_row, down = order_blocks(codes, near)
+    spread, from_below, from_above, by_col, by_row, down = lax.optimization_barrier(
+        (spread, from_below, from_above, by_col, by_row, down)
     )
-    plane_sum = jnp.sum(spread.astype(jnp.float32) * down[:, None], axis=0)
-    tail = jnp.broadcast_to(lift[None, :8], (16, 8, B))
-    plane_sum = jnp.concatenate([plane_sum, tail], axis=1).astype(jnp.float16)
+    padded = jnp.pad(spread, ((0, 0), (0, 0), (0, 8), (0, 0)), constant_values=1)
+    plane_sum = jnp.sum(padded.astype(jnp.float32) * down[:, None], axis=0)
+    plane_sum = plane_sum.astype(jnp.float16)
 
     def halves(near, from_below, from_above):
         half = stage(parity, near, from_below, from_above)

time: 107 us -> 107 us (level)
  no operation moved by 1% of the time
where the time goes in v7:
time: 107 us; the launch traced here: 106 us
  starting transfers between devices  52.3 us (49%)
  waiting for transfers between devices  28.1 us (26%)
  Pallas kernels  17.5 us (16%)
  other arithmetic  3.79 us (4%)
  local copies, waits for them, and re-layouts  2.21 us (2%)
  between operations  2.07 us (2%)
    all_to_all x1, starting transfers between devices, per_device(): got = lax.all_to_all(packet, FSDP, 0, 0, tiled=True)  18.7 us
    all_to_all x1, waiting for transfers between devices, per_device(): got = lax.all_to_all(packet, FSDP, 0, 0, tiled=True)  10.8 us
    all_to_all x1, starting transfers between devices, per_device(): spread = lax.all_to_all(paired, PLANE, 0, 0, tiled=True)  6.81 us
    all_to_all x1, starting transfers between devices, to_all(): lax.all_to_all(jnp.broadcast_to(part[None], (count,) + part.shape), axes,...  6.67 us
    ppermute x3, starting transfers between devices, flip(): return lax.ppermute(value, axis, [(i, i ^ by) for i in range(size)])  5.81 us
    pallas_call x1, Pallas kernels, project(): pl.pallas_call(project_kernel, out_shape=[jax.ShapeDtypeStruct(g.shape, j...  5.02 us
    all_to_all x1, starting transfers between devices, per_device(): near = lax.all_to_all(share, PLANE, 0, 0, tiled=True)  4.96 us
    all_to_all x1, waiting for transfers between devices, per_device(): ring = lax.all_to_all(plane_sum, 'z', 0, 0, tiled=True)  4.94 us
  transfers between devices with their start and end apart: 10, of which 9 were waited for; matrix products, arithmetic and copies ran while one was open for 2% of the time, Pallas kernels for 15%

profile of v7, /device:TPU:2, one launch (start us, length us, event | category | flops | bytes accessed | tf_op | source)
XLA Modules:
  0.0 106.1 jit_solution(803677815015355108)
XLA Ops:
  1.9 0.0 copy-start
  1.9 0.7 copy-done
  2.7 0.7 packet.1
  3.3 18.7 %all-to-all-start = ((bf16[64,4,128]{2,1,0:T(4,128)(2,1)}), bf16[64,4,128]{2,1,0:T(4,128)(2,1)S(1)}, u32[]{:S(2)}, u32[]{:S(2)}) async-start(bf16[64,4,128]{2,1,0:T(4,128)(2,1)} %packet.1), calls=%async_computation | async-start | bytes 131072 | tf_op jit(solution)/shard_map/all_to_all | solution.py:299
  22.1 0.0 copy-start.1
  22.1 0.0 copy-start.2
  22.1 2.1 %power.1 = f32[16,128]{1,0:T(8,128)S(1)} custom-call(bf16[256,4096]{1,0:T(8,128)(2,1)} %x_ref.3, bf16[256,1024]{1,0:T(8,128)(2,1)} %g_ref.3), custom_call_target="tpu_custom_call" | custom-call | tf_op jit(solution)/shard_map/power/pallas_call | solution.py:80
  24.2 2.0 %collective-permute-start.2 = (f32[16,128]{1,0:T(8,128)S(1)}, f32[16,128]{1,0:T(8,128)S(1)}, u32[]{:S(2)}, u32[]{:S(2)}) collective-permute-start(f32[16,128]{1,0:T(8,128)S(1)} %power.1), channel_id=1, source_target_pairs={{0,8},{8,0},{1,9},{9,1},{2,10},{10,2},{3,11},{11,3},{4,12},{12,4},... | collective-permute-start | bytes 24584 | tf_op jit(solution)/shard_map/ppermute | solution.py:286
  26.2 1.1 %collective-permute-done.2 = f32[16,128]{1,0:T(8,128)S(1)} collective-permute-done((f32[16,128]{1,0:T(8,128)S(1)}, f32[16,128]{1,0:T(8,128)S(1)}, u32[]{:S(2)}, u32[]{:S(2)}) %collective-permute-start.2) | collective-permute-done | bytes 8224 | tf_op jit(solution)/shard_map/ppermute | solution.py:286
  27.3 10.8 %all-to-all-done.got_ref = bf16[64,4,128]{2,1,0:T(4,128)(2,1)S(1)} async-done(((bf16[64,4,128]{2,1,0:T(4,128)(2,1)}), bf16[64,4,128]{2,1,0:T(4,128)(2,1)S(1)}, u32[]{:S(2)}, u32[]{:S(2)}) %all-to-all-start) | async-done | bytes 65568 | tf_op jit(solution)/shard_map/all_to_all | solution.py:299
  38.1 0.9 share.1
  39.0 5.0 %all-to-all-start.1 = ((bf16[16,144,128]{2,1,0:T(8,128)(2,1)}), bf16[16,144,128]{2,1,0:T(8,128)(2,1)S(1)}, u32[]{:S(2)}, u32[]{:S(2)}) async-start(bf16[16,144,128]{2,1,0:T(8,128)(2,1)} %share.1), calls=%async_computation.1 | async-start | bytes 1179648 | tf_op jit(solution)/shard_map/all_to_all | solution.py:306
  44.0 0.0 copy-done.1
  44.0 0.0 copy-done.2
  44.0 8.3 %conditional.2 = (f16[16,16,16,128]{3,2,1,0:T(8,128)(2,1)}, s32[64]{0:T(128)S(1)}) conditional(s32[]{:T(128)} %bitcast.6, () %tuple.31, (s32[]{:T(128)}, bf16[64,4,128]{2,1,0:T(4,128)(2,1)S(1)}, bf16[256,4096]{1,0:T(8,128)(2,1)S(1)}, bf16[256,1024]{1,0:T(8,128)(2,1)S(1)}, f32[16,128]{1,0:T(8,128)S(1)}) %tuple.50), branch_computations={%region_0.0_spmd, %region_1.0_spmd} | conditional | flops 3147841 | bytes 11700732 | solution.py:319
  44.0 0.1 copy.9
  44.2 0.0 copy-start.3
  44.2 2.0 %block_grads.3 = f32[16,16,16,128]{3,2,1,0:T(8,128)S(1)} custom-call(s32[1]{0:T(128)} %bitcast.2.parity_ref, s32[64]{0:T(128)S(1)} %fusion.code_ref, bf16[256,4096]{1,0:T(8,128)(2,1)S(1)} %get-tuple-element.44.x_ref, bf16[256,1024]{1,0:T(8,128)(2,1)S(1)} %get-tuple-element.45.g_ref), custom_call_target="tpu_custom_call" | custom-call | tf_op jit(solution)/shard_map/cond/branch_1_fun/block_grads/pallas_call | solution.py:93
  46.1 0.3 multiply_convert_fusion
  46.4 1.9 %collective-permute-start.1 = (f16[16,16,16,128]{3,2,1,0:T(8,128)(2,1)S(1)}, f16[16,16,16,128]{3,2,1,0:T(8,128)(2,1)S(1)}, u32[]{:S(2)}, u32[]{:S(2)}) collective-permute-start(f16[16,16,16,128]{3,2,1,0:T(8,128)(2,1)S(1)} %multiply_convert_fusion), channel_id=1, source_target_pairs={{0,8},{8,0},{1,9},{9,1},{2,10},{10,2},{3,11},{11,3},{4,12},{12,4},... | collective-permute-start | bytes 3145736 | tf_op jit(solution)/shard_map/cond/branch_1_fun/ppermute | solution.py:286
  48.3 0.0 copy-done.3
  48.4 2.0 %block_grads.2 = f32[16,16,16,128]{3,2,1,0:T(8,128)S(1)} custom-call(s32[1]{0:T(128)} %bitcast.parity_ref, s32[64]{0:T(128)S(1)} %fusion.code_ref, bf16[256,4096]{1,0:T(8,128)(2,1)S(1)} %get-tuple-element.44.x_ref, bf16[256,1024]{1,0:T(8,128)(2,1)S(1)} %get-tuple-element.45.g_ref), custom_call_target="tpu_custom_call" | custom-call | tf_op jit(solution)/shard_map/cond/branch_1_fun/block_grads/pallas_call | solution.py:93
  50.3 0.0 copy-start.4
  50.3 0.6 collective-permute-done.1
  51.0 1.3 %add_convert_fusion = f16[16,16,16,128]{3,2,1,0:T(8,128)(2,1)} fusion(f16[16,16,16,128]{3,2,1,0:T(8,128)(2,1)S(1)} %collective-permute-done.1, f32[16,16,16,128]{3,2,1,0:T(8,128)S(1)} %block_grads.2, f32[16,128]{1,0:T(8,128)S(1)} %multiply_exponential_fusion), kind=kLoop, calls=%fused_computation | loop fusion | flops 2097152 | bytes 4202496 | tf_op jit(solution)/shard_map/cond/branch_1_fun/convert_element_type | solution.py:314
  52.3 0.0 copy-done.4
  52.3 1.5 %all-to-all-done.1.near_hbm = bf16[16,144,128]{2,1,0:T(8,128)(2,1)S(1)} async-done(((bf16[16,144,128]{2,1,0:T(8,128)(2,1)}), bf16[16,144,128]{2,1,0:T(8,128)(2,1)S(1)}, u32[]{:S(2)}, u32[]{:S(2)}) %all-to-all-start.1) | async-done | bytes 589856 | tf_op jit(solution)/shard_map/all_to_all | solution.py:306
  53.9 6.8 %all-to-all-start.2 = ((f16[16,16,16,128]{3,2,1,0:T(8,128)(2,1)}), f16[16,16,16,128]{3,2,1,0:T(8,128)(2,1)}, u32[]{:S(2)}, u32[]{:S(2)}) async-start(f16[16,16,16,128]{3,2,1,0:T(8,128)(2,1)} %get-tuple-element.80), calls=%async_computation.2 | async-start | bytes 2097152 | tf_op jit(solution)/shard_map/all_to_all | solution.py:321
  60.7 2.1 %collective-permute-start.4 = (bf16[8,144,128]{2,1,0:T(8,128)(2,1)S(1)}, bf16[8,144,128]{2,1,0:T(8,128)(2,1)}, u32[]{:S(2)}, u32[]{:S(2)}) collective-permute-start(bf16[8,144,128]{2,1,0:T(8,128)(2,1)S(1)} %get-tuple-element.108), channel_id=1, source_target_pairs={{0,240},{16,0},{32,16},{48,32},{64,48},{80,64},{96,80},{112,96},{1... | collective-permute-start | bytes 884744 | tf_op jit(solution)/shard_map/ppermute | solution.py:324
  62.8 3.7 %collective-permute-start.3 = (bf16[8,144,128]{2,1,0:T(8,128)(2,1)S(1)}, bf16[8,144,128]{2,1,0:T(8,128)(2,1)}, u32[]{:S(2)}, u32[]{:S(2)}) collective-permute-start(bf16[8,144,128]{2,1,0:T(8,128)(2,1)S(1)} %get-tuple-element.109), channel_id=1, source_target_pairs={{0,16},{16,32},{32,48},{48,64},{64,80},{80,96},{96,112},{112,128},... | collective-permute-start | bytes 884744 | tf_op jit(solution)/shard_map/ppermute | solution.py:323
  66.6 1.8 %order.1 = (s32[64]{0:T(128)S(1)}, s32[64]{0:T(128)S(1)}, f32[16,24,128]{2,1,0:T(8,128)S(1)}) custom-call(s32[64]{0:T(128)S(1)} %get-tuple-element.78.code_ref, bf16[16,144,128]{2,1,0:T(8,128)(2,1)S(1)} %all-to-all-done.1.near_hbm), custom_call_target="tpu_custom_call" | custom-call | tf_op jit(solution)/shard_map/order/pallas_call | solution.py:199
  68.4 1.7 %collective-permute-done.4 = bf16[8,144,128]{2,1,0:T(8,128)(2,1)} collective-permute-done((bf16[8,144,128]{2,1,0:T(8,128)(2,1)S(1)}, bf16[8,144,128]{2,1,0:T(8,128)(2,1)}, u32[]{:S(2)}, u32[]{:S(2)}) %collective-permute-start.4) | collective-permute-done | bytes 294944 | tf_op jit(solution)/shard_map/ppermute | solution.py:324
  70.1 3.1 %collective-permute-done.3 = bf16[8,144,128]{2,1,0:T(8,128)(2,1)} collective-permute-done((bf16[8,144,128]{2,1,0:T(8,128)(2,1)S(1)}, bf16[8,144,128]{2,1,0:T(8,128)(2,1)}, u32[]{:S(2)}, u32[]{:S(2)}) %collective-permute-start.3) | collective-permute-done | bytes 294944 | tf_op jit(solution)/shard_map/ppermute | solution.py:323
  73.3 1.3 %all-to-all-done.2 = f16[16,16,16,128]{3,2,1,0:T(8,128)(2,1)} async-done(((f16[16,16,16,128]{3,2,1,0:T(8,128)(2,1)}), f16[16,16,16,128]{3,2,1,0:T(8,128)(2,1)}, u32[]{:S(2)}, u32[]{:S(2)}) %all-to-all-start.2) | async-done | bytes 1048608 | tf_op jit(solution)/shard_map/all_to_all | solution.py:321
  74.5 1.5 %multiply_reduce_fusion = f32[16,24,128]{2,1,0:T(8,128)S(1)} fusion(f32[16,24,128]{2,1,0:T(8,128)S(1)} %get-tuple-element.88, f16[16,16,16,128]{3,2,1,0:T(8,128)(2,1)} %all-to-all-done.2), kind=kLoop, calls=%fused_computation.5 | loop fusion | flops 2310144 | bytes 1441792 | tf_op jit(solution)/shard_map/reduce_sum | solution.py:330
  76.0 0.7 convert_element_type.35
  76.6 3.5 %all-to-all-start.3 = ((f16[16,24,128]{2,1,0:T(8,128)(2,1)}), f16[16,24,128]{2,1,0:T(8,128)(2,1)S(1)}, u32[]{:S(2)}, u32[]{:S(2)}) async-start(f16[16,24,128]{2,1,0:T(8,128)(2,1)} %convert_element_type.35), calls=%async_computation.3 | async-start | bytes 196608 | tf_op jit(solution)/shard_map/all_to_all | solution.py:341
  80.2 8.0 %conditional.3 = (bf16[64,64,128]{2,1,0:T(8,128)(2,1)}, bf16[64,64,128]{2,1,0:T(8,128)(2,1)}) conditional(s32[]{:T(128)} %bitcast.6, () %tuple.36, (s32[]{:T(128)}, bf16[16,144,128]{2,1,0:T(8,128)(2,1)S(1)}, bf16[8,144,128]{2,1,0:T(8,128)(2,1)}, bf16[8,144,128]{2,1,0:T(8,128)(2,1)}) %tuple.37), branch_computations={%region_3.4_spmd, %region_4.5_spmd} | conditional | flops 11 | bytes 4194469 | solution.py:342
  80.2 3.0 %stage.1 = bf16[64,64,128]{2,1,0:T(8,128)(2,1)} custom-call(s32[1]{0:T(128)} %bitcast.4.parity_ref, bf16[16,144,128]{2,1,0:T(8,128)(2,1)S(1)} %get-tuple-element.48.near_hbm, bf16[8,144,128]{2,1,0:T(8,128)(2,1)} %get-tuple-element.49.up_hbm, bf16[8,144,128]{2,1,0:T(8,128)(2,1)} %get-tuple-element.50.down_hbm), custom_call_target="tpu_custom_call" | custom-call | tf_op jit(solution)/shard_map/cond/branch_1_fun/stage/pallas_call | solution.py:159
  83.2 1.9 %collective-permute-start = (bf16[64,64,128]{2,1,0:T(8,128)(2,1)}, bf16[64,64,128]{2,1,0:T(8,128)(2,1)}, u32[]{:S(2)}, u32[]{:S(2)}) collective-permute-start(bf16[64,64,128]{2,1,0:T(8,128)(2,1)} %stage.1), channel_id=1, source_target_pairs={{0,8},{8,0},{1,9},{9,1},{2,10},{10,2},{3,11},{11,3},{4,12},{12,4},... | collective-permute-start | bytes 3145736 | tf_op jit(solution)/shard_map/cond/branch_1_fun/ppermute | solution.py:286
  85.2 3.0 %collective-permute-done = bf16[64,64,128]{2,1,0:T(8,128)(2,1)} collective-permute-done((bf16[64,64,128]{2,1,0:T(8,128)(2,1)}, bf16[64,64,128]{2,1,0:T(8,128)(2,1)}, u32[]{:S(2)}, u32[]{:S(2)}) %collective-permute-start) | collective-permute-done | bytes 1048608 | tf_op jit(solution)/shard_map/cond/branch_1_fun/ppermute | solution.py:286
  88.1 4.9 %all-to-all-done.3 = f16[16,24,128]{2,1,0:T(8,128)(2,1)S(1)} async-done(((f16[16,24,128]{2,1,0:T(8,128)(2,1)}), f16[16,24,128]{2,1,0:T(8,128)(2,1)S(1)}, u32[]{:S(2)}, u32[]{:S(2)}) %all-to-all-start.3) | async-done | bytes 98336 | tf_op jit(solution)/shard_map/all_to_all | solution.py:341
  93.2 0.6 broadcast_in_dim.4
  93.8 6.7 %all-to-all-start.4 = ((f32[8,16,128]{2,1,0:T(8,128)}), f32[8,16,128]{2,1,0:T(8,128)S(1)}, u32[]{:S(2)}, u32[]{:S(2)}) async-start(f32[8,16,128]{2,1,0:T(8,128)} %broadcast_in_dim.4), calls=%async_computation.4 | async-start | bytes 131072 | tf_op jit(solution)/shard_map/all_to_all | solution.py:290
  100.5 5.0 %project.1 = (bf16[256,1024]{1,0:T(8,128)(2,1)}, bf16[256,4096]{1,0:T(8,128)(2,1)}) custom-call(s32[1]{0:T(128)} %bitcast.5.core_ref, s32[64]{0:T(128)S(1)} %get-tuple-element.78.code_ref, s32[64]{0:T(128)S(1)} %get-tuple-element.85.by_col, s32[64]{0:T(128)S(1)} %get-tuple-element.86.by_row, bf16[256,4096]{1,0:T(8,128)(2,1)S(1)} %copy-done.1, ...), custom_call_target="tpu_custom_call" | custom-call | tf_op jit(solution)/shard_map/project/pallas_call | solution.py:265
  105.5 0.0 all-to-all-done.4
  105.5 0.6 copy.21
  (9 shorter events, 0.1 us)
Async XLA Ops:
  1.9 0.8 copy-start
  3.3 34.8 %all-to-all-start = ((bf16[64,4,128]{2,1,0:T(4,128)(2,1)}), bf16[64,4,128]{2,1,0:T(4,128)(2,1)S(1)}, u32[]{:S(2)}, u32[]{:S(2)}) async-start(bf16[64,4,128]{2,1,0:T(4,128)(2,1)} %packet.1), calls=%async_computation | async-start | bytes 131072 | tf_op jit(solution)/shard_map/all_to_all | solution.py:299
  22.1 21.9 %copy-start.1 = (bf16[256,4096]{1,0:T(8,128)(2,1)S(1)}, bf16[256,4096]{1,0:T(8,128)(2,1)}, u32[]{:S(2)}) copy-start(bf16[256,4096]{1,0:T(8,128)(2,1)} %x_ref.3) | copy-start | bytes 6291460
  22.1 21.9 %copy-start.2 = (bf16[256,1024]{1,0:T(8,128)(2,1)S(1)}, bf16[256,1024]{1,0:T(8,128)(2,1)}, u32[]{:S(2)}) copy-start(bf16[256,1024]{1,0:T(8,128)(2,1)} %g_ref.3) | copy-start | bytes 1572868
  24.2 3.1 %collective-permute-start.2 = (f32[16,128]{1,0:T(8,128)S(1)}, f32[16,128]{1,0:T(8,128)S(1)}, u32[]{:S(2)}, u32[]{:S(2)}) collective-permute-start(f32[16,128]{1,0:T(8,128)S(1)} %power.1), channel_id=1, source_target_pairs={{0,8},{8,0},{1,9},{9,1},{2,10},{10,2},{3,11},{11,3},{4,12},{12,4},... | collective-permute-start | bytes 24584 | tf_op jit(solution)/shard_map/ppermute | solution.py:286
  39.0 14.9 %all-to-all-start.1 = ((bf16[16,144,128]{2,1,0:T(8,128)(2,1)}), bf16[16,144,128]{2,1,0:T(8,128)(2,1)S(1)}, u32[]{:S(2)}, u32[]{:S(2)}) async-start(bf16[16,144,128]{2,1,0:T(8,128)(2,1)} %share.1), calls=%async_computation.1 | async-start | bytes 1179648 | tf_op jit(solution)/shard_map/all_to_all | solution.py:306
  44.2 4.2 %copy-start.3 = (s32[64]{0:T(128)}, s32[64]{0:T(128)S(1)}, u32[]{:S(2)}) copy-start(s32[64]{0:T(128)S(1)} %fusion.code_ref) | copy-start | bytes 772 | tf_op jit(solution)/shard_map/cond
  46.4 4.6 %collective-permute-start.1 = (f16[16,16,16,128]{3,2,1,0:T(8,128)(2,1)S(1)}, f16[16,16,16,128]{3,2,1,0:T(8,128)(2,1)S(1)}, u32[]{:S(2)}, u32[]{:S(2)}) collective-permute-start(f16[16,16,16,128]{3,2,1,0:T(8,128)(2,1)S(1)} %multiply_convert_fusion), channel_id=1, source_target_pairs={{0,8},{8,0},{1,9},{9,1},{2,10},{10,2},{3,11},{11,3},{4,12},{12,4},... | collective-permute-start | bytes 3145736 | tf_op jit(solution)/shard_map/cond/branch_1_fun/ppermute | solution.py:286
  50.3 2.0 %copy-start.4 = (s32[64]{0:T(128)S(1)}, s32[64]{0:T(128)}, u32[]{:S(2)}) copy-start(s32[64]{0:T(128)} %copy-done.3) | copy-start | bytes 772 | tf_op jit(solution)/shard_map/cond
  53.9 20.7 %all-to-all-start.2 = ((f16[16,16,16,128]{3,2,1,0:T(8,128)(2,1)}), f16[16,16,16,128]{3,2,1,0:T(8,128)(2,1)}, u32[]{:S(2)}, u32[]{:S(2)}) async-start(f16[16,16,16,128]{3,2,1,0:T(8,128)(2,1)} %get-tuple-element.80), calls=%async_computation.2 | async-start | bytes 2097152 | tf_op jit(solution)/shard_map/all_to_all | solution.py:321
  60.7 9.4 %collective-permute-start.4 = (bf16[8,144,128]{2,1,0:T(8,128)(2,1)S(1)}, bf16[8,144,128]{2,1,0:T(8,128)(2,1)}, u32[]{:S(2)}, u32[]{:S(2)}) collective-permute-start(bf16[8,144,128]{2,1,0:T(8,128)(2,1)S(1)} %get-tuple-element.108), channel_id=1, source_target_pairs={{0,240},{16,0},{32,16},{48,32},{64,48},{80,64},{96,80},{112,96},{1... | collective-permute-start | bytes 884744 | tf_op jit(solution)/shard_map/ppermute | solution.py:324
  62.8 10.4 %collective-permute-start.3 = (bf16[8,144,128]{2,1,0:T(8,128)(2,1)S(1)}, bf16[8,144,128]{2,1,0:T(8,128)(2,1)}, u32[]{:S(2)}, u32[]{:S(2)}) collective-permute-start(bf16[8,144,128]{2,1,0:T(8,128)(2,1)S(1)} %get-tuple-element.109), channel_id=1, source_target_pairs={{0,16},{16,32},{32,48},{48,64},{64,80},{80,96},{96,112},{112,128},... | collective-permute-start | bytes 884744 | tf_op jit(solution)/shard_map/ppermute | solution.py:323
  76.6 16.4 %all-to-all-start.3 = ((f16[16,24,128]{2,1,0:T(8,128)(2,1)}), f16[16,24,128]{2,1,0:T(8,128)(2,1)S(1)}, u32[]{:S(2)}, u32[]{:S(2)}) async-start(f16[16,24,128]{2,1,0:T(8,128)(2,1)} %convert_element_type.35), calls=%async_computation.3 | async-start | bytes 196608 | tf_op jit(solution)/shard_map/all_to_all | solution.py:341
  83.2 4.9 %collective-permute-start = (bf16[64,64,128]{2,1,0:T(8,128)(2,1)}, bf16[64,64,128]{2,1,0:T(8,128)(2,1)}, u32[]{:S(2)}, u32[]{:S(2)}) collective-permute-start(bf16[64,64,128]{2,1,0:T(8,128)(2,1)} %stage.1), channel_id=1, source_target_pairs={{0,8},{8,0},{1,9},{9,1},{2,10},{10,2},{3,11},{11,3},{4,12},{12,4},... | collective-permute-start | bytes 3145736 | tf_op jit(solution)/shard_map/cond/branch_1_fun/ppermute | solution.py:286
  93.8 11.7 %all-to-all-start.4 = ((f32[8,16,128]{2,1,0:T(8,128)}), f32[8,16,128]{2,1,0:T(8,128)S(1)}, u32[]{:S(2)}, u32[]{:S(2)}) async-start(f32[8,16,128]{2,1,0:T(8,128)} %broadcast_in_dim.4), calls=%async_computation.4 | async-start | bytes 131072 | tf_op jit(solution)/shard_map/all_to_all | solution.py:290
